TPU v7x, 32 devices: a whole 2x2x4 slice. The times are simulated.
32 devices in a mesh: batch: 8 (over y, x, core), seq: 4 (over z).
Axes of the slice: x: 2, y: 2, z: 4, core: 2. Of those that a mesh axis runs over, the one named last changes fastest.
Arguments:
- inputs: bfloat16 [16, 1728, 1024], P('batch', 'seq'), may hold values from -6 to 6
- timesteps: int32 [16], P('batch'), may hold values from 0 to 4999
- segments: int32 [16, 1728], P('batch'), may hold values from 0 to 13, as said below
- cotangent: bfloat16 [16, 1728, 1024], P('batch', 'seq'), may hold values from -6 to 6
- w_qkv: bfloat16 [1024, 3072], replicated, may hold values from -0.1875 to 0.1875
- b_query: bfloat16 [1024], replicated, may hold values from -3 to 3
- b_value: bfloat16 [1024], replicated, may hold values from -3 to 3
- w_out: bfloat16 [1024, 1024], replicated, may hold values from -1.5 to 1.5
- b_out: bfloat16 [1024], replicated, may hold values from -3 to 3
- ln1_gain: bfloat16 [1024], replicated, may hold values from 0.25 to 1.75
- ln1_bias: bfloat16 [1024], replicated, may hold values from -3 to 3
- w_up: bfloat16 [1024, 4096], replicated, may hold values from -0.1875 to 0.1875
- b_up: bfloat16 [4096], replicated, may hold values from -3 to 3
- w_down: bfloat16 [4096, 1024], replicated, may hold values from -0.09375 to 0.09375
- b_down: bfloat16 [1024], replicated, may hold values from -3 to 3
- ln2_gain: bfloat16 [1024], replicated, may hold values from 0.25 to 1.75
- ln2_bias: bfloat16 [1024], replicated, may hold values from -3 to 3
- w_time: bfloat16 [1024], replicated, may hold values from -4 to 4
- b_time: bfloat16 [1024], replicated, may hold values from -3 to 3
Outputs:
- output: bfloat16 [16, 1728, 1024], P('batch', 'seq')
- grad_inputs: bfloat16 [16, 1728, 1024], P('batch', 'seq')
- grad_w_qkv: float32 [1024, 3072], P(('batch', 'seq'))
- grad_b_query: float32 [1024], P(('batch', 'seq'))
- grad_b_value: float32 [1024], P(('batch', 'seq'))
- grad_w_out: float32 [1024, 1024], P(('batch', 'seq'))
- grad_b_out: float32 [1024], P(('batch', 'seq'))
- grad_ln1_gain: float32 [1024], P(('batch', 'seq'))
- grad_ln1_bias: float32 [1024], P(('batch', 'seq'))
- grad_w_up: float32 [1024, 4096], P(('batch', 'seq'))
- grad_b_up: float32 [4096], P(('batch', 'seq'))
- grad_w_down: float32 [4096, 1024], P(('batch', 'seq'))
- grad_b_down: float32 [1024], P(('batch', 'seq'))
- grad_ln2_gain: float32 [1024], P(('batch', 'seq'))
- grad_ln2_bias: float32 [1024], P(('batch', 'seq'))
- grad_w_time: float32 [1024], P(('batch', 'seq'))
- grad_b_time: float32 [1024], P(('batch', 'seq'))
Inputs may be any that keep to these rules, and one draw needn't show every extreme that they name: `segments`: in each sequence the ids rise by one from item to item, starting at 1 at position 0, over the first 1664 positions; the last 64 positions carry 0. Items are 512 or 128 positions long, except that in each index of batch one sequence is a single item. Padding positions attend only to padding.
All inputs are finite; a program needn't handle non-finite values.
Results may differ from a plain program's by a relative error of at most 0.014.
Values may be sent and summed in bfloat16 or wider, within the bound.
No kernel may reach another device: no remote copies, remote signals or barrier semaphores. Data moves between devices by JAX's collectives and lax.ppermute only.
A program may use at most 256 MiB of HBM per device.

v0:
```python
import jax
import jax.numpy as jnp
from jax import lax
from jax.sharding import PartitionSpec as P

D = 1024
HEADS = 16
TSTEPS = 5000


def gelu_exact(values):
    return jax.nn.gelu(values, approximate=False)


def norm_forward(values, gain, shift):
    centered = values - jnp.mean(values, axis=-1, keepdims=True)
    inverse = lax.rsqrt(jnp.mean(centered * centered, axis=-1, keepdims=True) + 1e-05)
    unit_part = centered * inverse
    return (unit_part * gain + shift, unit_part, inverse)


def norm_backward(grad_out, unit_part, inverse, gain):
    scaled = grad_out * gain
    centered = scaled - jnp.mean(scaled, axis=-1, keepdims=True)
    grad_in = inverse * (
        centered - unit_part * jnp.mean(scaled * unit_part, axis=-1, keepdims=True)
    )
    return (grad_in, jnp.sum(grad_out * unit_part, axis=0), jnp.sum(grad_out, axis=0))


def attention_forward(query_all, key_all, value_all, segments, head_dim):
    length, local_width = (query_all.shape[1], query_all.shape[2])
    head_count = local_width // head_dim
    block_len = length // 3
    score_scale = head_dim ** (-0.5)

    def per_sequence(pieces):
        queries, key_rows, value_rows, seq_ids = pieces
        key_heads = key_rows.reshape(length, head_count, head_dim)
        value_heads = value_rows.reshape(length, head_count, head_dim)

        def per_block(block_pieces):
            query_part, id_part = block_pieces
            query_heads = query_part.reshape(block_len, head_count, head_dim)
            scores = (
                jnp.einsum(
                    "qhd,khd->hqk", query_heads, key_heads, preferred_element_type=jnp.float32
                )
                * score_scale
            )
            masked = jnp.where(id_part[None, :, None] == seq_ids[None, None, :], scores, -1e30)
            maxima = jnp.max(masked, axis=-1, keepdims=True)
            exp_scores = jnp.exp(masked - maxima)
            totals = jnp.sum(exp_scores, axis=-1, keepdims=True)
            weights_low = (exp_scores / totals).astype(jnp.bfloat16)
            context = jnp.einsum(
                "hqk,khd->qhd", weights_low, value_heads, preferred_element_type=jnp.float32
            )
            return (
                context.astype(jnp.bfloat16).reshape(block_len, local_width),
                (maxima + jnp.log(totals))[..., 0],
            )

        contexts, logsums = lax.map(
            per_block, (queries.reshape(3, block_len, local_width), seq_ids.reshape(3, block_len))
        )
        return (contexts.reshape(length, local_width), logsums)

    return lax.map(per_sequence, (query_all, key_all, value_all, segments))


def attention_backward(query_all, key_all, value_all, segments, logsums, grad_all, head_dim):
    length, local_width = (query_all.shape[1], query_all.shape[2])
    head_count = local_width // head_dim
    block_len = length // 3
    score_scale = head_dim ** (-0.5)

    def per_sequence(pieces):
        queries, key_rows, value_rows, seq_ids, sum_rows, grad_rows = pieces
        key_heads = key_rows.reshape(length, head_count, head_dim)
        value_heads = value_rows.reshape(length, head_count, head_dim)

        def per_block(carry, block_pieces):
            key_total, value_total = carry
            query_part, id_part, sum_part, grad_part = block_pieces
            query_heads = query_part.reshape(block_len, head_count, head_dim)
            grad_heads = grad_part.reshape(block_len, head_count, head_dim)
            scores = (
                jnp.einsum(
                    "qhd,khd->hqk", query_heads, key_heads, preferred_element_type=jnp.float32
                )
                * score_scale
            )
            allowed = id_part[None, :, None] == seq_ids[None, None, :]
            prob_weights = jnp.where(allowed, jnp.exp(scores - sum_part[:, :, None]), 0.0)
            grad_probs = jnp.einsum(
                "qhd,khd->hqk", grad_heads, value_heads, preferred_element_type=jnp.float32
            )
            delta = jnp.sum(prob_weights * grad_probs, axis=-1, keepdims=True)
            grad_scores = (prob_weights * (grad_probs - delta)).astype(jnp.bfloat16)
            query_grad = (
                jnp.einsum(
                    "hqk,khd->qhd", grad_scores, key_heads, preferred_element_type=jnp.float32
                )
                * score_scale
            )
            key_total = (
                key_total
                + jnp.einsum(
                    "hqk,qhd->khd", grad_scores, query_heads, preferred_element_type=jnp.float32
                )
                * score_scale
            )
            value_total = value_total + jnp.einsum(
                "hqk,qhd->khd",
                prob_weights.astype(jnp.bfloat16),
                grad_heads,
                preferred_element_type=jnp.float32,
            )
            return (
                (key_total, value_total),
                query_grad.astype(jnp.bfloat16).reshape(block_len, local_width),
            )

        zero_heads = jnp.zeros((length, head_count, head_dim), jnp.float32)
        (key_total, value_total), query_grads = lax.scan(
            per_block,
            (zero_heads, zero_heads),
            (
                queries.reshape(3, block_len, local_width),
                seq_ids.reshape(3, block_len),
                sum_rows,
                grad_rows.reshape(3, block_len, local_width),
            ),
        )
        return (
            query_grads.reshape(length, local_width),
            key_total.astype(jnp.bfloat16).reshape(length, local_width),
            value_total.astype(jnp.bfloat16).reshape(length, local_width),
        )

    return lax.map(per_sequence, (query_all, key_all, value_all, segments, logsums, grad_all))


def per_device(
    inputs,
    timesteps,
    segments,
    cotangent,
    w_qkv,
    b_query,
    b_value,
    w_out,
    b_out,
    ln1_gain,
    ln1_bias,
    w_up,
    b_up,
    w_down,
    b_down,
    ln2_gain,
    ln2_bias,
    w_time,
    b_time,
):
    groups, local_len, model_width = inputs.shape
    row_count = groups * local_len
    head_dim = D // HEADS
    fraction = timesteps.astype(jnp.float32) / TSTEPS
    start_sum = (
        inputs.astype(jnp.float32)
        + fraction[:, None, None] * w_time.astype(jnp.float32)
        + b_time.astype(jnp.float32)
    )
    start_low = start_sum.astype(jnp.bfloat16)
    projected = jnp.einsum("bld,de->ble", start_low, w_qkv, preferred_element_type=jnp.float32)
    query_low = (projected[..., :model_width] + b_query.astype(jnp.float32)).astype(jnp.bfloat16)
    key_low = projected[..., model_width : 2 * model_width].astype(jnp.bfloat16)
    value_low = (projected[..., 2 * model_width :] + b_value.astype(jnp.float32)).astype(
        jnp.bfloat16
    )
    query_all, key_all, value_all = (
        lax.all_to_all(query_low, "seq", split_axis=2, concat_axis=1, tiled=True),
        lax.all_to_all(key_low, "seq", split_axis=2, concat_axis=1, tiled=True),
        lax.all_to_all(value_low, "seq", split_axis=2, concat_axis=1, tiled=True),
    )
    context_heads, logsums = attention_forward(query_all, key_all, value_all, segments, head_dim)
    context = lax.all_to_all(context_heads, "seq", split_axis=1, concat_axis=2, tiled=True)
    context_rows = context.reshape(row_count, model_width)
    start_rows = start_sum.reshape(row_count, model_width)
    residual_one = (
        start_rows
        + jnp.dot(context_rows, w_out, preferred_element_type=jnp.float32)
        + b_out.astype(jnp.float32)
    )
    normed, unit_one, inverse_one = norm_forward(
        residual_one, ln1_gain.astype(jnp.float32), ln1_bias.astype(jnp.float32)
    )
    normed_low = normed.astype(jnp.bfloat16)
    hidden_pre = jnp.dot(normed_low, w_up, preferred_element_type=jnp.float32) + b_up.astype(
        jnp.float32
    )
    activated, gelu_pull = jax.vjp(gelu_exact, hidden_pre)
    activated_low = activated.astype(jnp.bfloat16)
    residual_two = (
        normed
        + jnp.dot(activated_low, w_down, preferred_element_type=jnp.float32)
        + b_down.astype(jnp.float32)
    )
    result, unit_two, inverse_two = norm_forward(
        residual_two, ln2_gain.astype(jnp.float32), ln2_bias.astype(jnp.float32)
    )
    output = result.astype(jnp.bfloat16).reshape(groups, local_len, model_width)
    grad_result = cotangent.reshape(row_count, model_width).astype(jnp.float32)
    grad_two, grad_ln2_gain, grad_ln2_bias = norm_backward(
        grad_result, unit_two, inverse_two, ln2_gain.astype(jnp.float32)
    )
    grad_b_down = jnp.sum(grad_two, axis=0)
    grad_two_low = grad_two.astype(jnp.bfloat16)
    grad_w_down = jnp.einsum(
        "rf,rd->fd", activated_low, grad_two_low, preferred_element_type=jnp.float32
    )
    grad_activated = jnp.einsum(
        "rd,fd->rf", grad_two_low, w_down, preferred_element_type=jnp.float32
    )
    grad_hidden = gelu_pull(grad_activated)[0]
    grad_b_up = jnp.sum(grad_hidden, axis=0)
    grad_hidden_low = grad_hidden.astype(jnp.bfloat16)
    grad_w_up = jnp.einsum(
        "rd,rf->df", normed_low, grad_hidden_low, preferred_element_type=jnp.float32
    )
    grad_normed = grad_two + jnp.einsum(
        "rf,df->rd", grad_hidden_low, w_up, preferred_element_type=jnp.float32
    )
    grad_one, grad_ln1_gain, grad_ln1_bias = norm_backward(
        grad_normed, unit_one, inverse_one, ln1_gain.astype(jnp.float32)
    )
    grad_b_out = jnp.sum(grad_one, axis=0)
    grad_one_low = grad_one.astype(jnp.bfloat16)
    grad_w_out = jnp.einsum(
        "rd,re->de", context_rows, grad_one_low, preferred_element_type=jnp.float32
    )
    grad_context = (
        jnp.einsum("re,de->rd", grad_one_low, w_out, preferred_element_type=jnp.float32)
        .astype(jnp.bfloat16)
        .reshape(groups, local_len, model_width)
    )
    grad_context_heads = lax.all_to_all(
        grad_context, "seq", split_axis=2, concat_axis=1, tiled=True
    )
    query_grads, key_grads, value_grads = attention_backward(
        query_all, key_all, value_all, segments, logsums, grad_context_heads, head_dim
    )
    grad_query, grad_key, grad_value = (
        lax.all_to_all(query_grads, "seq", split_axis=1, concat_axis=2, tiled=True),
        lax.all_to_all(key_grads, "seq", split_axis=1, concat_axis=2, tiled=True),
        lax.all_to_all(value_grads, "seq", split_axis=1, concat_axis=2, tiled=True),
    )
    grad_projected = jnp.concatenate((grad_query, grad_key, grad_value), axis=2).reshape(
        row_count, 3 * model_width
    )
    grad_w_qkv = jnp.einsum(
        "rd,re->de",
        start_low.reshape(row_count, model_width),
        grad_projected,
        preferred_element_type=jnp.float32,
    )
    grad_b_query = jnp.sum(grad_query.astype(jnp.float32), axis=(0, 1))
    grad_b_value = jnp.sum(grad_value.astype(jnp.float32), axis=(0, 1))
    grad_start = grad_one + jnp.einsum(
        "re,de->rd", grad_projected, w_qkv, preferred_element_type=jnp.float32
    )
    grad_inputs = grad_start.astype(jnp.bfloat16).reshape(groups, local_len, model_width)
    per_sequence_grad = jnp.sum(grad_start.reshape(groups, local_len, model_width), axis=1)
    grad_w_time = jnp.einsum("g,gd->d", fraction, per_sequence_grad)
    grad_b_time = jnp.sum(per_sequence_grad, axis=0)
    (
        sum_w_qkv,
        sum_b_query,
        sum_b_value,
        sum_w_out,
        sum_b_out,
        sum_ln1_gain,
        sum_ln1_bias,
        sum_w_up,
        sum_b_up,
        sum_w_down,
        sum_b_down,
        sum_ln2_gain,
        sum_ln2_bias,
        sum_w_time,
        sum_b_time,
    ) = (
        lax.psum_scatter(grad_w_qkv, ("batch", "seq"), scatter_dimension=0, tiled=True),
        lax.psum_scatter(grad_b_query, ("batch", "seq"), scatter_dimension=0, tiled=True),
        lax.psum_scatter(grad_b_value, ("batch", "seq"), scatter_dimension=0, tiled=True),
        lax.psum_scatter(grad_w_out, ("batch", "seq"), scatter_dimension=0, tiled=True),
        lax.psum_scatter(grad_b_out, ("batch", "seq"), scatter_dimension=0, tiled=True),
        lax.psum_scatter(grad_ln1_gain, ("batch", "seq"), scatter_dimension=0, tiled=True),
        lax.psum_scatter(grad_ln1_bias, ("batch", "seq"), scatter_dimension=0, tiled=True),
        lax.psum_scatter(grad_w_up, ("batch", "seq"), scatter_dimension=0, tiled=True),
        lax.psum_scatter(grad_b_up, ("batch", "seq"), scatter_dimension=0, tiled=True),
        lax.psum_scatter(grad_w_down, ("batch", "seq"), scatter_dimension=0, tiled=True),
        lax.psum_scatter(grad_b_down, ("batch", "seq"), scatter_dimension=0, tiled=True),
        lax.psum_scatter(grad_ln2_gain, ("batch", "seq"), scatter_dimension=0, tiled=True),
        lax.psum_scatter(grad_ln2_bias, ("batch", "seq"), scatter_dimension=0, tiled=True),
        lax.psum_scatter(grad_w_time, ("batch", "seq"), scatter_dimension=0, tiled=True),
        lax.psum_scatter(grad_b_time, ("batch", "seq"), scatter_dimension=0, tiled=True),
    )
    return (
        output,
        grad_inputs,
        sum_w_qkv,
        sum_b_query,
        sum_b_value,
        sum_w_out,
        sum_b_out,
        sum_ln1_gain,
        sum_ln1_bias,
        sum_w_up,
        sum_b_up,
        sum_w_down,
        sum_b_down,
        sum_ln2_gain,
        sum_ln2_bias,
        sum_w_time,
        sum_b_time,
    )


def solution(mesh):
    placed = (
        P("batch", "seq", None),
        P("batch"),
        P("batch", None),
        P("batch", "seq", None),
        P(),
        P(),
        P(),
        P(),
        P(),
        P(),
        P(),
        P(),
        P(),
        P(),
        P(),
        P(),
        P(),
        P(),
        P(),
    )
    return jax.shard_map(
        per_device,
        mesh=mesh,
        in_specs=placed,
        out_specs=(
            P("batch", "seq", None),
            P("batch", "seq", None),
            P(("batch", "seq"), None),
            P(("batch", "seq")),
            P(("batch", "seq")),
            P(("batch", "seq"), None),
            P(("batch", "seq")),
            P(("batch", "seq")),
            P(("batch", "seq")),
            P(("batch", "seq"), None),
            P(("batch", "seq")),
            P(("batch", "seq"), None),
            P(("batch", "seq")),
            P(("batch", "seq")),
            P(("batch", "seq")),
            P(("batch", "seq")),
            P(("batch", "seq")),
        ),
        check_vma=False,
    )
```

profile of v0, /device:TPU:0, one launch (start us, length us, event | category | flops | bytes accessed | tf_op | source)
XLA Modules:
  0.0 2065.4 jit_solution(10952345442941073343)
XLA Ops:
  11.4 8.3 fusion.27
  30.8 6.3 all-to-all-start.2
  43.3 42.2 %all-to-all-done.2 = bf16[2,432,1024]{1,0,2:T(2,128)(2,1)} async-done(((bf16[2,432,1024]{1,0,2:T(2,128)(2,1)}), bf16[2,432,1024]{1,0,2:T(2,128)(2,1)}, u32[]{:S(2)}, u32[]{:S(2)}) %all-to-all-start.2) | async-done | bytes 1769504 | tf_op jit(solution)/shard_map/all_to_all | solution.py:185
  93.4 6.2 copy.127
  99.6 38.1 %all-to-all-done = bf16[2,432,1024]{1,0,2:T(2,128)(2,1)} async-done(((bf16[2,432,1024]{1,0,2:T(2,128)(2,1)}), bf16[2,432,1024]{1,0,2:T(2,128)(2,1)}, u32[]{:S(2)}, u32[]{:S(2)}) %all-to-all-start) | async-done | bytes 1769504 | tf_op jit(solution)/shard_map/all_to_all | solution.py:183
  142.1 6.4 copy.154
  161.4 28.5 %all-to-all-done.1 = bf16[2,432,1024]{1,0,2:T(2,128)(2,1)} async-done(((bf16[2,432,1024]{1,0,2:T(2,128)(2,1)}), bf16[2,432,1024]{1,0,2:T(2,128)(2,1)}, u32[]{:S(2)}, u32[]{:S(2)}) %all-to-all-start.1) | async-done | bytes 1769504 | tf_op jit(solution)/shard_map/all_to_all | solution.py:184
  189.9 6.4 copy.153
  204.4 132.0 %while.54 = (s32[]{:T(128)}, bf16[2,1728,256]{2,1,0:T(8,128)(2,1)}, f32[2,3,4,576]{3,2,1,0:T(4,128)}, bf16[2,1728,256]{2,1,0:T(8,128)(2,1)}, s32[2,1728]{1,0:T(2...) while((s32[]{:T(128)}, bf16[2,1728,256]{2,1,0:T(8,128)(2,1)}, ...), condition=%wide.region_5.6_spmd, body=%wide.region_0.5_spmd.sunk | while | flops 1068132096 | bytes 67270984 | solution.py:69
  210.3 57.3 %while.57 = (s32[]{:T(128)}, bf16[3,576,256]{2,1,0:T(8,128)(2,1)}, f32[3,4,576]{2,1,0:T(4,128)S(1)}, s32[3,576]{1,0:T(4,128)S(1)}, s32[1728]{0:T(1024)S(1)}, /*i...) while((s32[]{:T(128)}, bf16[3,576,256]{2,1,0:T(8,128)(2,1)}, ...), condition=%wide.region_4.4_spmd, body=%wide.region_1.3_spmd.sunk | while | flops 1068132096 | bytes 60105860 | solution.py:64
  276.3 57.3 %while.57 = (s32[]{:T(128)}, bf16[3,576,256]{2,1,0:T(8,128)(2,1)}, f32[3,4,576]{2,1,0:T(4,128)S(1)}, s32[3,576]{1,0:T(4,128)S(1)}, s32[1728]{0:T(1024)S(1)}, /*i...) while((s32[]{:T(128)}, bf16[3,576,256]{2,1,0:T(8,128)(2,1)}, ...), condition=%wide.region_4.4_spmd, body=%wide.region_1.3_spmd.sunk | while | flops 1068132096 | bytes 60105860 | solution.py:64
  336.4 14.4 copy.135
  366.5 29.5 %all-to-all-done.3 = bf16[2,1728,256]{2,0,1:T(2,128)(2,1)} async-done(((bf16[2,1728,256]{2,0,1:T(2,128)(2,1)}), bf16[2,1728,256]{2,0,1:T(2,128)(2,1)}, u32[]{:S(2)}, u32[]{:S(2)}) %all-to-all-start.3) | async-done | bytes 1769504 | tf_op jit(solution)/shard_map/all_to_all | solution.py:188
  402.5 43.4 %multiply_convert_fusion.1 = (bf16[864,4096]{1,0:T(8,128)(2,1)S(1)}, f32[864,4096]{1,0:T(8,128)}, f32[864,4096]{1,0:T(8,128)}) fusion(f32[4096]{0:T(1024)S(1)} %convert_element_type.133, bf16[1024,4096]{1,0:T(8,128)(2,1)} %param.38, f32[1024]{0:T(1024)S(1)} %convert_element_type.131, f32[1024]{0:T(1024)S(1)} %convert_element_type.130, ...), kind=kOutput, calls=%fused_computation.53 | convolution fusion | flops 7486636032 | bytes 47352576 | tf_op jit(solution)/shard_map/dot_general | solution.py:200
  445.9 8.0 fusion.77
  461.0 23.7 %fusion.78 = (f32[4096]{0:T(1024)}, bf16[864,4096]{1,0:T(8,128)(2,1)}) fusion(f32[864,4096]{1,0:T(8,128)} %get-tuple-element.502, bf16[4096,1024]{1,0:T(8,128)(2,1)} %param.40, f32[864,1024]{1,0:T(8,128)} %get-tuple-element.498, f32[864,4096]{1,0:T(8,128)} %get-tuple-element.520, f32[4096]{0:T(1024)S(1)} %convert_element_type.133), kind=kOutput, calls=%fused_computation.147 | convolution fusion | flops 7305261056 | bytes 47349760 | tf_op jit(solution)/shard_map/rd,fd->rf/dot_general | solution.py:223
  484.7 15.3 multiply_reduce_fusion.1
  515.0 47.6 %all-to-all-done.4 = bf16[2,432,1024]{1,0,2:T(2,128)(2,1)S(1)} async-done(((bf16[2,432,1024]{1,0,2:T(2,128)(2,1)}), bf16[2,432,1024]{1,0,2:T(2,128)(2,1)S(1)}, u32[]{:S(2)}, u32[]{:S(2)}) %all-to-all-start.4) | async-done | bytes 1769504 | tf_op jit(solution)/shard_map/all_to_all | solution.py:248
  570.1 373.0 %while.56 = (s32[]{:T(128)}, bf16[2,1728,256]{2,1,0:T(8,128)(2,1)}, bf16[2,1728,256]{1,2,0:T(8,128)(2,1)}, bf16[2,1728,256]{1,2,0:T(8,128)(2,1)}, bf16[2,1728,25...) while((s32[]{:T(128)}, bf16[2,1728,256]{2,1,0:T(8,128)(2,1)}, ...), condition=%wide.region_18.19_spmd, body=%wide.region_14.18_spmd.sunk | while | flops 2612143872 | bytes 241089728 | solution.py:142
  578.7 171.3 %while.58 = (s32[]{:T(128)}, f32[1728,4,64]{0,2,1:T(8,128)}, f32[1728,4,64]{0,2,1:T(8,128)}, bf16[3,576,256]{2,1,0:T(8,128)(2,1)}, bf16[3,576,256]{2,1,0:T(8,128...) while((s32[]{:T(128)}, f32[1728,4,64]{0,2,1:T(8,128)}, ...), condition=%wide.region_17.17_spmd.clone, body=%wide.region_15.16_spmd.clone.sunk | while | flops 2611259136 | bytes 170095792 | solution.py:126
  580.0 8.1 fusion.136
  589.0 12.7 multiply_reduce_fusion.8
  601.7 14.6 multiply_convert_fusion.3
  616.4 6.4 fusion.137
  626.1 9.0 fusion.138
  636.5 8.1 fusion.136
  645.5 12.8 multiply_reduce_fusion.8
  658.2 14.6 multiply_convert_fusion.3
  672.9 6.9 fusion.137
  683.1 9.5 fusion.138
  693.9 8.1 fusion.136
  702.9 12.8 multiply_reduce_fusion.8
  715.6 14.6 multiply_convert_fusion.3
  730.3 6.9 fusion.137
  740.5 9.5 fusion.138
  764.9 171.3 %while.58 = (s32[]{:T(128)}, f32[1728,4,64]{0,2,1:T(8,128)}, f32[1728,4,64]{0,2,1:T(8,128)}, bf16[3,576,256]{2,1,0:T(8,128)(2,1)}, bf16[3,576,256]{2,1,0:T(8,128...) while((s32[]{:T(128)}, f32[1728,4,64]{0,2,1:T(8,128)}, ...), condition=%wide.region_17.17_spmd.clone, body=%wide.region_15.16_spmd.clone.sunk | while | flops 2611259136 | bytes 170095792 | solution.py:126
  766.2 8.1 fusion.136
  775.2 12.8 multiply_reduce_fusion.8
  787.9 14.6 multiply_convert_fusion.3
  802.6 6.4 fusion.137
  812.3 9.0 fusion.138
  822.6 8.1 fusion.136
  831.6 12.8 multiply_reduce_fusion.8
  844.4 14.6 multiply_convert_fusion.3
  859.0 6.9 fusion.137
  869.3 9.5 fusion.138
  880.0 8.1 fusion.136
  889.0 12.8 multiply_reduce_fusion.8
  901.8 14.6 multiply_convert_fusion.3
  916.4 6.9 fusion.137
  926.7 9.5 fusion.138
  952.2 7.0 fusion.55
  959.3 14.2 copy.143
  973.5 39.9 %all-to-all-done.6 = bf16[2,1728,256]{2,0,1:T(2,128)(2,1)S(1)} async-done(((bf16[2,1728,256]{2,0,1:T(2,128)(2,1)}), bf16[2,1728,256]{2,0,1:T(2,128)(2,1)S(1)}, u32[]{:S(2)}, u32[]{:S(2)}) %all-to-all-start.6) | async-done | bytes 1769504 | tf_op jit(solution)/shard_map/all_to_all | solution.py:256
  1023.6 57.0 %all-to-all-done.5 = bf16[2,1728,256]{2,0,1:T(2,128)(2,1)S(1)} async-done(((bf16[2,1728,256]{2,0,1:T(2,128)(2,1)}), bf16[2,1728,256]{2,0,1:T(2,128)(2,1)S(1)}, u32[]{:S(2)}, u32[]{:S(2)}) %all-to-all-start.5) | async-done | bytes 1769504 | tf_op jit(solution)/shard_map/all_to_all | solution.py:255
  1095.5 53.3 %all-to-all-done.7 = bf16[2,1728,256]{2,0,1:T(2,128)(2,1)} async-done(((bf16[2,1728,256]{2,0,1:T(2,128)(2,1)}), bf16[2,1728,256]{2,0,1:T(2,128)(2,1)}, u32[]{:S(2)}, u32[]{:S(2)}) %all-to-all-start.7) | async-done | bytes 1769504 | tf_op jit(solution)/shard_map/all_to_all | solution.py:257
  1151.9 9.7 convolution_bitcast_fusion
  1161.7 16.1 fusion.58
  1178.5 16.6 fusion.44
  1202.2 11.0 fusion.76
  1215.9 43.0 %all-reduce.11 = (f32[1024]{0:T(1024)S(1)}, f32[1024]{0:T(1024)S(1)}, f32[1024]{0:T(1024)S(1)}, f32[1024]{0:T(1024)S(1)}, f32[1024]{0:T(1024)S(1)}, /*index=5*/f...) all-reduce(f32[1024]{0:T(1024)S(1)} %bitcast.252, ...), channel_id=3, replica_groups=mesh['batch'=8,'seq'=4] {'batch','seq'}, use_global_device_ids=true, to_apply=%region_21.22.clone | all-reduce | flops 14336 | bytes 114688
  1265.3 61.8 %reduce-scatter.5.cloned.1.call-done = f32[32,3072]{1,0:T(8,128)} async-done(((f32[1024,3072]{1,0:T(8,128)}), f32[32,3072]{1,0:T(8,128)}) %reduce-scatter.5.cloned.1.call-update) | async-done | bytes 393232 | tf_op jit(solution)/shard_map/reduce_scatter | solution.py:294
  1327.1 366.3 %reduce-scatter.11.cloned.1.call-done = f32[128,1024]{1,0:T(8,128)} async-done(((f32[4096,1024]{1,0:T(8,128)}), f32[128,1024]{1,0:T(8,128)}) %reduce-scatter.11.cloned.1.call-update) | async-done | bytes 524304 | tf_op jit(solution)/shard_map/reduce_scatter | solution.py:303
  1693.4 365.0 %reduce-scatter.9.cloned.1.call-done = f32[32,4096]{1,0:T(8,128)} async-done(((f32[1024,4096]{1,0:T(8,128)}), f32[32,4096]{1,0:T(8,128)}) %reduce-scatter.9.cloned.1.call-update) | async-done | bytes 524304 | tf_op jit(solution)/shard_map/reduce_scatter | solution.py:301
  (428 shorter events, 354.6 us)
Async XLA Ops:
  7.2 392.2 %copy-start = (bf16[1024,1024]{1,0:T(8,128)(2,1)S(1)}, bf16[1024,1024]{1,0:T(8,128)(2,1)}, u32[]{:S(2)}) copy-start(bf16[1024,1024]{1,0:T(8,128)(2,1)} %param.34) | copy-start | bytes 6291460
  19.7 5.0 copy-start.17
  30.8 54.6 %all-to-all-start.2 = ((bf16[2,432,1024]{1,0,2:T(2,128)(2,1)}), bf16[2,432,1024]{1,0,2:T(2,128)(2,1)}, u32[]{:S(2)}, u32[]{:S(2)}) async-start(bf16[2,432,1024]{1,0,2:T(2,128)(2,1)} %copy.130), calls=%async_computation.2 | async-start | bytes 4194304 | tf_op jit(solution)/shard_map/all_to_all | solution.py:185
  85.5 52.2 %all-to-all-start = ((bf16[2,432,1024]{1,0,2:T(2,128)(2,1)}), bf16[2,432,1024]{1,0,2:T(2,128)(2,1)}, u32[]{:S(2)}, u32[]{:S(2)}) async-start(bf16[2,432,1024]{1,0,2:T(2,128)(2,1)} %copy.125), calls=%async_computation | async-start | bytes 4194304 | tf_op jit(solution)/shard_map/all_to_all | solution.py:183
  137.7 52.2 %all-to-all-start.1 = ((bf16[2,432,1024]{1,0,2:T(2,128)(2,1)}), bf16[2,432,1024]{1,0,2:T(2,128)(2,1)}, u32[]{:S(2)}, u32[]{:S(2)}) async-start(bf16[2,432,1024]{1,0,2:T(2,128)(2,1)} %copy.127), calls=%async_computation.1 | async-start | bytes 4194304 | tf_op jit(solution)/shard_map/all_to_all | solution.py:184
  218.7 4.7 copy-start.7
  237.8 4.7 copy-start.7
  256.9 4.7 copy-start.7
  284.6 4.7 copy-start.7
  303.7 4.7 copy-start.7
  322.8 4.7 copy-start.7
  336.3 19.0 copy-start.60
  336.3 19.0 copy-start.61
  336.4 19.0 copy-start.62
  336.4 19.0 copy-start.54
  336.4 19.1 copy-start.63
  336.4 19.7 copy-start.64
  350.8 8.9 copy-start.65
  350.8 45.3 %all-to-all-start.3 = ((bf16[2,1728,256]{2,0,1:T(2,128)(2,1)}), bf16[2,1728,256]{2,0,1:T(2,128)(2,1)}, u32[]{:S(2)}, u32[]{:S(2)}) async-start(bf16[2,1728,256]{2,0,1:T(2,128)(2,1)} %copy.135), calls=%async_computation.3 | async-start | bytes 3538944 | tf_op jit(solution)/shard_map/all_to_all | solution.py:188
  355.3 144.7 %copy-start.33 = (f32[1024]{0:T(1024)}, f32[1024]{0:T(1024)S(1)}, u32[]{:S(2)}) copy-start(f32[1024]{0:T(1024)S(1)} %convert_element_type.129) | copy-start | bytes 12292
  355.4 144.6 %copy-start.47 = (f32[1024]{0:T(1024)}, f32[1024]{0:T(1024)S(1)}, u32[]{:S(2)}) copy-start(f32[1024]{0:T(1024)S(1)} %convert_element_type.130) | copy-start | bytes 12292
  355.4 90.5 %copy-start.57 = (f32[1024]{0:T(1024)}, f32[1024]{0:T(1024)S(1)}, u32[]{:S(2)}) copy-start(f32[1024]{0:T(1024)S(1)} %convert_element_type.131) | copy-start | bytes 12292
  356.0 8.0 copy-start.31
  356.0 8.0 copy-start.38
  356.0 8.0 copy-start.45
  359.7 4.4 copy-start.26
  396.0 3.4 copy-start.21
  401.5 44.4 %copy-start.4 = (f32[864,1024]{1,0:T(8,128)}, f32[864,1024]{1,0:T(8,128)S(1)}, u32[]{:S(2)}) copy-start(f32[864,1024]{1,0:T(8,128)S(1)} %bitcast_add_fusion) | copy-start | bytes 10616836
  401.8 98.2 %copy-start.35 = (f32[864]{0:T(1024)}, f32[864]{0:T(1024)S(1)}, u32[]{:S(2)}) copy-start(f32[864]{0:T(1024)S(1)} %broadcast_multiply_fusion.6) | copy-start | bytes 10372
  402.5 97.6 %copy-start.49 = (f32[864]{0:T(1024)}, f32[864]{0:T(1024)S(1)}, u32[]{:S(2)}) copy-start(f32[864]{0:T(1024)S(1)} %add_rsqrt_fusion.1) | copy-start | bytes 10372
  402.5 43.5 %copy-start.59 = (f32[1024]{0:T(1024)S(1)}, f32[1024]{0:T(1024)}, u32[]{:S(2)}) copy-start(f32[1024]{0:T(1024)} %convert_element_type.135) | copy-start | bytes 12292
  402.5 43.5 %copy-start.66 = (bf16[4096,1024]{1,0:T(8,128)(2,1)S(1)}, bf16[4096,1024]{1,0:T(8,128)(2,1)}, u32[]{:S(2)}) copy-start(bf16[4096,1024]{1,0:T(8,128)(2,1)} %param.40) | copy-start | bytes 25165828
  445.9 8.0 copy-start.68
  445.9 8.5 copy-start.15
  484.7 15.3 copy-start.5
  502.0 3.2 copy-start.19
  511.3 51.3 %all-to-all-start.4 = ((bf16[2,432,1024]{1,0,2:T(2,128)(2,1)}), bf16[2,432,1024]{1,0,2:T(2,128)(2,1)S(1)}, u32[]{:S(2)}, u32[]{:S(2)}) async-start(bf16[2,432,1024]{1,0,2:T(2,128)(2,1)} %copy.137), calls=%async_computation.4 | async-start | bytes 4194304 | tf_op jit(solution)/shard_map/all_to_all | solution.py:248
  570.5 7.4 copy-start.9
  616.4 6.4 copy-start.2
  672.9 6.9 copy-start.2
  730.3 6.9 copy-start.2
  750.0 3.2 copy-start.24
  751.7 4.1 copy-start.8
  752.1 4.6 copy-start.10
  756.8 7.4 copy-start.9
  802.6 6.4 copy-start.2
  859.0 6.9 copy-start.2
  916.4 6.9 copy-start.2
  936.2 3.2 copy-start.24
  937.9 4.1 copy-start.8
  938.3 4.6 copy-start.10
  948.6 64.7 %all-to-all-start.6 = ((bf16[2,1728,256]{2,0,1:T(2,128)(2,1)}), bf16[2,1728,256]{2,0,1:T(2,128)(2,1)S(1)}, u32[]{:S(2)}, u32[]{:S(2)}) async-start(bf16[2,1728,256]{2,0,1:T(2,128)(2,1)} %copy.145), calls=%async_computation.6 | async-start | bytes 3538944 | tf_op jit(solution)/shard_map/all_to_all | solution.py:256
  952.2 313.2 %reduce-scatter.7.cloned.1.call-start = ((), (), s32[]{:S(2)}) async-start(), calls=%async_computation.13 | async-start | bytes 4325376 | tf_op jit(solution)/shard_map/reduce_scatter | solution.py:297
  1014.5 66.1 %all-to-all-start.5 = ((bf16[2,1728,256]{2,0,1:T(2,128)(2,1)}), bf16[2,1728,256]{2,0,1:T(2,128)(2,1)S(1)}, u32[]{:S(2)}, u32[]{:S(2)}) async-start(bf16[2,1728,256]{2,0,1:T(2,128)(2,1)} %copy.143), calls=%async_computation.5 | async-start | bytes 3538944 | tf_op jit(solution)/shard_map/all_to_all | solution.py:255
  1080.6 7.1 copy-start.11
  1080.6 68.3 %all-to-all-start.7 = ((bf16[2,1728,256]{2,0,1:T(2,128)(2,1)}), bf16[2,1728,256]{2,0,1:T(2,128)(2,1)}, u32[]{:S(2)}, u32[]{:S(2)}) async-start(bf16[2,1728,256]{2,0,1:T(2,128)(2,1)} %copy.148), calls=%async_computation.7 | async-start | bytes 3538944 | tf_op jit(solution)/shard_map/all_to_all | solution.py:257
  1085.0 242.2 %reduce-scatter.5.cloned.1.call-start = ((), (), s32[]{:S(2)}) async-start(), calls=%async_computation.12 | async-start | bytes 12976128 | tf_op jit(solution)/shard_map/reduce_scatter | solution.py:294
  1095.5 55.4 %copy-start.39 = (f32[2,1024]{1,0:T(2,128)S(1)}, f32[2,1024]{1,0:T(2,128)}, u32[]{:S(2)}) copy-start(f32[2,1024]{1,0:T(2,128)} %copy-done.37) | copy-start | bytes 24580
  1095.5 55.5 %copy-start.46 = (f32[1024]{0:T(1024)S(1)}, f32[1024]{0:T(1024)}, u32[]{:S(2)}) copy-start(f32[1024]{0:T(1024)} %copy-done.44) | copy-start | bytes 12292
  1148.9 3.1 copy-start.30
  1161.7 531.8 %reduce-scatter.11.cloned.1.call-start = ((), (), s32[]{:S(2)}) async-start(), calls=%async_computation.15 | async-start | bytes 17301504 | tf_op jit(solution)/shard_map/reduce_scatter | solution.py:303
  1177.8 880.6 %reduce-scatter.9.cloned.1.call-start = ((), (), s32[]{:S(2)}) async-start(), calls=%async_computation.14 | async-start | bytes 17301504 | tf_op jit(solution)/shard_map/reduce_scatter | solution.py:301
  1199.5 2.7 copy-start.20
  1202.2 856.3 %copy-start.1 = (bf16[1024,1024]{1,0:T(8,128)(2,1)S(1)}, bf16[1024,1024]{1,0:T(8,128)(2,1)}, u32[]{:S(2)}) copy-start(bf16[1024,1024]{1,0:T(8,128)(2,1)} %param.34) | copy-start | bytes 6291460
  (35 other events, 61.4 us)
Sparse Core Ops, SparseCore 0:
  959.4 205.2 reduce-scatter.6
  1171.3 155.8 reduce-scatter.4
  1330.1 363.2 reduce-scatter.10
  1696.3 362.1 reduce-scatter.8
where the time goes:
time: 2070 us
  waiting for transfers between devices  1130 us (55%)
  matrix products  460 us (22%)
  local copies, waits for them, and re-layouts  224 us (11%)
  other arithmetic  157 us (8%)
  blocking collectives  43 us (2%)
  starting transfers between devices  35.1 us (2%)
    reduce_scatter x1, waiting for transfers between devices, per_device(): lax.psum_scatter(grad_w_down, ('batch', 'seq'), scatter_dimension=0, tile...  366 us
    reduce_scatter x1, waiting for transfers between devices, per_device(): lax.psum_scatter(grad_w_up, ('batch', 'seq'), scatter_dimension=0, tiled=...  365 us
    convert_element_type x6, other arithmetic, per_block(): grad_scores = (prob_weights * (grad_probs - delta)).astype(jnp.bfloat16)  87.9 us
    dot_general x12, matrix products, per_block(): jnp.einsum('qhd,khd->hqk', query_heads, key_heads, preferred_element_type...  77.4 us
    dot_general x6, matrix products, per_block(): jnp.einsum('qhd,khd->hqk', grad_heads, value_heads, preferred_element_typ...  76.5 us
    reduce_scatter x1, waiting for transfers between devices, per_device(): lax.psum_scatter(grad_w_qkv, ('batch', 'seq'), scatter_dimension=0, tiled...  61.8 us
    all_to_all x1, waiting for transfers between devices, per_device(): lax.all_to_all(query_grads, 'seq', split_axis=1, concat_axis=2, tiled=True)  57 us
    dot_general x6, matrix products, per_block(): jnp.einsum('hqk,qhd->khd', prob_weights.astype(jnp.bfloat16), grad_heads,...  55.9 us
  transfers between devices with their start and end apart: 12, of which 11 were waited for; matrix products, arithmetic and copies ran while one was open for 7% of the time, Pallas kernels for 0%

commit v1 on v0

--- a/solution.py
+++ b/solution.py
@@ -1,11 +1,134 @@
+import functools
+
 import jax
 import jax.numpy as jnp
 from jax import lax
+from jax.experimental import pallas as pl
+from jax.experimental.pallas import tpu as pltpu
 from jax.sharding import PartitionSpec as P
 
 D = 1024
 HEADS = 16
 TSTEPS = 5000
+AXES = ("batch", "seq")
+
+
+BF=jnp.bfloat16; F32=jnp.float32
+NT=(((1,),(1,)),((),())); NN=(((1,),(0,)),((),())); TN=(((0,),(0,)),((),()))
+def dot(a,b,d): return lax.dot_general(a,b,d,preferred_element_type=F32)
+FILLED=1664; PAD=64
+def lanes(rows):
+    return lax.broadcasted_iota(jnp.int32,(rows,128),1)
+def parts3(x):
+    a=x.astype(BF).astype(F32); r=x-a; b=r.astype(BF).astype(F32); c=r-b
+    return a,b,c
+def augment(base,h,x,lane):
+    a,b,c=parts3(x)
+    o=(1-h)*64
+    f=base.astype(F32)
+    f=jnp.where((lane>=o)&(lane<o+64),jnp.where(lane==o,a,jnp.where(lane==o+1,b,jnp.where(lane==o+2,c,0.0))),f)
+    return f.astype(BF)
+def ones3(base,h,lane,n=3):
+    o=(1-h)*64
+    f=base.astype(F32)
+    f=jnp.where((lane>=o)&(lane<o+64),jnp.where(lane<o+n,1.0,0.0),f)
+    return f.astype(BF)
+def fwd_item(q_ref,k_ref,v_ref,o_ref,ol_ref,qa_ref,off,n,bq):
+    k=k_ref[pl.ds(off,n),:]
+    v=v_ref[pl.ds(off,n),:]
+    lk=lanes(n)
+    vs=[ones3(v,h,lk,1) for h in (0,1)]
+    lq=lanes(bq)
+    for r in range(n//bq):
+        rows=pl.ds(off+r*bq,bq)
+        q=q_ref[rows,:]
+        outs=[]
+        for h in (0,1):
+            qh=jnp.where((lq//64)==h,q.astype(F32),0.0).astype(BF)
+            s=dot(qh,k,NT)
+            m=jnp.max(s,axis=1,keepdims=True)
+            p=jnp.exp2(s-m).astype(BF)
+            o=dot(p,vs[h],NN)
+            l=o[:,(1-h)*64:(1-h)*64+1]
+            outs.append(o/l)
+            qa_ref[h,rows,:]=augment(q,h,-(m+jnp.log2(l)),lq)
+        o=jnp.where(lq<64,outs[0],outs[1])
+        o_ref[rows,:]=o.astype(BF)
+        ol_ref[rows,:]=(o-o.astype(BF).astype(F32)).astype(BF)
+def walk(seg_ref,item,bs):
+    single=seg_ref[0]==seg_ref[12]
+    @pl.when(single)
+    def _():
+        item(0,FILLED,bs[0])
+    @pl.when(jnp.logical_not(single))
+    def _():
+        def step(i,c):
+            me=seg_ref[i]
+            first=(i==0)|(seg_ref[jnp.maximum(i-1,0)]!=me)
+            last3=jnp.minimum(i+3,12)
+            long=first&(i+3<=12)&(seg_ref[last3]==me)
+            off=pl.multiple_of(i*128,128)
+            @pl.when(long)
+            def _(): item(off,512,bs[1])
+            @pl.when(first&jnp.logical_not(long))
+            def _(): item(off,128,bs[2])
+            return c
+        lax.fori_loop(0,13,step,0)
+    item(FILLED,PAD,PAD)
+def fwd_kernel(bs,seg_ref,q_ref,k_ref,v_ref,o_ref,ol_ref,qa_ref):
+    walk(seg_ref,functools.partial(fwd_item,q_ref,k_ref,v_ref,o_ref,ol_ref,qa_ref),bs)
+def attn_fwd(seg13,qkv,bs=(832,256,128)):
+    L,W3=qkv.shape; W=W3//3; n=W//128
+    spec=lambda j: pl.BlockSpec((L,128),lambda p,s,j=j:(0,p+j*n))
+    return pl.pallas_call(functools.partial(fwd_kernel,bs),
+        out_shape=(jax.ShapeDtypeStruct((L,W),BF),)*2+(jax.ShapeDtypeStruct((2*n,L,128),BF),),
+        grid_spec=pltpu.PrefetchScalarGridSpec(num_scalar_prefetch=1,grid=(n,),
+            in_specs=[spec(0),spec(1),spec(2)],
+            out_specs=(pl.BlockSpec((L,128),lambda p,s:(0,p)),pl.BlockSpec((L,128),lambda p,s:(0,p)),pl.BlockSpec((2,L,128),lambda p,s:(p,0,0)))),
+        compiler_params=pltpu.CompilerParams(vmem_limit_bytes=50<<20),name="attn_forward",
+        cost_estimate=pl.CostEstimate(flops=2*2*2*n*L*L*256,bytes_accessed=10*L*W,transcendentals=2*n*L*L))(seg13,qkv,qkv,qkv)
+def bwd_item(mode,qa_ref,k_ref,v_ref,o_ref,ol_ref,g_ref,dq_ref,dk_ref,dv_ref,acc,off,n,bk):
+    item=pl.ds(off,n)
+    ln=lanes(n)
+    g=g_ref[item,:]
+    prod=g.astype(F32)*(o_ref[item,:].astype(F32)+ol_ref[item,:].astype(F32))
+    lb=lanes(bk)
+    nb=n//bk
+    gas=[augment(g,h,-jnp.sum(jnp.where((ln//64)==h,prod,0.0),axis=1,keepdims=True),ln) for h in (0,1)]
+    for b in range(nb):
+        rows=pl.ds(off+b*bk,bk)
+        k=k_ref[rows,:]; v=v_ref[rows,:]
+        dks=[];dvs=[]
+        for h in (0,1):
+            ga=gas[h]
+            qa=qa_ref[h,item,:]
+            kh=ones3(k,h,lb); vh=ones3(v,h,lb)
+            p=jnp.exp2(dot(kh,qa,NT))
+            d=dot(vh,ga,NT)
+            ds=(p*d).astype(BF)
+            dvs.append(dot(p.astype(BF),ga,NN))
+            dks.append(dot(ds,qa,NN))
+            if mode=='TN':
+                dq=dot(ds,kh,TN)
+                if b==0: acc[h,item,:]=dq
+                else: acc[h,item,:]+=dq
+        dk_ref[rows,:]=(jnp.where(lb<64,dks[0],dks[1])*0.6931471805599453).astype(BF)
+        dv_ref[rows,:]=jnp.where(lb<64,dvs[0],dvs[1]).astype(BF)
+    dq_ref[item,:]=(jnp.where(ln<64,acc[0,item,:],acc[1,item,:])*0.125).astype(BF)
+def bwd_kernel(bs,mode,seg_ref,qa_ref,k_ref,v_ref,o_ref,ol_ref,g_ref,dq_ref,dk_ref,dv_ref,acc):
+    walk(seg_ref,functools.partial(bwd_item,mode,qa_ref,k_ref,v_ref,o_ref,ol_ref,g_ref,dq_ref,dk_ref,dv_ref,acc),bs)
+def attn_bwd(seg13,qa,qkv,o,ol,g,bs=(832,256,128),mode='TN'):
+    L,W3=qkv.shape; W=W3//3; n=W//128
+    spec=lambda j: pl.BlockSpec((L,128),lambda p,s,j=j:(0,p+j*n))
+    one=pl.BlockSpec((L,128),lambda p,s:(0,p))
+    return pl.pallas_call(functools.partial(bwd_kernel,bs,mode),
+        out_shape=(jax.ShapeDtypeStruct((L,W),BF),)*3,
+        grid_spec=pltpu.PrefetchScalarGridSpec(num_scalar_prefetch=1,grid=(n,),
+            in_specs=[pl.BlockSpec((2,L,128),lambda p,s:(p,0,0)),spec(1),spec(2),one,one,one],
+            out_specs=(one,one,one),
+            scratch_shapes=[pltpu.VMEM((2,L,128),F32)]),
+        compiler_params=pltpu.CompilerParams(vmem_limit_bytes=50<<20),name="attn_backward",
+        cost_estimate=pl.CostEstimate(flops=5*2*2*n*L*L*256,bytes_accessed=16*L*W,transcendentals=2*n*L*L))(seg13,qa,qkv,qkv,o,ol,g)
 
 
 def gelu_exact(values):
@@ -328,6 +451,317 @@
     )
 
 
+LOG2E = 1.4426950408889634
+
+
+class Plan:
+    def __init__(self, mesh):
+        sizes = dict(mesh.shape)
+        self.batch, self.depth = sizes["batch"], sizes["seq"]
+        chips = self.batch // 2
+        side = 1
+        while side * side < chips:
+            side *= 2
+        self.nx, self.ny = side, chips // side
+
+    def perm(self, target):
+        pairs = []
+        for y in range(self.ny):
+            for x in range(self.nx):
+                for c in range(2):
+                    for z in range(self.depth):
+                        to = target(y, x, c, z)
+                        if to is not None:
+                            pairs.append((self.index(y, x, c, z), self.index(*to)))
+        return pairs
+
+    def index(self, y, x, c, z):
+        return ((y * self.nx + x) * 2 + c) * self.depth + z
+
+    def send(self, value, target):
+        return lax.ppermute(value, AXES, self.perm(target))
+
+    def sibling(self, value):
+        return self.send(value, lambda y, x, c, z: (y, x, 1 - c, z))
+
+
+def pick(array, index, axis):
+    return lax.dynamic_index_in_dim(array, index, axis, keepdims=False)
+
+
+def scatter_sum(plan, terms, order, where):
+    y, x, z = where
+    for axis in order:
+        if axis == "x":
+            if plan.nx == 1:
+                terms = terms[:, 0]
+                continue
+            at = terms.ndim - 4
+            total = pick(terms, x, at).astype(F32)
+            for r in range(1, plan.nx):
+                got = plan.send(
+                    pick(terms, (x + r) % plan.nx, at),
+                    lambda y, x, c, z, r=r: (y, (x + r) % plan.nx, c, z),
+                )
+                total = total + got.astype(F32)
+        else:
+            total = pick(terms, y, 0).astype(F32)
+            for r in range(1, plan.ny):
+                got = plan.send(
+                    pick(terms, (y + r) % plan.ny, 0),
+                    lambda y, x, c, z, r=r: ((y + r) % plan.ny, x, c, z),
+                )
+                total = total + got.astype(F32)
+        terms = total.astype(terms.dtype)
+    total = pick(terms, z, 0).astype(F32)
+    for r in range(1, plan.depth):
+        got = plan.send(
+            pick(terms, (z + r) % plan.depth, 0),
+            lambda y, x, c, z, r=r: (y, x, c, (z + r) % plan.depth),
+        )
+        total = total + got.astype(F32)
+    return total
+
+
+def per_chip(
+    plan,
+    inputs,
+    timesteps,
+    segments,
+    cotangent,
+    w_qkv,
+    b_query,
+    b_value,
+    w_out,
+    b_out,
+    ln1_gain,
+    ln1_bias,
+    w_up,
+    b_up,
+    w_down,
+    b_down,
+    ln2_gain,
+    ln2_bias,
+    w_time,
+    b_time,
+):
+    local_len = inputs.shape[1]
+    rows = 2 * local_len
+    length = segments.shape[1]
+    b = lax.axis_index("batch")
+    z = lax.axis_index("seq")
+    c, x, y = b % 2, (b // 2) % plan.nx, b // 2 // plan.nx
+    part = z % 2
+    where = (y, x, z)
+    first = (segments[1, 0] == segments[1, 128 * 12]).astype(jnp.int32)
+    which = lambda s: (first + s) % 2
+    facts = jnp.concatenate(
+        [segments[:, : 128 * 13 : 128], timesteps[:, None], jnp.zeros((2, 2), jnp.int32)], axis=1
+    )
+    facts = jnp.stack([pick(facts, which(0), 0), pick(facts, which(1), 0)])
+    other_facts = plan.sibling(facts)
+    facts = jnp.where(z // 2 == c, facts, other_facts)
+    mine = pick(facts, z % 2, 0)
+    seg13 = mine[:13]
+    fraction = mine[13].astype(F32) / TSTEPS
+
+    def gather_rows(array):
+        got = [
+            plan.send(
+                pick(array, which((part + j) % 2), 0),
+                lambda y, x, c, z, j=j: (y, x, z // 2, 2 * c + (z + j) % 2),
+            )
+            for j in (0, 1)
+        ]
+        return jnp.concatenate(
+            [jnp.where(part == 0, got[0], got[1]), jnp.where(part == 0, got[1], got[0])], axis=0
+        )
+
+    def spread_rows(array):
+        array = array.reshape(2, local_len, array.shape[-1])
+        got = [
+            plan.send(
+                pick(array, (part + j) % 2, 0),
+                lambda y, x, c, z, j=j: (y, x, z // 2, 2 * c + (z + j) % 2),
+            )
+            for j in (0, 1)
+        ]
+        swap = (part + first) % 2
+        return jnp.stack(
+            [jnp.where(swap == 0, got[0], got[1]), jnp.where(swap == 0, got[1], got[0])], axis=0
+        )
+
+    def whole(own, other):
+        return jnp.where(c == 0, jnp.concatenate([own, other]), jnp.concatenate([other, own]))
+
+    def halves(array, axis):
+        shape = array.shape
+        cut = shape[:axis] + (plan.ny * plan.nx, 2, -1) + shape[axis + 1 :]
+        flat = shape[:axis] + (-1,) + shape[axis + 1 :]
+        split = array.reshape(cut)
+        return (
+            pick(split, c, axis + 1).reshape(flat),
+            pick(split, 1 - c, axis + 1).reshape(flat),
+        )
+
+    def blocks(array):
+        return array.reshape(plan.ny, plan.nx, plan.depth, -1, array.shape[-1])
+
+    model = inputs.shape[-1]
+    own_inputs = gather_rows(inputs)
+    own_cotangent = gather_rows(cotangent)
+    start = (
+        own_inputs.astype(F32) + fraction * w_time.astype(F32)[None] + b_time.astype(F32)[None]
+    )
+    start_low = start.astype(BF)
+    start_full = whole(start_low, plan.sibling(start_low))
+    w_three = w_qkv.reshape(model, 3, model)
+    w_own = jnp.concatenate([halves(w_three[:, i], 1)[0] for i in range(3)], axis=1)
+    w_oth = jnp.concatenate([halves(w_three[:, i], 1)[1] for i in range(3)], axis=1)
+    half = model // 2
+    bias = jnp.concatenate(
+        [
+            halves(b_query.astype(F32), 0)[0],
+            jnp.zeros((half,), F32),
+            halves(b_value.astype(F32), 0)[0],
+        ]
+    )
+    scale = jnp.where(jnp.arange(3 * half) < half, 0.125 * LOG2E, 1.0)
+    qkv = ((jnp.dot(start_full, w_own, preferred_element_type=F32) + bias) * scale).astype(BF)
+    context, context_rest, query_rows = attn_fwd(seg13, qkv)
+    my_ctx, away_ctx = pick(context.reshape(2, rows, half), c, 0), pick(
+        context.reshape(2, rows, half), 1 - c, 0
+    )
+    ctx_rows = jnp.concatenate([my_ctx, plan.sibling(away_ctx)], axis=1)
+    w_out_own, w_out_oth = halves(w_out, 0)
+    w_out_cat = jnp.concatenate([w_out_own, w_out_oth])
+    residual_one = (
+        start + jnp.dot(ctx_rows, w_out_cat, preferred_element_type=F32) + b_out.astype(F32)
+    )
+    normed, unit_one, inverse_one = norm_forward(
+        residual_one, ln1_gain.astype(F32), ln1_bias.astype(F32)
+    )
+    normed_low = normed.astype(BF)
+    hidden_pre = jnp.dot(normed_low, w_up, preferred_element_type=F32) + b_up.astype(F32)
+    activated, gelu_pull = jax.vjp(gelu_exact, hidden_pre)
+    activated_low = activated.astype(BF)
+    residual_two = (
+        normed
+        + jnp.dot(activated_low, w_down, preferred_element_type=F32)
+        + b_down.astype(F32)
+    )
+    result, unit_two, inverse_two = norm_forward(
+        residual_two, ln2_gain.astype(F32), ln2_bias.astype(F32)
+    )
+    output = spread_rows(result.astype(BF))
+    grad_result = own_cotangent.astype(F32)
+    grad_two, grad_ln2_gain, grad_ln2_bias = norm_backward(
+        grad_result, unit_two, inverse_two, ln2_gain.astype(F32)
+    )
+    grad_b_down = jnp.sum(grad_two, axis=0)
+    grad_two_low = grad_two.astype(BF)
+    act_own, act_oth = halves(activated_low, 1)
+    down_away = lax.dot_general(act_oth, grad_two_low, TN, preferred_element_type=F32).astype(BF)
+    down_got = plan.sibling(down_away)
+    grad_activated = lax.dot_general(grad_two_low, w_down, NT, preferred_element_type=F32)
+    grad_hidden = gelu_pull(grad_activated)[0]
+    grad_b_up = jnp.sum(grad_hidden, axis=0)
+    grad_hidden_low = grad_hidden.astype(BF)
+    grad_normed = grad_two + lax.dot_general(
+        grad_hidden_low, w_up, NT, preferred_element_type=F32
+    )
+    nl_own, nl_oth = halves(normed_low, 1)
+    up_away = lax.dot_general(nl_oth, grad_hidden_low, TN, preferred_element_type=F32).astype(BF)
+    up_got = plan.sibling(up_away)
+    grad_one, grad_ln1_gain, grad_ln1_bias = norm_backward(
+        grad_normed, unit_one, inverse_one, ln1_gain.astype(F32)
+    )
+    grad_b_out = jnp.sum(grad_one, axis=0)
+    grad_one_low = grad_one.astype(BF)
+    grad_one_full = whole(grad_one_low, plan.sibling(grad_one_low))
+    down_sum = (
+        lax.dot_general(act_own, grad_two_low, TN, preferred_element_type=F32)
+        + down_got.astype(F32)
+    ).astype(BF)
+    sum_w_down = scatter_sum(plan, blocks(down_sum), "xy", where)
+    up_sum = (
+        lax.dot_general(nl_own, grad_hidden_low, TN, preferred_element_type=F32)
+        + up_got.astype(F32)
+    ).astype(BF)
+    sum_w_up = scatter_sum(plan, blocks(up_sum), "yx", where)
+    out_sum = lax.dot_general(context, grad_one_full, TN, preferred_element_type=F32).astype(BF)
+    sum_w_out = scatter_sum(plan, blocks(out_sum), "xy", where)
+    grad_context = lax.dot_general(
+        grad_one_full, w_out_own, NT, preferred_element_type=F32
+    ).astype(BF)
+    grads = attn_bwd(seg13, query_rows, qkv, context, context_rest, grad_context)
+    grad_qkv = jnp.concatenate(grads, axis=1)
+    both = grad_qkv.reshape(2, rows, 3 * half)
+    qkv_mine = pick(both, c, 0)
+    qkv_got = plan.sibling(pick(both, 1 - c, 0))
+    grad_start = (
+        grad_one
+        + lax.dot_general(qkv_mine, w_own, NT, preferred_element_type=F32)
+        + lax.dot_general(qkv_got, w_oth, NT, preferred_element_type=F32)
+    )
+    grad_inputs = spread_rows(grad_start.astype(BF))
+    sf_own, sf_oth = halves(start_full, 1)
+    qkv_away = lax.dot_general(sf_oth, grad_qkv, TN, preferred_element_type=F32).astype(BF)
+    qkv_keep = lax.dot_general(sf_own, grad_qkv, TN, preferred_element_type=F32).astype(BF)
+    qkv_cross = plan.sibling(qkv_away)
+    sum_own = scatter_sum(plan, blocks(qkv_keep), "xy", where)
+    sum_oth = scatter_sum(plan, blocks(qkv_cross), "yx", where)
+    quads = plan.ny * plan.nx
+    pair = jnp.where(c == 0, jnp.stack([sum_own, sum_oth]), jnp.stack([sum_oth, sum_own]))
+    sum_w_qkv = (
+        pair.reshape(2, -1, 3, quads, half // quads).transpose(1, 2, 3, 0, 4).reshape(-1, 3 * model)
+    )
+    grad_b_own = jnp.sum(grad_qkv.astype(F32), axis=0)
+    grad_b_time = jnp.sum(grad_start, axis=0)
+    grad_w_time = fraction * grad_b_time
+    zero = jnp.zeros((quads, 2, half // quads), F32)
+
+    def placed(v):
+        return lax.dynamic_update_index_in_dim(zero, v.reshape(quads, half // quads), c, 1).reshape(-1)
+
+    vectors = [
+        placed(grad_b_own[:half]),
+        placed(grad_b_own[2 * half :]),
+        grad_b_out,
+        grad_ln1_gain,
+        grad_ln1_bias,
+        grad_b_down,
+        grad_ln2_gain,
+        grad_ln2_bias,
+        grad_w_time,
+        grad_b_time,
+    ]
+    small = jnp.concatenate([v[:, None] for v in vectors] + [grad_b_up.reshape(model, -1)], axis=1)
+    small_own, small_oth = halves(small, 0)
+    small_own = small_own + plan.sibling(small_oth)
+    small_sum = scatter_sum(plan, blocks(small_own), "xy", where)
+    v = [small_sum[:, i] for i in range(10)]
+    return (
+        output,
+        grad_inputs,
+        sum_w_qkv,
+        v[0],
+        v[1],
+        sum_w_out,
+        v[2],
+        v[3],
+        v[4],
+        sum_w_up,
+        small_sum[:, 10:].reshape(-1),
+        sum_w_down,
+        v[5],
+        v[6],
+        v[7],
+        v[8],
+        v[9],
+    )
+
+
 def solution(mesh):
     placed = (
         P("batch", "seq", None),
@@ -350,8 +784,12 @@
         P(),
         P(),
     )
+    sizes = dict(mesh.shape)
+    body = per_device
+    if sizes["seq"] == 4 and sizes["batch"] % 2 == 0:
+        body = functools.partial(per_chip, Plan(mesh))
     return jax.shard_map(
-        per_device,
+        body,
         mesh=mesh,
         in_specs=placed,
         out_specs=(

time: 2070 us -> 797 us (0.39)
  waiting for transfers between devices: 1130 us -> 169 us
  matrix products: 460 us -> 172 us
  Pallas kernels: 0 us -> 107 us
  other arithmetic: 157 us -> 50.5 us
  starting transfers between devices: 35.1 us -> 121 us
  local copies, waits for them, and re-layouts: 224 us -> 162 us
  blocking collectives: 43 us -> 0 us
    reduce_scatter x4 -> x0, waiting for transfers between devices: 793 us -> none  [the longest x1 366 us: per_device(): lax.psum_scatter(grad_w_down, ('batch', 'seq'), scatter_dimension=0, tile...]
    all_to_all x8 -> x0, waiting for transfers between devices: 336 us -> none  [the longest x1 57 us: per_device(): lax.all_to_all(query_grads, 'seq', split_axis=1, concat_axis=2, tiled=True)]
    dot_general x55 -> x16, matrix products: 460 us -> 172 us  [the longest x1 41.7 us: per_chip(): jnp.dot(normed_low, w_up, preferred_element_type=F32) + b_up.astype(F32)]
    ppermute x0 -> x47, waiting for transfers between devices: none -> 169 us  [send(): return lax.ppermute(value, AXES, self.perm(target))]
    ppermute x0 -> x47, starting transfers between devices: none -> 121 us  [send(): return lax.ppermute(value, AXES, self.perm(target))]
    pallas_call x0 -> x2, Pallas kernels: none -> 107 us  [the longest x1 67.3 us: attn_bwd(): pl.pallas_call(functools.partial(bwd_kernel, bs, mode), out_shape=(jax.Sh...]
    convert_element_type x22, other arithmetic: 99.1 us -> 21.9 us  [the longest x10 10.7 us: scatter_sum(): terms = total.astype(terms.dtype)]
    while x62 -> x0, local copies, waits for them, and re-layouts: 54.7 us -> none  [the longest x3 25.2 us: attention_backward(): lax.map(per_sequence, (query_all, key_all, value_all, segments, logsums,...]
  transfers between devices with their start and end apart: 12 -> 47, of which waited for: 11 -> 20; matrix products, arithmetic and copies ran while one was open for 7% -> 33% of each run, Pallas kernels for 0% -> 9%
where the time goes in v1:
time: 797 us; the launch traced here: 785 us
  matrix products  172 us (22%)
  waiting for transfers between devices  169 us (21%)
  local copies, waits for them, and re-layouts  162 us (20%)
  starting transfers between devices  121 us (15%)
  Pallas kernels  107 us (13%)
  other arithmetic  50.5 us (6%)
    ppermute x47, waiting for transfers between devices, send(): return lax.ppermute(value, AXES, self.perm(target))  169 us
    ppermute x47, starting transfers between devices, send(): return lax.ppermute(value, AXES, self.perm(target))  121 us
    pallas_call x1, Pallas kernels, attn_bwd(): pl.pallas_call(functools.partial(bwd_kernel, bs, mode), out_shape=(jax.Sh...  67.3 us
    unnamed x157, local copies, waits for them, and re-layouts  62.1 us
    dot_general x1, matrix products, per_chip(): jnp.dot(normed_low, w_up, preferred_element_type=F32) + b_up.astype(F32)  41.7 us
    pallas_call x1, Pallas kernels, attn_fwd(): pl.pallas_call(functools.partial(fwd_kernel, bs), out_shape=(jax.ShapeDty...  39.6 us
    dynamic_slice x11, local copies, waits for them, and re-layouts, pick(): return lax.dynamic_index_in_dim(array, index, axis, keepdims=False)  32.1 us
    dot_general x1, matrix products, per_chip(): lax.dot_general(grad_two_low, w_down, NT, preferred_element_type=F32)  23.4 us
  transfers between devices with their start and end apart: 47, of which 20 were waited for; matrix products, arithmetic and copies ran while one was open for 33% of the time, Pallas kernels for 9%

profile of v1, /device:TPU:0, one launch (start us, length us, event | category | flops | bytes accessed | tf_op | source)
XLA Modules:
  0.0 784.9 jit_solution(2126107766025184157)
XLA Ops:
  3.4 2.8 dynamic-slice_bitcast_fusion.8
  8.0 3.0 collective-permute-start.8
  12.4 8.2 %collective-permute-start = (bf16[432,1024]{1,0:T(8,128)(2,1)}, bf16[432,1024]{1,0:T(8,128)(2,1)}, u32[]{:S(2)}, u32[]{:S(2)}) collective-permute-start(bf16[432,1024]{1,0:T(8,128)(2,1)} %get-tuple-element.79), channel_id=1, source_target_pairs={{0,0},{1,1},{2,4},{3,5},{4,2},{5,3},{6,6},{7,7},{8,8},{9,9},{10,12... | collective-permute-start | bytes 2654216 | tf_op jit(solution)/shard_map/ppermute | solution.py:482
  24.2 7.3 collective-permute-done.8
  31.6 18.4 %collective-permute-done.1 = bf16[432,1024]{1,0:T(8,128)(2,1)S(1)} collective-permute-done((bf16[432,1024]{1,0:T(8,128)(2,1)}, bf16[432,1024]{1,0:T(8,128)(2,1)S(1)}, u32[]{:S(2)}, u32[]{:S(2)}) %collective-permute-start.1) | collective-permute-done | bytes 884768 | tf_op jit(solution)/shard_map/ppermute | solution.py:482
  50.9 2.9 broadcast_select_fusion.1
  55.5 38.9 %collective-permute-start.3 = (bf16[864,1024]{1,0:T(8,128)(2,1)}, bf16[864,1024]{1,0:T(8,128)(2,1)}, u32[]{:S(2)}, u32[]{:S(2)}) collective-permute-start(bf16[864,1024]{1,0:T(8,128)(2,1)} %fusion.20), channel_id=1, source_target_pairs={{0,4},{1,5},{2,6},{3,7},{4,0},{5,1},{6,2},{7,3},{8,12},{9,13},{10,... | collective-permute-start | bytes 5308424 | tf_op jit(solution)/shard_map/ppermute | solution.py:482
  96.2 8.7 %copy.136 = bf16[1024,3072]{0,1:T(8,128)(2,1)} copy(bf16[1024,3072]{1,0:T(8,128)(2,1)} %param.23) | data formatting | bytes 12582912 | tf_op args[4]
  106.7 3.0 constant_dynamic-slice_fusion.16
  109.8 3.6 fusion.95
  119.2 2.4 copy.138
  122.9 12.4 %multiply_convert_fusion.1.q_ref.k_ref.v_ref = bf16[1728,1536]{1,0:T(8,128)(2,1)} fusion(f32[1536]{0:T(1024)S(1)} %fusion.67, f32[1536]{0:T(1024)S(1)} %pad_maximum_fusion.7, bf16[864,1024]{1,0:T(8,128)(2,1)} %collective-permute-done.3, bf16[864,1024]{1,0:T(8,128)(2,1)} %fusion.20, pred[]{:T(512)S(6)} %eq.79, bf16[1024,512]{0,1:T(8,128)(2,1)} %bitcast.303, ...), kind=kOutput, calls=%fused_computation.18 | convolution fusion | flops 5469143040 | bytes 12005377 | tf_op jit(solution)/shard_map/dot_general | solution.py:630
  135.3 39.6 %attn_forward.1 = (bf16[1728,512]{1,0:T(8,128)(2,1)S(1)}, bf16[1728,512]{1,0:T(8,128)(2,1)S(1)}, bf16[8,1728,128]{2,1,0:T(8,128)(2,1)}) custom-call(s32[13]{0:T(128)S(1)} %slice_bitcast_fusion.12.seg_ref, bf16[1728,1536]{1,0:T(8,128)(2,1)} %multiply_convert_fusion.1.q_ref.k_ref.v_ref, bf16[1728,1536]{1,0:T(8,128)(2,1)} %multiply_convert_fusion.1.q_ref.k_ref.v_ref, ...), custom_call_target="tpu_custom_call" | custom-call | flops 24461180928 | bytes 8847360 | tf_op jit(solution)/shard_map/attn_forward/pallas_call | solution.py:83
  177.2 2.5 add_convert_fusion.2
  179.7 5.5 concatenate.92
  185.2 4.6 copy.141
  189.9 5.5 maximum_select_fusion
  199.1 3.4 fusion.98
  205.0 5.3 reshape.375
  210.3 41.7 %multiply_convert_fusion = (bf16[864,4096]{1,0:T(8,128)(2,1)}, f32[864,4096]{1,0:T(8,128)}, f32[864,4096]{1,0:T(8,128)}) fusion(f32[4096]{0:T(1024)} %convert_element_type.320, bf16[864,1024]{1,0:T(8,128)(2,1)} %fusion.28, bf16[1024,4096]{1,0:T(8,128)(2,1)} %param.30), kind=kOutput, calls=%fused_computation.3 | convolution fusion | flops 7481327616 | bytes 45563904 | tf_op jit(solution)/shard_map/dot_general | solution.py:645
  252.1 16.7 %reshape.380 = bf16[864,4,2,512]{3,2,1,0:T(2,128)(2,1)} reshape(bf16[864,4096]{1,0:T(8,128)(2,1)} %get-tuple-element.41) | data formatting | bytes 14155776 | tf_op jit(solution)/shard_map/reshape | solution.py:601
  268.8 12.6 %fusion.99 = (f32[864]{0:T(1024)S(1)}, f32[864,1024]{1,0:T(8,128)S(1)}) fusion(f32[1024]{0:T(1024)} %convert_element_type.322, bf16[864,4096]{1,0:T(8,128)(2,1)} %get-tuple-element.41, bf16[4096,1024]{1,0:T(8,128)(2,1)} %param.32, f32[1024]{0:T(1024)} %convert_element_type.318, f32[1024]{0:T(1024)S(1)} %convert_element_type.317, ...), kind=kOutput, calls=%fused_computation.272 | convolution fusion | flops 7253949440 | bytes 22567040 | tf_op jit(solution)/shard_map/dot_general | solution.py:650
  284.9 3.9 fusion.91
  290.2 8.4 %collective-permute-start.5 = (bf16[432,1024]{1,0:T(8,128)(2,1)}, bf16[432,1024]{1,0:T(8,128)(2,1)}, u32[]{:S(2)}, u32[]{:S(2)}) collective-permute-start(bf16[432,1024]{1,0:T(8,128)(2,1)} %get-tuple-element.73), channel_id=1, source_target_pairs={{0,0},{1,1},{2,4},{3,5},{4,2},{5,3},{6,6},{7,7},{8,8},{9,9},{10,12... | collective-permute-start | bytes 2654216 | tf_op jit(solution)/shard_map/ppermute | solution.py:482
  298.6 4.5 collective-permute-start.6
  303.1 23.4 %fusion.100 = (f32[4096]{0:T(1024)}, bf16[864,4096]{1,0:T(8,128)(2,1)}) fusion(f32[864,4096]{1,0:T(8,128)} %get-tuple-element.42, bf16[4096,1024]{1,0:T(8,128)(2,1)} %param.32, f32[864,1024]{1,0:T(8,128)} %get-tuple-element.38, f32[864,4096]{1,0:T(8,128)} %get-tuple-element.120, f32[4096]{0:T(1024)} %convert_element_type.320), kind=kOutput, calls=%fused_computation.273 | convolution fusion | flops 7305261056 | bytes 47349760 | tf_op jit(solution)/shard_map/dot_general | solution.py:666
  326.5 14.2 %multiply_reduce_fusion = (f32[1024]{0:T(1024)}, f32[864]{0:T(1024)S(1)}, f32[864]{0:T(1024)S(1)}, f32[1024]{0:T(1024)}, f32[864,1024]{1,0:T(8,128)S(1)}) fusion(f32[864,1024]{1,0:T(8,128)S(1)} %get-tuple-element.119, f32[864]{0:T(1024)S(1)} %add_rsqrt_fusion.1, f32[864]{0:T(1024)S(1)} %broadcast_multiply_fusion.6, f32[1024]{0:T(1024)S(1)} %convert_element_type.317, ...), kind=kOutput, calls=%fused_computation.46 | convolution fusion | flops 7256600576 | bytes 26109440 | tf_op jit(solution)/shard_map/dot_general | solution.py:670
  347.1 4.8 constant_dynamic-slice_fusion.3
  352.0 4.4 copy.171
  356.4 9.3 %convolution_convert_fusion = bf16[512,4096]{1,0:T(8,128)(2,1)} fusion(bf16[864,512]{0,1:T(8,128)(2,1)S(1)} %bitcast.313, bf16[864,4096]{1,0:T(8,128)(2,1)} %get-tuple-element.126), kind=kOutput, calls=%fused_computation.21 | convolution fusion | flops 3625975808 | bytes 12156928 | tf_op jit(solution)/shard_map/dot_general | solution.py:674
  366.2 17.6 %constant_dynamic-slice_fusion.1 = (bf16[864,4,1,512]{3,2,1,0:T(2,128)(2,1)}, bf16[864,4,1,512]{3,2,1,0:T(2,128)(2,1)}) fusion(bf16[864,4,2,512]{3,2,1,0:T(2,128)(2,1)} %reshape.380, s32[]{:T(128)S(6)} %select_n.392, s32[]{:T(128)S(6)} %select_n.394), kind=kLoop, calls=%fused_computation.187 | loop fusion | bytes 14155784 | tf_op jit(solution)/shard_map/jit(dynamic_index_in_dim)/dynamic_slice | solution.py:489
  383.9 3.4 copy.170
  387.2 17.7 %copy.173 = bf16[864,4,1,512]{0,3,1,2:T(8,128)(2,1)} copy(bf16[864,4,1,512]{3,2,1,0:T(2,128)(2,1)} %get-tuple-element.44) | data formatting | bytes 7077888
  405.0 17.9 %copy.172 = bf16[864,4,1,512]{0,3,1,2:T(8,128)(2,1)} copy(bf16[864,4,1,512]{3,2,1,0:T(2,128)(2,1)} %get-tuple-element.43) | data formatting | bytes 7077888
  422.9 8.2 %convolution_convert_fusion.1 = bf16[2048,1024]{1,0:T(8,128)(2,1)} fusion(bf16[864,2048]{0,1:T(8,128)(2,1)} %bitcast.289, f32[864,1024]{1,0:T(8,128)S(1)} %copy-done.15), kind=kOutput, calls=%fused_computation.32 | convolution fusion | flops 3626860544 | bytes 11272192 | tf_op jit(solution)/shard_map/dot_general | solution.py:664
  434.1 6.5 convolution_convert_fusion.2.g_ref
  440.7 67.3 %attn_backward.1 = (bf16[1728,512]{1,0:T(8,128)(2,1)S(1)}, bf16[1728,512]{1,0:T(8,128)(2,1)S(1)}, bf16[1728,512]{1,0:T(8,128)(2,1)}) custom-call(s32[13]{0:T(128)S(1)} %slice_bitcast_fusion.12.seg_ref, bf16[8,1728,128]{2,1,0:T(8,128)(2,1)} %get-tuple-element.24.qa_ref, bf16[1728,1536]{1,0:T(8,128)(2,1)} %multiply_convert_fusion.1.q_ref.k_ref.v_ref, ...), custom_call_target="tpu_custom_call" | custom-call | flops 61152952320 | bytes 14155776 | tf_op jit(solution)/shard_map/attn_backward/pallas_call | solution.py:124
  512.7 3.0 convolution_convert_fusion.3
  515.8 3.0 convolution_convert_fusion.4
  520.6 5.4 convolution_convert_fusion.5
  526.8 4.7 fusion.29
  531.5 18.6 %collective-permute-done.30 = bf16[2,4,32,1024]{3,2,1,0:T(8,128)(2,1)S(1)} collective-permute-done((bf16[2,4,32,1024]{3,2,1,0:T(8,128)(2,1)S(1)}, bf16[2,4,32,1024]{3,2,1,0:T(8,128)(2,1)S(1)}, u32[]{:S(2)}, u32[]{:S(2)}) %collective-permute-start.30) | collective-permute-done | bytes 524320 | tf_op jit(solution)/shard_map/ppermute | solution.py:482
  552.8 6.8 collective-permute-done.31
  559.9 6.9 collective-permute-done.14
  566.8 2.5 collective-permute-start.33
  571.5 2.7 collective-permute-start.17
  579.0 2.7 collective-permute-done.16
  581.7 2.6 collective-permute-done.15
  586.7 4.8 collective-permute-done.19
  595.4 9.1 %add_convert_fusion.1 = bf16[512,4096]{1,0:T(8,128)(2,1)S(1)} fusion(bf16[512,4096]{1,0:T(8,128)(2,1)} %collective-permute-done.35, bf16[864,512]{0,1:T(8,128)(2,1)} %bitcast.312, bf16[864,4096]{1,0:T(8,128)(2,1)} %get-tuple-element.126), kind=kOutput, calls=%fused_computation.20 | convolution fusion | flops 3630170112 | bytes 16351232 | tf_op jit(solution)/shard_map/dot_general | solution.py:688
  604.6 7.3 fusion.96
  618.9 7.4 add_convert_fusion
  628.5 34.1 %collective-permute-done.26 = f32[4,32,14]{1,0,2:T(4,128)S(1)} collective-permute-done((f32[4,32,14]{1,0,2:T(4,128)S(1)}, f32[4,32,14]{1,0,2:T(4,128)S(1)}, u32[]{:S(2)}, u32[]{:S(2)}) %collective-permute-start.26) | collective-permute-done | bytes 7200 | tf_op jit(solution)/shard_map/ppermute | solution.py:482
  674.1 2.4 collective-permute-done.23
  676.5 8.4 %collective-permute-start.11 = (bf16[432,1024]{1,0:T(8,128)(2,1)}, bf16[432,1024]{1,0:T(8,128)(2,1)}, u32[]{:S(2)}, u32[]{:S(2)}) collective-permute-start(bf16[432,1024]{1,0:T(8,128)(2,1)} %get-tuple-element.65), channel_id=1, source_target_pairs={{0,0},{1,1},{2,4},{3,5},{4,2},{5,3},{6,6},{7,7},{8,8},{9,9},{10,12... | collective-permute-start | bytes 2654216 | tf_op jit(solution)/shard_map/ppermute | solution.py:482
  684.9 3.6 collective-permute-start.12
  689.3 3.1 fusion.10
  695.0 21.1 %collective-permute-done.12 = bf16[432,1024]{1,0:T(8,128)(2,1)} collective-permute-done((bf16[432,1024]{1,0:T(8,128)(2,1)}, bf16[432,1024]{1,0:T(8,128)(2,1)}, u32[]{:S(2)}, u32[]{:S(2)}) %collective-permute-start.12) | collective-permute-done | bytes 884768 | tf_op jit(solution)/shard_map/ppermute | solution.py:482
  719.1 2.6 fusion.9
  723.3 12.3 %collective-permute-done.37 = bf16[4,32,4096]{2,1,0:T(8,128)(2,1)} collective-permute-done((bf16[4,32,4096]{2,1,0:T(8,128)(2,1)S(1)}, bf16[4,32,4096]{2,1,0:T(8,128)(2,1)}, u32[]{:S(2)}, u32[]{:S(2)}) %collective-permute-start.37) | collective-permute-done | bytes 1048608 | tf_op jit(solution)/shard_map/ppermute | solution.py:482
  737.2 2.6 collective-permute-start.40
  746.5 11.6 %collective-permute-start.44 = (bf16[128,1024]{1,0:T(8,128)(2,1)S(1)}, bf16[128,1024]{1,0:T(8,128)(2,1)S(1)}, u32[]{:S(2)}, u32[]{:S(2)}) collective-permute-start(bf16[128,1024]{1,0:T(8,128)(2,1)S(1)} %get-tuple-element.81), channel_id=1, source_target_pairs={{0,1},{1,2},{2,3},{3,0},{4,5},{5,6},{6,7},{7,4},{8,9},{9,10},{10,1... | collective-permute-start | bytes 786440 | tf_op jit(solution)/shard_map/ppermute | solution.py:482
  758.1 17.4 %collective-permute-done.39 = bf16[32,4096]{1,0:T(8,128)(2,1)S(1)} collective-permute-done((bf16[32,4096]{1,0:T(8,128)(2,1)S(1)}, bf16[32,4096]{1,0:T(8,128)(2,1)S(1)}, u32[]{:S(2)}, u32[]{:S(2)}) %collective-permute-start.39) | collective-permute-done | bytes 262176 | tf_op jit(solution)/shard_map/ppermute | solution.py:482
  776.5 7.3 collective-permute-done.45
  (333 shorter events, 105.9 us)
Async XLA Ops:
  3.4 18.0 %copy-start.62 = (s32[2]{0:T(128)S(1)}, s32[2]{0:T(128)}, u32[]{:S(2)}) copy-start(s32[2]{0:T(128)} %param.20) | copy-start | bytes 28
  3.4 18.4 %copy-start.52 = (bf16[1024]{0:T(1024)(128)(2,1)S(1)}, bf16[1024]{0:T(1024)(128)(2,1)}, u32[]{:S(2)}) copy-start(bf16[1024]{0:T(1024)(128)(2,1)} %param.37) | copy-start | bytes 6148
  3.4 20.8 %copy-start.61 = (bf16[1024]{0:T(1024)(128)(2,1)S(1)}, bf16[1024]{0:T(1024)(128)(2,1)}, u32[]{:S(2)}) copy-start(bf16[1024]{0:T(1024)(128)(2,1)} %param.36) | copy-start | bytes 6148
  6.2 18.0 %collective-permute-start.7 = (bf16[432,1024]{1,0:T(8,128)(2,1)}, bf16[432,1024]{1,0:T(8,128)(2,1)S(1)}, u32[]{:S(2)}, u32[]{:S(2)}) collective-permute-start(bf16[432,1024]{1,0:T(8,128)(2,1)} %get-tuple-element.69), channel_id=1, source_target_pairs={{0,0},{1,1},{2,4},{3,5},{4,2},{5,3},{6,6},{7,7},{8,8},{9,9},{10,12... | collective-permute-start | bytes 2654216 | tf_op jit(solution)/shard_map/ppermute | solution.py:482
  8.0 23.5 %collective-permute-start.8 = (bf16[432,1024]{1,0:T(8,128)(2,1)}, bf16[432,1024]{1,0:T(8,128)(2,1)S(1)}, u32[]{:S(2)}, u32[]{:S(2)}) collective-permute-start(bf16[432,1024]{1,0:T(8,128)(2,1)} %get-tuple-element.70), channel_id=1, source_target_pairs={{0,1},{1,0},{2,5},{3,4},{4,3},{5,2},{6,7},{7,6},{8,9},{9,8},{10,13... | collective-permute-start | bytes 2654216 | tf_op jit(solution)/shard_map/ppermute | solution.py:482
  12.4 37.5 %collective-permute-start.1 = (bf16[432,1024]{1,0:T(8,128)(2,1)}, bf16[432,1024]{1,0:T(8,128)(2,1)S(1)}, u32[]{:S(2)}, u32[]{:S(2)}) collective-permute-start(bf16[432,1024]{1,0:T(8,128)(2,1)} %get-tuple-element.80), channel_id=1, source_target_pairs={{0,1},{1,0},{2,5},{3,4},{4,3},{5,2},{6,7},{7,6},{8,9},{9,8},{10,13... | collective-permute-start | bytes 2654216 | tf_op jit(solution)/shard_map/ppermute | solution.py:482
  12.4 38.4 %collective-permute-start = (bf16[432,1024]{1,0:T(8,128)(2,1)}, bf16[432,1024]{1,0:T(8,128)(2,1)}, u32[]{:S(2)}, u32[]{:S(2)}) collective-permute-start(bf16[432,1024]{1,0:T(8,128)(2,1)} %get-tuple-element.79), channel_id=1, source_target_pairs={{0,0},{1,1},{2,4},{3,5},{4,2},{5,3},{6,6},{7,7},{8,8},{9,9},{10,12... | collective-permute-start | bytes 2654216 | tf_op jit(solution)/shard_map/ppermute | solution.py:482
  21.7 1.2 collective-permute-start.2
  53.7 63.2 %copy-start.6 = (bf16[432,1024]{1,0:T(8,128)(2,1)}, bf16[432,1024]{1,0:T(8,128)(2,1)S(1)}, u32[]{:S(2)}) copy-start(bf16[432,1024]{1,0:T(8,128)(2,1)S(1)} %get-tuple-element.131) | copy-start | bytes 2654212
  53.7 64.8 %copy-start.8 = (bf16[432,1024]{1,0:T(8,128)(2,1)}, bf16[432,1024]{1,0:T(8,128)(2,1)S(1)}, u32[]{:S(2)}) copy-start(bf16[432,1024]{1,0:T(8,128)(2,1)S(1)} %get-tuple-element.132) | copy-start | bytes 2654212
  53.7 40.6 %copy-start.53 = (bf16[1024]{0:T(1024)(128)(2,1)S(1)}, bf16[1024]{0:T(1024)(128)(2,1)}, u32[]{:S(2)}) copy-start(bf16[1024]{0:T(1024)(128)(2,1)} %param.33) | copy-start | bytes 6148
  53.7 41.2 %copy-start.48 = (bf16[4096]{0:T(1024)(128)(2,1)S(1)}, bf16[4096]{0:T(1024)(128)(2,1)}, u32[]{:S(2)}) copy-start(bf16[4096]{0:T(1024)(128)(2,1)} %param.31) | copy-start | bytes 24580
  53.7 41.8 %copy-start.54 = (bf16[1024]{0:T(1024)(128)(2,1)S(1)}, bf16[1024]{0:T(1024)(128)(2,1)}, u32[]{:S(2)}) copy-start(bf16[1024]{0:T(1024)(128)(2,1)} %param.27) | copy-start | bytes 6148
  55.5 67.4 %collective-permute-start.3 = (bf16[864,1024]{1,0:T(8,128)(2,1)}, bf16[864,1024]{1,0:T(8,128)(2,1)}, u32[]{:S(2)}, u32[]{:S(2)}) collective-permute-start(bf16[864,1024]{1,0:T(8,128)(2,1)} %fusion.20), channel_id=1, source_target_pairs={{0,4},{1,5},{2,6},{3,7},{4,0},{5,1},{6,2},{7,3},{8,12},{9,13},{10,... | collective-permute-start | bytes 5308424 | tf_op jit(solution)/shard_map/ppermute | solution.py:482
  96.2 10.5 %copy-start.59 = (bf16[1024]{0:T(1024)(128)(2,1)S(1)}, bf16[1024]{0:T(1024)(128)(2,1)}, u32[]{:S(2)}) copy-start(bf16[1024]{0:T(1024)(128)(2,1)} %param.24) | copy-start | bytes 6148
  96.2 10.5 %copy-start.60 = (bf16[1024]{0:T(1024)(128)(2,1)S(1)}, bf16[1024]{0:T(1024)(128)(2,1)}, u32[]{:S(2)}) copy-start(bf16[1024]{0:T(1024)(128)(2,1)} %param.25) | copy-start | bytes 6148
  177.2 20.4 %collective-permute-start.4 = (bf16[864,512]{1,0:T(8,128)(2,1)S(1)}, bf16[864,512]{1,0:T(8,128)(2,1)}, u32[]{:S(2)}, u32[]{:S(2)}) collective-permute-start(bf16[864,512]{1,0:T(8,128)(2,1)S(1)} %get-tuple-element.76), channel_id=1, source_target_pairs={{0,4},{1,5},{2,6},{3,7},{4,0},{5,1},{6,2},{7,3},{8,12},{9,13},{10,... | collective-permute-start | bytes 2654216 | tf_op jit(solution)/shard_map/ppermute | solution.py:482
  290.2 140.9 %collective-permute-start.5 = (bf16[432,1024]{1,0:T(8,128)(2,1)}, bf16[432,1024]{1,0:T(8,128)(2,1)}, u32[]{:S(2)}, u32[]{:S(2)}) collective-permute-start(bf16[432,1024]{1,0:T(8,128)(2,1)} %get-tuple-element.73), channel_id=1, source_target_pairs={{0,0},{1,1},{2,4},{3,5},{4,2},{5,3},{6,6},{7,7},{8,8},{9,9},{10,12... | collective-permute-start | bytes 2654216 | tf_op jit(solution)/shard_map/ppermute | solution.py:482
  298.6 132.5 %collective-permute-start.6 = (bf16[432,1024]{1,0:T(8,128)(2,1)}, bf16[432,1024]{1,0:T(8,128)(2,1)}, u32[]{:S(2)}, u32[]{:S(2)}) collective-permute-start(bf16[432,1024]{1,0:T(8,128)(2,1)} %get-tuple-element.74), channel_id=1, source_target_pairs={{0,1},{1,0},{2,5},{3,4},{4,3},{5,2},{6,7},{7,6},{8,9},{9,8},{10,13... | collective-permute-start | bytes 2654216 | tf_op jit(solution)/shard_map/ppermute | solution.py:482
  345.8 88.3 %collective-permute-start.9 = (bf16[864,1024]{1,0:T(8,128)(2,1)}, bf16[864,1024]{1,0:T(8,128)(2,1)}, u32[]{:S(2)}, u32[]{:S(2)}) collective-permute-start(bf16[864,1024]{1,0:T(8,128)(2,1)} %convert_element_type.329), channel_id=1, source_target_pairs={{0,4},{1,5},{2,6},{3,7},{4,0},{5,1},{6,2},{7,3},{8,12},{9,13},{10,... | collective-permute-start | bytes 5308424 | tf_op jit(solution)/shard_map/ppermute | solution.py:482
  365.7 229.7 %collective-permute-start.35 = (bf16[512,4096]{1,0:T(8,128)(2,1)}, bf16[512,4096]{1,0:T(8,128)(2,1)}, u32[]{:S(2)}, u32[]{:S(2)}) collective-permute-start(bf16[512,4096]{1,0:T(8,128)(2,1)} %convolution_convert_fusion), channel_id=1, source_target_pairs={{0,4},{1,5},{2,6},{3,7},{4,0},{5,1},{6,2},{7,3},{8,12},{9,13},{10,... | collective-permute-start | bytes 12582920 | tf_op jit(solution)/shard_map/ppermute | solution.py:482
  405.0 17.9 %copy-start.15 = (f32[864,1024]{1,0:T(8,128)S(1)}, f32[864,1024]{1,0:T(8,128)}, u32[]{:S(2)}) copy-start(f32[864,1024]{1,0:T(8,128)} %get-tuple-element.38) | copy-start | bytes 10616836
  512.1 92.5 %collective-permute-start.10 = (bf16[864,1536]{1,0:T(8,128)(2,1)}, bf16[864,1536]{1,0:T(8,128)(2,1)}, u32[]{:S(2)}, u32[]{:S(2)}) collective-permute-start(bf16[864,1536]{1,0:T(8,128)(2,1)} %dynamic-slice_bitcast_fusion), channel_id=1, source_target_pairs={{0,4},{1,5},{2,6},{3,7},{4,0},{5,1},{6,2},{7,3},{8,12},{9,13},{10,... | collective-permute-start | bytes 7962632 | tf_op jit(solution)/shard_map/ppermute | solution.py:482
  515.7 53.7 %collective-permute-start.18 = (bf16[512,1536]{1,0:T(8,128)(2,1)S(1)}, bf16[512,1536]{1,0:T(8,128)(2,1)S(1)}, u32[]{:S(2)}, u32[]{:S(2)}) collective-permute-start(bf16[512,1536]{1,0:T(8,128)(2,1)S(1)} %convolution_convert_fusion.3), channel_id=1, source_target_pairs={{0,4},{1,5},{2,6},{3,7},{4,0},{5,1},{6,2},{7,3},{8,12},{9,13},{10,... | collective-permute-start | bytes 4718600 | tf_op jit(solution)/shard_map/ppermute | solution.py:482
  518.9 33.1 %collective-permute-start.13 = (bf16[2,4,32,1536]{3,2,1,0:T(8,128)(2,1)S(1)}, bf16[2,4,32,1536]{3,2,1,0:T(8,128)(2,1)S(1)}, u32[]{:S(2)}, u32[]{:S(2)}) collective-permute-start(bf16[2,4,32,1536]{3,2,1,0:T(8,128)(2,1)S(1)} %dynamic-slice_bitcast_fusion.16), channel_id=1, source_target_pairs={{0,8},{1,9},{2,10},{3,11},{4,12},{5,13},{6,14},{7,15},{8,0},{9,1},... | collective-permute-start | bytes 2359304 | tf_op jit(solution)/shard_map/ppermute | solution.py:482
  526.1 24.1 %collective-permute-start.30 = (bf16[2,4,32,1024]{3,2,1,0:T(8,128)(2,1)S(1)}, bf16[2,4,32,1024]{3,2,1,0:T(8,128)(2,1)S(1)}, u32[]{:S(2)}, u32[]{:S(2)}) collective-permute-start(bf16[2,4,32,1024]{3,2,1,0:T(8,128)(2,1)S(1)} %dynamic-slice_bitcast_fusion.17), channel_id=1, source_target_pairs={{0,8},{1,9},{2,10},{3,11},{4,12},{5,13},{6,14},{7,15},{8,0},{9,1},... | collective-permute-start | bytes 1572872 | tf_op jit(solution)/shard_map/ppermute | solution.py:482
  531.5 21.3 %copy-start.42 = (f32[1024]{0:T(1024)S(1)}, f32[1024]{0:T(1024)}, u32[]{:S(2)}) copy-start(f32[1024]{0:T(1024)} %get-tuple-element.31) | copy-start | bytes 12292
  550.4 25.4 %copy-start.41 = (f32[1024]{0:T(1024)S(1)}, f32[1024]{0:T(1024)}, u32[]{:S(2)}) copy-start(f32[1024]{0:T(1024)} %get-tuple-element.36) | copy-start | bytes 12292
  550.4 9.3 %collective-permute-start.31 = (bf16[4,32,1024]{2,1,0:T(8,128)(2,1)S(1)}, bf16[4,32,1024]{2,1,0:T(8,128)(2,1)S(1)}, u32[]{:S(2)}, u32[]{:S(2)}) collective-permute-start(bf16[4,32,1024]{2,1,0:T(8,128)(2,1)S(1)} %dynamic-slice_bitcast_fusion.26), channel_id=1, source_target_pairs={{0,16},{1,17},{2,18},{3,19},{4,20},{5,21},{6,22},{7,23},{8,24},{9,... | collective-permute-start | bytes 786440 | tf_op jit(solution)/shard_map/ppermute | solution.py:482
  552.3 14.5 %collective-permute-start.14 = (bf16[4,32,1536]{2,1,0:T(8,128)(2,1)S(1)}, bf16[4,32,1536]{2,1,0:T(8,128)(2,1)S(1)}, u32[]{:S(2)}, u32[]{:S(2)}) collective-permute-start(bf16[4,32,1536]{2,1,0:T(8,128)(2,1)S(1)} %dynamic-slice_bitcast_fusion.19), channel_id=1, source_target_pairs={{0,16},{1,17},{2,18},{3,19},{4,20},{5,21},{6,22},{7,23},{8,24},{9,... | collective-permute-start | bytes 1179656 | tf_op jit(solution)/shard_map/ppermute | solution.py:482
  559.8 11.7 %collective-permute-start.34 = (bf16[32,1024]{1,0:T(8,128)(2,1)S(1)}, bf16[32,1024]{1,0:T(8,128)(2,1)S(1)}, u32[]{:S(2)}, u32[]{:S(2)}) collective-permute-start(bf16[32,1024]{1,0:T(8,128)(2,1)S(1)} %get-tuple-element.94), channel_id=1, source_target_pairs={{0,3},{1,0},{2,1},{3,2},{4,7},{5,4},{6,5},{7,6},{8,11},{9,8},{10,9... | collective-permute-start | bytes 196616 | tf_op jit(solution)/shard_map/ppermute | solution.py:482
  566.8 7.5 collective-permute-start.33
  569.5 6.3 collective-permute-start.32
  571.5 5.5 collective-permute-start.17
  574.3 17.2 %collective-permute-start.19 = (bf16[2,4,32,1536]{3,2,1,0:T(8,128)(2,1)}, bf16[2,4,32,1536]{3,2,1,0:T(8,128)(2,1)}, u32[]{:S(2)}, u32[]{:S(2)}) collective-permute-start(bf16[2,4,32,1536]{3,2,1,0:T(8,128)(2,1)} %dynamic-slice_bitcast_fusion.15), channel_id=1, source_target_pairs={{0,16},{1,17},{2,18},{3,19},{4,20},{5,21},{6,22},{7,23},{8,24},{9,... | collective-permute-start | bytes 2359304 | tf_op jit(solution)/shard_map/ppermute | solution.py:482
  575.8 5.9 collective-permute-start.16
  577.0 7.3 collective-permute-start.15
  581.7 37.1 %collective-permute-start.41 = (bf16[2048,1024]{1,0:T(8,128)(2,1)}, bf16[2048,1024]{1,0:T(8,128)(2,1)}, u32[]{:S(2)}, u32[]{:S(2)}) collective-permute-start(bf16[2048,1024]{1,0:T(8,128)(2,1)} %convolution_convert_fusion.1), channel_id=1, source_target_pairs={{0,4},{1,5},{2,6},{3,7},{4,0},{5,1},{6,2},{7,3},{8,12},{9,13},{10,... | collective-permute-start | bytes 12582920 | tf_op jit(solution)/shard_map/ppermute | solution.py:482
  593.9 75.2 %collective-permute-start.20 = (bf16[4,32,1536]{2,1,0:T(8,128)(2,1)}, bf16[4,32,1536]{2,1,0:T(8,128)(2,1)}, u32[]{:S(2)}, u32[]{:S(2)}) collective-permute-start(bf16[4,32,1536]{2,1,0:T(8,128)(2,1)} %dynamic-slice_bitcast_fusion.18), channel_id=1, source_target_pairs={{0,8},{1,9},{2,10},{3,11},{4,12},{5,13},{6,14},{7,15},{8,0},{9,1},... | collective-permute-start | bytes 1179656 | tf_op jit(solution)/shard_map/ppermute | solution.py:482
  612.1 3.2 collective-permute-start.24
  613.7 75.6 %collective-permute-start.36 = (bf16[2,4,32,4096]{3,2,1,0:T(8,128)(2,1)}, bf16[2,4,32,4096]{3,2,1,0:T(8,128)(2,1)}, u32[]{:S(2)}, u32[]{:S(2)}) collective-permute-start(bf16[2,4,32,4096]{3,2,1,0:T(8,128)(2,1)} %dynamic-slice_bitcast_fusion.2), channel_id=1, source_target_pairs={{0,16},{1,17},{2,18},{3,19},{4,20},{5,21},{6,22},{7,23},{8,24},{9,... | collective-permute-start | bytes 6291464 | tf_op jit(solution)/shard_map/ppermute | solution.py:482
  618.2 8.1 %collective-permute-start.25 = (f32[2,4,32,14]{2,1,3,0:T(4,128)S(1)}, f32[2,4,32,14]{2,1,3,0:T(4,128)S(1)}, u32[]{:S(2)}, u32[]{:S(2)}) collective-permute-start(f32[2,4,32,14]{2,1,3,0:T(4,128)S(1)} %bitcast.319), channel_id=1, source_target_pairs={{0,8},{1,9},{2,10},{3,11},{4,12},{5,13},{6,14},{7,15},{8,0},{9,1},... | collective-permute-start | bytes 43016 | tf_op jit(solution)/shard_map/ppermute | solution.py:482
  626.3 39.8 %copy-start.13 = (bf16[2048,1024]{1,0:T(8,128)(2,1)}, bf16[2048,1024]{1,0:T(8,128)(2,1)S(1)}, u32[]{:S(2)}) copy-start(bf16[2048,1024]{1,0:T(8,128)(2,1)S(1)} %add_convert_fusion) | copy-start | bytes 12582916
  626.3 38.4 %copy-start.22 = (bf16[864,1024]{1,0:T(8,128)(2,1)S(1)}, bf16[864,1024]{1,0:T(8,128)(2,1)}, u32[]{:S(2)}) copy-start(bf16[864,1024]{1,0:T(8,128)(2,1)} %get-tuple-element.52) | copy-start | bytes 5308420
  626.4 36.2 %collective-permute-start.26 = (f32[4,32,14]{1,0,2:T(4,128)S(1)}, f32[4,32,14]{1,0,2:T(4,128)S(1)}, u32[]{:S(2)}, u32[]{:S(2)}) collective-permute-start(f32[4,32,14]{1,0,2:T(4,128)S(1)} %dynamic-slice_bitcast_fusion.36), channel_id=1, source_target_pairs={{0,16},{1,17},{2,18},{3,19},{4,20},{5,21},{6,22},{7,23},{8,24},{9,... | collective-permute-start | bytes 21512 | tf_op jit(solution)/shard_map/ppermute | solution.py:482
  626.9 42.2 %copy-start.17 = (bf16[2,4,32,1536]{3,2,1,0:T(8,128)(2,1)S(1)}, bf16[2,4,32,1536]{3,2,1,0:T(8,128)(2,1)}, u32[]{:S(2)}) copy-start(bf16[2,4,32,1536]{3,2,1,0:T(8,128)(2,1)} %copy-done.16) | copy-start | bytes 2359300
  662.6 3.7 collective-permute-start.29
  663.0 4.5 collective-permute-start.28
  663.7 5.4 collective-permute-start.27
  666.3 52.7 %collective-permute-start.42 = (bf16[2,4,128,1024]{3,2,1,0:T(8,128)(2,1)}, bf16[2,4,128,1024]{3,2,1,0:T(8,128)(2,1)}, u32[]{:S(2)}, u32[]{:S(2)}) collective-permute-start(bf16[2,4,128,1024]{3,2,1,0:T(8,128)(2,1)} %dynamic-slice_bitcast_fusion.1), channel_id=1, source_target_pairs={{0,8},{1,9},{2,10},{3,11},{4,12},{5,13},{6,14},{7,15},{8,0},{9,1},... | collective-permute-start | bytes 6291464 | tf_op jit(solution)/shard_map/ppermute | solution.py:482
  670.3 6.2 collective-permute-start.23
  671.9 13.0 %collective-permute-start.22 = (bf16[32,1536]{1,0:T(8,128)(2,1)S(1)}, bf16[32,1536]{1,0:T(8,128)(2,1)S(1)}, u32[]{:S(2)}, u32[]{:S(2)}) collective-permute-start(bf16[32,1536]{1,0:T(8,128)(2,1)S(1)} %get-tuple-element.92), channel_id=1, source_target_pairs={{0,2},{1,3},{2,0},{3,1},{4,6},{5,7},{6,4},{7,5},{8,10},{9,11},{10,... | collective-permute-start | bytes 294920 | tf_op jit(solution)/shard_map/ppermute | solution.py:482
  671.9 16.5 %collective-permute-start.21 = (bf16[32,1536]{1,0:T(8,128)(2,1)S(1)}, bf16[32,1536]{1,0:T(8,128)(2,1)S(1)}, u32[]{:S(2)}, u32[]{:S(2)}) collective-permute-start(bf16[32,1536]{1,0:T(8,128)(2,1)S(1)} %get-tuple-element.90), channel_id=1, source_target_pairs={{0,1},{1,2},{2,3},{3,0},{4,5},{5,6},{6,7},{7,4},{8,9},{9,10},{10,1... | collective-permute-start | bytes 294920 | tf_op jit(solution)/shard_map/ppermute | solution.py:482
  676.5 18.5 %collective-permute-start.11 = (bf16[432,1024]{1,0:T(8,128)(2,1)}, bf16[432,1024]{1,0:T(8,128)(2,1)}, u32[]{:S(2)}, u32[]{:S(2)}) collective-permute-start(bf16[432,1024]{1,0:T(8,128)(2,1)} %get-tuple-element.65), channel_id=1, source_target_pairs={{0,0},{1,1},{2,4},{3,5},{4,2},{5,3},{6,6},{7,7},{8,8},{9,9},{10,12... | collective-permute-start | bytes 2654216 | tf_op jit(solution)/shard_map/ppermute | solution.py:482
  684.9 31.2 %collective-permute-start.12 = (bf16[432,1024]{1,0:T(8,128)(2,1)}, bf16[432,1024]{1,0:T(8,128)(2,1)}, u32[]{:S(2)}, u32[]{:S(2)}) collective-permute-start(bf16[432,1024]{1,0:T(8,128)(2,1)} %get-tuple-element.66), channel_id=1, source_target_pairs={{0,1},{1,0},{2,5},{3,4},{4,3},{5,2},{6,7},{7,6},{8,9},{9,8},{10,13... | collective-permute-start | bytes 2654216 | tf_op jit(solution)/shard_map/ppermute | solution.py:482
  692.4 43.2 %collective-permute-start.37 = (bf16[4,32,4096]{2,1,0:T(8,128)(2,1)S(1)}, bf16[4,32,4096]{2,1,0:T(8,128)(2,1)}, u32[]{:S(2)}, u32[]{:S(2)}) collective-permute-start(bf16[4,32,4096]{2,1,0:T(8,128)(2,1)S(1)} %dynamic-slice_bitcast_fusion.4), channel_id=1, source_target_pairs={{0,8},{1,9},{2,10},{3,11},{4,12},{5,13},{6,14},{7,15},{8,0},{9,1},... | collective-permute-start | bytes 3145736 | tf_op jit(solution)/shard_map/ppermute | solution.py:482
  695.0 24.0 %copy-start.14 = (bf16[2048,1024]{1,0:T(8,128)(2,1)S(1)}, bf16[2048,1024]{1,0:T(8,128)(2,1)}, u32[]{:S(2)}) copy-start(bf16[2048,1024]{1,0:T(8,128)(2,1)} %copy-done.13) | copy-start | bytes 12582916
  721.7 20.2 %collective-permute-start.43 = (bf16[4,128,1024]{2,1,0:T(8,128)(2,1)S(1)}, bf16[4,128,1024]{2,1,0:T(8,128)(2,1)S(1)}, u32[]{:S(2)}, u32[]{:S(2)}) collective-permute-start(bf16[4,128,1024]{2,1,0:T(8,128)(2,1)S(1)} %dynamic-slice_bitcast_fusion.3), channel_id=1, source_target_pairs={{0,16},{1,17},{2,18},{3,19},{4,20},{5,21},{6,22},{7,23},{8,24},{9,... | collective-permute-start | bytes 3145736 | tf_op jit(solution)/shard_map/ppermute | solution.py:482
  737.2 9.4 %collective-permute-start.40 = (bf16[32,4096]{1,0:T(8,128)(2,1)S(1)}, bf16[32,4096]{1,0:T(8,128)(2,1)S(1)}, u32[]{:S(2)}, u32[]{:S(2)}) collective-permute-start(bf16[32,4096]{1,0:T(8,128)(2,1)S(1)} %get-tuple-element.85), channel_id=1, source_target_pairs={{0,3},{1,0},{2,1},{3,2},{4,7},{5,4},{6,5},{7,6},{8,11},{9,8},{10,9... | collective-permute-start | bytes 786440 | tf_op jit(solution)/shard_map/ppermute | solution.py:482
  739.8 35.8 %collective-permute-start.39 = (bf16[32,4096]{1,0:T(8,128)(2,1)S(1)}, bf16[32,4096]{1,0:T(8,128)(2,1)S(1)}, u32[]{:S(2)}, u32[]{:S(2)}) collective-permute-start(bf16[32,4096]{1,0:T(8,128)(2,1)S(1)} %get-tuple-element.86), channel_id=1, source_target_pairs={{0,2},{1,3},{2,0},{3,1},{4,6},{5,7},{6,4},{7,5},{8,10},{9,11},{10,... | collective-permute-start | bytes 786440 | tf_op jit(solution)/shard_map/ppermute | solution.py:482
  740.2 35.3 %collective-permute-start.38 = (bf16[32,4096]{1,0:T(8,128)(2,1)S(1)}, bf16[32,4096]{1,0:T(8,128)(2,1)S(1)}, u32[]{:S(2)}, u32[]{:S(2)}) collective-permute-start(bf16[32,4096]{1,0:T(8,128)(2,1)S(1)} %get-tuple-element.84), channel_id=1, source_target_pairs={{0,1},{1,2},{2,3},{3,0},{4,5},{5,6},{6,7},{7,4},{8,9},{9,10},{10,1... | collective-permute-start | bytes 786440 | tf_op jit(solution)/shard_map/ppermute | solution.py:482
  742.4 34.1 %collective-permute-start.46 = (bf16[128,1024]{1,0:T(8,128)(2,1)S(1)}, bf16[128,1024]{1,0:T(8,128)(2,1)S(1)}, u32[]{:S(2)}, u32[]{:S(2)}) collective-permute-start(bf16[128,1024]{1,0:T(8,128)(2,1)S(1)} %get-tuple-element.82), channel_id=1, source_target_pairs={{0,3},{1,0},{2,1},{3,2},{4,7},{5,4},{6,5},{7,6},{8,11},{9,8},{10,9... | collective-permute-start | bytes 786440 | tf_op jit(solution)/shard_map/ppermute | solution.py:482
  744.6 39.2 %collective-permute-start.45 = (bf16[128,1024]{1,0:T(8,128)(2,1)S(1)}, bf16[128,1024]{1,0:T(8,128)(2,1)S(1)}, u32[]{:S(2)}, u32[]{:S(2)}) collective-permute-start(bf16[128,1024]{1,0:T(8,128)(2,1)S(1)} %get-tuple-element.83), channel_id=1, source_target_pairs={{0,2},{1,3},{2,0},{3,1},{4,6},{5,7},{6,4},{7,5},{8,10},{9,11},{10,... | collective-permute-start | bytes 786440 | tf_op jit(solution)/shard_map/ppermute | solution.py:482
  746.5 37.3 %collective-permute-start.44 = (bf16[128,1024]{1,0:T(8,128)(2,1)S(1)}, bf16[128,1024]{1,0:T(8,128)(2,1)S(1)}, u32[]{:S(2)}, u32[]{:S(2)}) collective-permute-start(bf16[128,1024]{1,0:T(8,128)(2,1)S(1)} %get-tuple-element.81), channel_id=1, source_target_pairs={{0,1},{1,2},{2,3},{3,0},{4,5},{5,6},{6,7},{7,4},{8,9},{9,10},{10,1... | collective-permute-start | bytes 786440 | tf_op jit(solution)/shard_map/ppermute | solution.py:482
  (49 other events, 237.5 us)

commit v2 on v1

--- a/solution.py
+++ b/solution.py
@@ -33,102 +33,141 @@
     f=base.astype(F32)
     f=jnp.where((lane>=o)&(lane<o+64),jnp.where(lane<o+n,1.0,0.0),f)
     return f.astype(BF)
-def fwd_item(q_ref,k_ref,v_ref,o_ref,ol_ref,qa_ref,off,n,bq):
-    k=k_ref[pl.ds(off,n),:]
-    v=v_ref[pl.ds(off,n),:]
-    lk=lanes(n)
-    vs=[ones3(v,h,lk,1) for h in (0,1)]
-    lq=lanes(bq)
-    for r in range(n//bq):
-        rows=pl.ds(off+r*bq,bq)
-        q=q_ref[rows,:]
-        outs=[]
-        for h in (0,1):
-            qh=jnp.where((lq//64)==h,q.astype(F32),0.0).astype(BF)
-            s=dot(qh,k,NT)
-            m=jnp.max(s,axis=1,keepdims=True)
-            p=jnp.exp2(s-m).astype(BF)
-            o=dot(p,vs[h],NN)
-            l=o[:,(1-h)*64:(1-h)*64+1]
-            outs.append(o/l)
-            qa_ref[h,rows,:]=augment(q,h,-(m+jnp.log2(l)),lq)
-        o=jnp.where(lq<64,outs[0],outs[1])
-        o_ref[rows,:]=o.astype(BF)
-        ol_ref[rows,:]=(o-o.astype(BF).astype(F32)).astype(BF)
-def walk(seg_ref,item,bs):
-    single=seg_ref[0]==seg_ref[12]
+def fwd_tile(q,k,vs,lane,keep):
+    outs=[];augs=[]
+    for h in (0,1):
+        qh=jnp.where((lane//64)==h,q.astype(F32),0.0).astype(BF)
+        s=dot(qh,k,NT)
+        if keep is not None: s=jnp.where(keep,s,-1e30)
+        m=jnp.max(s,axis=1,keepdims=True)
+        p=jnp.exp2(s-m).astype(BF)
+        o=dot(p,vs[h],NN)
+        l=o[:,(1-h)*64:(1-h)*64+1]
+        outs.append(o/l)
+        augs.append(augment(q,h,-(m+jnp.log2(l)),lane))
+    return jnp.where(lane<64,outs[0],outs[1]),augs
+def fwd_store(refs,rows,o,augs):
+    o_ref,ol_ref,qa_ref=refs
+    o_ref[rows,:]=o.astype(BF)
+    ol_ref[rows,:]=(o-o.astype(BF).astype(F32)).astype(BF)
+    for h in (0,1): qa_ref[h,rows,:]=augs[h]
+def fwd_kernel(bq,info,q_ref,k_ref,v_ref,*refs):
+    single=info[0]==1
     @pl.when(single)
     def _():
-        item(0,FILLED,bs[0])
+        k=k_ref[0:FILLED,:]; v=v_ref[0:FILLED,:]
+        vs=[ones3(v,h,lanes(FILLED),1) for h in (0,1)]
+        for r in range(0,FILLED,bq):
+            n=min(bq,FILLED-r)
+            o,augs=fwd_tile(q_ref[r:r+n,:],k,vs,lanes(n),None)
+            fwd_store(refs,slice(r,r+n),o,augs)
     @pl.when(jnp.logical_not(single))
     def _():
-        def step(i,c):
-            me=seg_ref[i]
-            first=(i==0)|(seg_ref[jnp.maximum(i-1,0)]!=me)
-            last3=jnp.minimum(i+3,12)
-            long=first&(i+3<=12)&(seg_ref[last3]==me)
-            off=pl.multiple_of(i*128,128)
-            @pl.when(long)
-            def _(): item(off,512,bs[1])
-            @pl.when(first&jnp.logical_not(long))
-            def _(): item(off,128,bs[2])
-            return c
-        lax.fori_loop(0,13,step,0)
-    item(FILLED,PAD,PAD)
-def fwd_kernel(bs,seg_ref,q_ref,k_ref,v_ref,o_ref,ol_ref,qa_ref):
-    walk(seg_ref,functools.partial(fwd_item,q_ref,k_ref,v_ref,o_ref,ol_ref,qa_ref),bs)
-def attn_fwd(seg13,qkv,bs=(832,256,128)):
-    L,W3=qkv.shape; W=W3//3; n=W//128
-    spec=lambda j: pl.BlockSpec((L,128),lambda p,s,j=j:(0,p+j*n))
-    return pl.pallas_call(functools.partial(fwd_kernel,bs),
-        out_shape=(jax.ShapeDtypeStruct((L,W),BF),)*2+(jax.ShapeDtypeStruct((2*n,L,128),BF),),
-        grid_spec=pltpu.PrefetchScalarGridSpec(num_scalar_prefetch=1,grid=(n,),
+        col=lax.broadcasted_iota(jnp.int32,(128,512),1)
+        lw=lanes(512); lq=lanes(128)
+        for i in range(13):
+            lo=info[1+i]; hi=info[14+i]
+            at=jnp.minimum(lo,9)
+            window=pl.ds(pl.multiple_of(at*128,128),512)
+            k=k_ref[window,:]; v=v_ref[window,:]
+            vs=[ones3(v,h,lw,1) for h in (0,1)]
+            keep=(col>=(lo-at)*128)&(col<(hi-at)*128)
+            rows=slice(i*128,i*128+128)
+            o,augs=fwd_tile(q_ref[rows,:],k,vs,lq,keep)
+            fwd_store(refs,rows,o,augs)
+    rows=slice(FILLED,FILLED+PAD)
+    lp=lanes(PAD)
+    v=v_ref[rows,:]
+    o,augs=fwd_tile(q_ref[rows,:],k_ref[rows,:],[ones3(v,h,lp,1) for h in (0,1)],lp,None)
+    fwd_store(refs,rows,o,augs)
+def attn_fwd(info,qkv,first,count,bq=832):
+    L,W3=qkv.shape; n=W3//384
+    spec=lambda j: pl.BlockSpec((L,128),lambda p,s,j=j:(0,p+first+j*n))
+    one=pl.BlockSpec((L,128),lambda p,s:(0,p))
+    return pl.pallas_call(functools.partial(fwd_kernel,bq),
+        out_shape=(jax.ShapeDtypeStruct((L,count*128),BF),)*2+(jax.ShapeDtypeStruct((2*count,L,128),BF),),
+        grid_spec=pltpu.PrefetchScalarGridSpec(num_scalar_prefetch=1,grid=(count,),
             in_specs=[spec(0),spec(1),spec(2)],
-            out_specs=(pl.BlockSpec((L,128),lambda p,s:(0,p)),pl.BlockSpec((L,128),lambda p,s:(0,p)),pl.BlockSpec((2,L,128),lambda p,s:(p,0,0)))),
+            out_specs=(one,one,pl.BlockSpec((2,L,128),lambda p,s:(p,0,0)))),
         compiler_params=pltpu.CompilerParams(vmem_limit_bytes=50<<20),name="attn_forward",
-        cost_estimate=pl.CostEstimate(flops=2*2*2*n*L*L*256,bytes_accessed=10*L*W,transcendentals=2*n*L*L))(seg13,qkv,qkv,qkv)
-def bwd_item(mode,qa_ref,k_ref,v_ref,o_ref,ol_ref,g_ref,dq_ref,dk_ref,dv_ref,acc,off,n,bk):
-    item=pl.ds(off,n)
-    ln=lanes(n)
-    g=g_ref[item,:]
-    prod=g.astype(F32)*(o_ref[item,:].astype(F32)+ol_ref[item,:].astype(F32))
-    lb=lanes(bk)
-    nb=n//bk
-    gas=[augment(g,h,-jnp.sum(jnp.where((ln//64)==h,prod,0.0),axis=1,keepdims=True),ln) for h in (0,1)]
-    for b in range(nb):
-        rows=pl.ds(off+b*bk,bk)
-        k=k_ref[rows,:]; v=v_ref[rows,:]
-        dks=[];dvs=[]
-        for h in (0,1):
-            ga=gas[h]
-            qa=qa_ref[h,item,:]
-            kh=ones3(k,h,lb); vh=ones3(v,h,lb)
-            p=jnp.exp2(dot(kh,qa,NT))
-            d=dot(vh,ga,NT)
-            ds=(p*d).astype(BF)
-            dvs.append(dot(p.astype(BF),ga,NN))
-            dks.append(dot(ds,qa,NN))
-            if mode=='TN':
-                dq=dot(ds,kh,TN)
-                if b==0: acc[h,item,:]=dq
-                else: acc[h,item,:]+=dq
-        dk_ref[rows,:]=(jnp.where(lb<64,dks[0],dks[1])*0.6931471805599453).astype(BF)
-        dv_ref[rows,:]=jnp.where(lb<64,dvs[0],dvs[1]).astype(BF)
-    dq_ref[item,:]=(jnp.where(ln<64,acc[0,item,:],acc[1,item,:])*0.125).astype(BF)
-def bwd_kernel(bs,mode,seg_ref,qa_ref,k_ref,v_ref,o_ref,ol_ref,g_ref,dq_ref,dk_ref,dv_ref,acc):
-    walk(seg_ref,functools.partial(bwd_item,mode,qa_ref,k_ref,v_ref,o_ref,ol_ref,g_ref,dq_ref,dk_ref,dv_ref,acc),bs)
-def attn_bwd(seg13,qa,qkv,o,ol,g,bs=(832,256,128),mode='TN'):
-    L,W3=qkv.shape; W=W3//3; n=W//128
-    spec=lambda j: pl.BlockSpec((L,128),lambda p,s,j=j:(0,p+j*n))
+        cost_estimate=pl.CostEstimate(flops=8*count*L*L*256,bytes_accessed=10*L*count*128,transcendentals=2*count*L*L))(info,qkv,qkv,qkv)
+def deltas(g,o,ol,lane):
+    prod=g.astype(F32)*(o.astype(F32)+ol.astype(F32))
+    return [augment(g,h,-jnp.sum(jnp.where((lane//64)==h,prod,0.0),axis=1,keepdims=True),lane) for h in (0,1)]
+def bwd_tile(qa,k,v,ga,h,lane,keep):
+    kh=ones3(k,h,lane); vh=ones3(v,h,lane)
+    p=jnp.exp2(dot(kh,qa,NT))
+    d=dot(vh,ga,NT)
+    if keep is not None: p=jnp.where(keep,p,0.0)
+    ds=(p*d).astype(BF)
+    return dot(ds,kh,TN),dot(ds,qa,NN),dot(p.astype(BF),ga,NN)
+LN2=0.6931471805599453
+def both(a,lane): return jnp.where(lane<64,a[0],a[1])
+def bwd_kernel(bk,info,qa_ref,k_ref,v_ref,o_ref,ol_ref,g_ref,dq_ref,dk_ref,dv_ref,sum_ref,acc,acc_k,acc_v):
+    single=info[0]==1
+    @pl.when(single)
+    def _():
+        lf=lanes(FILLED)
+        gas=deltas(g_ref[0:FILLED,:],o_ref[0:FILLED,:],ol_ref[0:FILLED,:],lf)
+        for r in range(0,FILLED,bk):
+            n=min(bk,FILLED-r)
+            rows=slice(r,r+n); lb=lanes(n)
+            k=k_ref[rows,:]; v=v_ref[rows,:]
+            dks=[];dvs=[]
+            for h in (0,1):
+                dq,dk,dv=bwd_tile(qa_ref[h,0:FILLED,:],k,v,gas[h],h,lb,None)
+                if r==0: acc[h,0:FILLED,:]=dq
+                else: acc[h,0:FILLED,:]+=dq
+                dks.append(dk); dvs.append(dv)
+            dk_ref[rows,:]=(both(dks,lb)*LN2).astype(BF)
+            dv_ref[rows,:]=both(dvs,lb).astype(BF)
+        dq_ref[0:FILLED,:]=(jnp.where(lf<64,acc[0,0:FILLED,:],acc[1,0:FILLED,:])*0.125).astype(BF)
+    @pl.when(jnp.logical_not(single))
+    def _():
+        row=lax.broadcasted_iota(jnp.int32,(512,128),0)
+        lw=lanes(512); lq=lanes(128)
+        acc_k[...]=jnp.zeros_like(acc_k); acc_v[...]=jnp.zeros_like(acc_v)
+        for i in range(13):
+            lo=info[1+i]; hi=info[14+i]
+            at=jnp.minimum(lo,9)
+            window=pl.ds(pl.multiple_of(at*128,128),512)
+            k=k_ref[window,:]; v=v_ref[window,:]
+            keep=(row>=(lo-at)*128)&(row<(hi-at)*128)
+            rows=slice(i*128,i*128+128)
+            gas=deltas(g_ref[rows,:],o_ref[rows,:],ol_ref[rows,:],lq)
+            dqs=[]
+            for h in (0,1):
+                dq,dk,dv=bwd_tile(qa_ref[h,rows,:],k,v,gas[h],h,lw,keep)
+                dqs.append(dq)
+                acc_k[h,window,:]+=dk
+                acc_v[h,window,:]+=dv
+            dq_ref[rows,:]=(both(dqs,lq)*0.125).astype(BF)
+        lf=lanes(FILLED)
+        dk_ref[0:FILLED,:]=(jnp.where(lf<64,acc_k[0],acc_k[1])*LN2).astype(BF)
+        dv_ref[0:FILLED,:]=jnp.where(lf<64,acc_v[0],acc_v[1]).astype(BF)
+    rows=slice(FILLED,FILLED+PAD)
+    lp=lanes(PAD)
+    gas=deltas(g_ref[rows,:],o_ref[rows,:],ol_ref[rows,:],lp)
+    t=[bwd_tile(qa_ref[h,rows,:],k_ref[rows,:],v_ref[rows,:],gas[h],h,lp,None) for h in (0,1)]
+    dq_ref[rows,:]=(both([a[0] for a in t],lp)*0.125).astype(BF)
+    dk_ref[rows,:]=(both([a[1] for a in t],lp)*LN2).astype(BF)
+    dv_ref[rows,:]=both([a[2] for a in t],lp).astype(BF)
+    sum_ref[0:1,:]=jnp.sum(dq_ref[...].astype(F32),axis=0,keepdims=True)
+    sum_ref[1:2,:]=jnp.sum(dv_ref[...].astype(F32),axis=0,keepdims=True)
+def attn_bwd(info,qa,qkv,o,ol,g,first,count,inner,bk=832):
+    L,W3=qkv.shape; n=W3//384
+    spec=lambda j: pl.BlockSpec((L,128),lambda p,s,j=j:(0,p+first+j*n))
     one=pl.BlockSpec((L,128),lambda p,s:(0,p))
-    return pl.pallas_call(functools.partial(bwd_kernel,bs,mode),
-        out_shape=(jax.ShapeDtypeStruct((L,W),BF),)*3,
-        grid_spec=pltpu.PrefetchScalarGridSpec(num_scalar_prefetch=1,grid=(n,),
-            in_specs=[pl.BlockSpec((2,L,128),lambda p,s:(p,0,0)),spec(1),spec(2),one,one,one],
-            out_specs=(one,one,one),
-            scratch_shapes=[pltpu.VMEM((2,L,128),F32)]),
-        compiler_params=pltpu.CompilerParams(vmem_limit_bytes=50<<20),name="attn_backward",
-        cost_estimate=pl.CostEstimate(flops=5*2*2*n*L*L*256,bytes_accessed=16*L*W,transcendentals=2*n*L*L))(seg13,qa,qkv,qkv,o,ol,g)
+    part=pl.BlockSpec((L,128),lambda p,s:(0,p+inner))
+    every=pl.BlockSpec((L,128),lambda p,s:(0,p+first))
+    return pl.pallas_call(functools.partial(bwd_kernel,bk),
+        out_shape=(jax.ShapeDtypeStruct((L,count*128),BF),)*3+(jax.ShapeDtypeStruct((2,count*128),F32),),
+        grid_spec=pltpu.PrefetchScalarGridSpec(num_scalar_prefetch=1,grid=(count,),
+            in_specs=[pl.BlockSpec((2,L,128),lambda p,s:(p+inner,0,0)),spec(1),spec(2),part,part,every],
+            out_specs=(one,one,one,pl.BlockSpec((2,128),lambda p,s:(0,p))),
+            scratch_shapes=[pltpu.VMEM((2,FILLED,128),F32)]*3),
+        compiler_params=pltpu.CompilerParams(vmem_limit_bytes=56<<20),name="attn_backward",
+        cost_estimate=pl.CostEstimate(flops=20*count*L*L*256,bytes_accessed=16*L*count*128,transcendentals=2*count*L*L))(info,qa,qkv,qkv,o,ol,g)
 
 
 def gelu_exact(values):
@@ -451,7 +490,250 @@
     )
 
 
+GROUPS = 2
+SLOPE = F32
 LOG2E = 1.4426950408889634
+
+
+def layer_norm(values):
+    centered = values - jnp.mean(values, axis=1, keepdims=True)
+    inverse = lax.rsqrt(jnp.mean(centered * centered, axis=1, keepdims=True) + 1e-05)
+    return centered * inverse, inverse
+
+
+def layer_norm_back(scaled, unit_part, inverse):
+    return inverse * (
+        scaled
+        - jnp.mean(scaled, axis=1, keepdims=True)
+        - unit_part * jnp.mean(scaled * unit_part, axis=1, keepdims=True)
+    )
+
+
+def gelu_pair(v):
+    bell = jnp.exp2(v * v * (-0.5 * LOG2E))
+    base = 1.0 + 0.2316418882663604 * jnp.abs(v)
+    t = pltpu.reciprocal(base, approx=True)
+    t = t * (2.0 - base * t)
+    tail = t * (
+        0.127414796
+        + t * (-0.142248368 + t * (0.7107068705 + t * (-0.7265760135 + t * 0.5307027145)))
+    )
+    tail = tail * bell
+    cover = jnp.where(v >= 0, 1.0 - tail, tail)
+    return v * cover, cover + v * bell * 0.3989422804014327
+
+
+def middle_kernel(
+    fc,
+    sel_ref,
+    frac_ref,
+    inp_ref,
+    ctx_a_ref,
+    ctx_b_ref,
+    cot_ref,
+    vec_ref,
+    b_up_ref,
+    wo_a_ref,
+    wo_b_ref,
+    w_up_hbm,
+    w_down_hbm,
+    out_ref,
+    norm_ref,
+    act_ref,
+    two_ref,
+    hid_ref,
+    one_ref,
+    onel_ref,
+    small_ref,
+    smallup_ref,
+    w_up,
+    w_down,
+    slope,
+    sems,
+):
+    step = pl.program_id(0)
+    up_copy = pltpu.make_async_copy(w_up_hbm, w_up, sems.at[0])
+    down_copy = pltpu.make_async_copy(w_down_hbm, w_down, sems.at[1])
+
+    @pl.when(step == 0)
+    def _():
+        up_copy.start()
+        down_copy.start()
+        small_ref[...] = jnp.zeros_like(small_ref)
+        smallup_ref[...] = jnp.zeros_like(smallup_ref)
+
+    vec = lambda i: vec_ref[i : i + 1, :]
+    start = inp_ref[...].astype(F32) + (frac_ref[0] * vec(0) + vec(1))
+    residual = (
+        start
+        + dot(ctx_a_ref[...], wo_a_ref[...].reshape(-1, wo_a_ref.shape[-1]), NN)
+        + dot(ctx_b_ref[...], wo_b_ref[...].reshape(-1, wo_b_ref.shape[-1]), NN)
+        + vec(2)
+    )
+    unit_one, inverse_one = layer_norm(residual)
+    normed = unit_one * vec(3) + vec(4)
+    low = normed.astype(BF)
+    norm_ref[...] = low
+
+    @pl.when(step == 0)
+    def _():
+        up_copy.wait()
+        down_copy.wait()
+
+    width = w_up.shape[1]
+    total = normed + vec(5)
+    for f in range(0, width, fc):
+        cols = slice(f, f + fc)
+        v = dot(low, w_up[:, cols], NN) + b_up_ref[:, cols]
+        a, g = gelu_pair(v)
+        a = a.astype(BF)
+        act_ref[:, cols] = a
+        slope[:, cols] = g.astype(slope.dtype)
+        total = total + dot(a, w_down[cols, :], NN)
+    unit_two, inverse_two = layer_norm(total)
+    out_ref[...] = (unit_two * vec(6) + vec(7)).astype(BF)
+    cot = cot_ref[...].astype(F32)
+    two = layer_norm_back(cot * vec(6), unit_two, inverse_two)
+    add = lambda v: jnp.sum(v, axis=0, keepdims=True)
+    small_ref[3:4, :] += add(two)
+    small_ref[4:5, :] += add(cot * unit_two)
+    small_ref[5:6, :] += add(cot)
+    two_low = two.astype(BF)
+    two_ref[...] = two_low
+    total = two
+    for f in range(0, width, fc):
+        cols = slice(f, f + fc)
+        d = dot(two_low, w_down[cols, :], NT) * slope[:, cols].astype(F32)
+        smallup_ref[:, cols] += add(d)
+        d = d.astype(BF)
+        hid_ref[:, cols] = d
+        total = total + dot(d, w_up[:, cols], NT)
+    small_ref[1:2, :] += add(total * unit_one)
+    small_ref[2:3, :] += add(total)
+    one = layer_norm_back(total * vec(3), unit_one, inverse_one)
+    small_ref[0:1, :] += add(one)
+    one_ref[...] = one
+    onel_ref[...] = one.astype(BF)
+
+
+def middle(core, fraction, inp, ctx_a, ctx_b, cot, vecs, b_up, w_out, w_up, w_down, br=288, fc=2048):
+    rows, model = inp.shape
+    width = w_up.shape[1]
+    half = model // 2
+    quads = w_out.shape[0]
+    row = lambda w: pl.BlockSpec((br, w), lambda i, s: (i, 0))
+    fixed = lambda shape: pl.BlockSpec(shape, lambda i, s: (0,) * len(shape))
+    wo = lambda flip: pl.BlockSpec(
+        (quads, 1, model // quads // 2, model),
+        (lambda i, s: (0, s[0], 0, 0)) if not flip else (lambda i, s: (0, 1 - s[0], 0, 0)),
+    )
+    out = lambda w, t: jax.ShapeDtypeStruct((rows, w), t)
+    return pl.pallas_call(
+        functools.partial(middle_kernel, fc),
+        out_shape=(
+            out(model, BF),
+            out(model, BF),
+            out(width, BF),
+            out(model, BF),
+            out(width, BF),
+            out(model, F32),
+            out(model, BF),
+            jax.ShapeDtypeStruct((8, model), F32),
+            jax.ShapeDtypeStruct((1, width), F32),
+        ),
+        grid_spec=pltpu.PrefetchScalarGridSpec(
+            num_scalar_prefetch=1,
+            grid=(rows // br,),
+            in_specs=[
+                pl.BlockSpec(memory_space=pltpu.SMEM),
+                row(model),
+                row(half),
+                row(half),
+                row(model),
+                fixed((8, model)),
+                fixed((1, width)),
+                wo(False),
+                wo(True),
+                pl.BlockSpec(memory_space=pl.ANY),
+                pl.BlockSpec(memory_space=pl.ANY),
+            ],
+            out_specs=(
+                row(model),
+                row(model),
+                row(width),
+                row(model),
+                row(width),
+                row(model),
+                row(model),
+                fixed((8, model)),
+                fixed((1, width)),
+            ),
+            scratch_shapes=[
+                pltpu.VMEM(w_up.shape, BF),
+                pltpu.VMEM(w_down.shape, BF),
+                pltpu.VMEM((br, width), SLOPE),
+                pltpu.SemaphoreType.DMA((2,)),
+            ],
+        ),
+        compiler_params=pltpu.CompilerParams(vmem_limit_bytes=60 << 20),
+        cost_estimate=pl.CostEstimate(
+            flops=4 * rows * model * (model // 2 + 2 * width),
+            bytes_accessed=4 * model * width + rows * (16 * model + 4 * width),
+            transcendentals=rows * width * 2,
+        ),
+        name="middle",
+    )(core, fraction, inp, ctx_a, ctx_b, cot, vecs, b_up, w_out, w_out, w_up, w_down)
+
+
+def grad_kernel(count, extra, *refs):
+    lhs = [r[...] for r in refs[1 : 1 + count]]
+    rhs_ref = refs[1 + count]
+    out_ref = refs[-1]
+    left = lhs[0] if count == 1 else jnp.concatenate(lhs, axis=1)
+    total = dot(left, rhs_ref[...], TN)
+    if extra:
+        total = total + refs[2 + count][...].astype(F32)
+    out_ref[...] = total.astype(BF)
+
+
+def weight_grad(sel, lhs, rhs, add=None, cols=1024, quads=4, pairs=2):
+    depth, width = lhs.shape
+    n = rhs.shape[1]
+    w = width // (quads * pairs)
+    extra = add is not None
+    if w >= 512:
+        grid, count = (quads,), 1
+        ins = [
+            pl.BlockSpec((depth, w), lambda i, s: (0, pairs * i + s[0])),
+            pl.BlockSpec((depth, n), lambda i, s: (0, 0)),
+        ]
+        out = pl.BlockSpec((w, n), lambda i, s: (i, 0))
+        args = [lhs, rhs]
+    else:
+        grid, count = (n // cols,), quads
+        ins = [
+            pl.BlockSpec((depth, w), lambda i, s, q=q: (0, pairs * q + s[0])) for q in range(quads)
+        ] + [pl.BlockSpec((depth, cols), lambda i, s: (0, i))]
+        out = pl.BlockSpec((quads * w, cols), lambda i, s: (0, i))
+        args = [lhs] * quads + [rhs]
+    if extra:
+        ins.append(out)
+        args.append(add)
+    total = quads * w
+    return pl.pallas_call(
+        functools.partial(grad_kernel, count, extra),
+        out_shape=jax.ShapeDtypeStruct((total, n), BF),
+        grid_spec=pltpu.PrefetchScalarGridSpec(
+            num_scalar_prefetch=1, grid=grid, in_specs=ins, out_specs=out
+        ),
+        compiler_params=pltpu.CompilerParams(vmem_limit_bytes=48 << 20),
+        cost_estimate=pl.CostEstimate(
+            flops=2 * depth * total * n,
+            bytes_accessed=2 * depth * (total + n) + (4 if extra else 2) * total * n,
+            transcendentals=0,
+        ),
+        name="weight_grad",
+    )(sel, *args)
 
 
 class Plan:
@@ -562,7 +844,14 @@
     other_facts = plan.sibling(facts)
     facts = jnp.where(z // 2 == c, facts, other_facts)
     mine = pick(facts, z % 2, 0)
-    seg13 = mine[:13]
+    marks = mine[:13]
+    info = jnp.concatenate(
+        [
+            (marks[:1] == marks[12:]).astype(jnp.int32),
+            jnp.sum((marks[None, :] < marks[:, None]).astype(jnp.int32), axis=1),
+            jnp.sum((marks[None, :] <= marks[:, None]).astype(jnp.int32), axis=1),
+        ]
+    )
     fraction = mine[13].astype(F32) / TSTEPS
 
     def gather_rows(array):
@@ -608,17 +897,12 @@
         return array.reshape(plan.ny, plan.nx, plan.depth, -1, array.shape[-1])
 
     model = inputs.shape[-1]
-    own_inputs = gather_rows(inputs)
-    own_cotangent = gather_rows(cotangent)
-    start = (
-        own_inputs.astype(F32) + fraction * w_time.astype(F32)[None] + b_time.astype(F32)[None]
-    )
-    start_low = start.astype(BF)
-    start_full = whole(start_low, plan.sibling(start_low))
-    w_three = w_qkv.reshape(model, 3, model)
-    w_own = jnp.concatenate([halves(w_three[:, i], 1)[0] for i in range(3)], axis=1)
-    w_oth = jnp.concatenate([halves(w_three[:, i], 1)[1] for i in range(3)], axis=1)
     half = model // 2
+    quads = plan.ny * plan.nx
+    core = jnp.stack([c]).astype(jnp.int32)
+    away = 1 - core
+    w_four = w_qkv.reshape(model, 3, quads, 2, half // quads)
+    w_own, w_oth = pick(w_four, c, 3), pick(w_four, 1 - c, 3)
     bias = jnp.concatenate(
         [
             halves(b_query.astype(F32), 0)[0],
@@ -626,97 +910,96 @@
             halves(b_value.astype(F32), 0)[0],
         ]
     )
+    w_out_own = halves(w_out, 0)[0]
+    w_all = w_own.reshape(model, 3 * half)
+    groups = [range(g * (quads // GROUPS), (g + 1) * (quads // GROUPS)) for g in range(GROUPS)]
+    cut = lambda w: [w[:, :, g.start : g.stop].reshape(model, -1) for g in groups]
+    w_cut, w_cut_oth = cut(w_own), cut(w_oth)
+    own_inputs = gather_rows(inputs)
+    own_inputs, w_all, w_cut, w_cut_oth, w_out_own = lax.optimization_barrier(
+        (own_inputs, w_all, w_cut, w_cut_oth, w_out_own)
+    )
+    start = (
+        own_inputs.astype(F32) + fraction * w_time.astype(F32)[None] + b_time.astype(F32)[None]
+    )
+    start_low = start.astype(BF)
+    start_sib = plan.sibling(start_low)
+    cotangent, _ = lax.optimization_barrier((cotangent, start_low))
+    own_cotangent = gather_rows(cotangent)
+    start_full = whole(start_low, start_sib)
     scale = jnp.where(jnp.arange(3 * half) < half, 0.125 * LOG2E, 1.0)
-    qkv = ((jnp.dot(start_full, w_own, preferred_element_type=F32) + bias) * scale).astype(BF)
-    context, context_rest, query_rows = attn_fwd(seg13, qkv)
-    my_ctx, away_ctx = pick(context.reshape(2, rows, half), c, 0), pick(
-        context.reshape(2, rows, half), 1 - c, 0
-    )
-    ctx_rows = jnp.concatenate([my_ctx, plan.sibling(away_ctx)], axis=1)
-    w_out_own, w_out_oth = halves(w_out, 0)
-    w_out_cat = jnp.concatenate([w_out_own, w_out_oth])
-    residual_one = (
-        start + jnp.dot(ctx_rows, w_out_cat, preferred_element_type=F32) + b_out.astype(F32)
-    )
-    normed, unit_one, inverse_one = norm_forward(
-        residual_one, ln1_gain.astype(F32), ln1_bias.astype(F32)
-    )
-    normed_low = normed.astype(BF)
-    hidden_pre = jnp.dot(normed_low, w_up, preferred_element_type=F32) + b_up.astype(F32)
-    activated, gelu_pull = jax.vjp(gelu_exact, hidden_pre)
-    activated_low = activated.astype(BF)
-    residual_two = (
-        normed
-        + jnp.dot(activated_low, w_down, preferred_element_type=F32)
-        + b_down.astype(F32)
-    )
-    result, unit_two, inverse_two = norm_forward(
-        residual_two, ln2_gain.astype(F32), ln2_bias.astype(F32)
-    )
-    output = spread_rows(result.astype(BF))
-    grad_result = own_cotangent.astype(F32)
-    grad_two, grad_ln2_gain, grad_ln2_bias = norm_backward(
-        grad_result, unit_two, inverse_two, ln2_gain.astype(F32)
-    )
-    grad_b_down = jnp.sum(grad_two, axis=0)
-    grad_two_low = grad_two.astype(BF)
-    act_own, act_oth = halves(activated_low, 1)
-    down_away = lax.dot_general(act_oth, grad_two_low, TN, preferred_element_type=F32).astype(BF)
-    down_got = plan.sibling(down_away)
-    grad_activated = lax.dot_general(grad_two_low, w_down, NT, preferred_element_type=F32)
-    grad_hidden = gelu_pull(grad_activated)[0]
-    grad_b_up = jnp.sum(grad_hidden, axis=0)
-    grad_hidden_low = grad_hidden.astype(BF)
-    grad_normed = grad_two + lax.dot_general(
-        grad_hidden_low, w_up, NT, preferred_element_type=F32
-    )
-    nl_own, nl_oth = halves(normed_low, 1)
-    up_away = lax.dot_general(nl_oth, grad_hidden_low, TN, preferred_element_type=F32).astype(BF)
-    up_got = plan.sibling(up_away)
-    grad_one, grad_ln1_gain, grad_ln1_bias = norm_backward(
-        grad_normed, unit_one, inverse_one, ln1_gain.astype(F32)
-    )
-    grad_b_out = jnp.sum(grad_one, axis=0)
-    grad_one_low = grad_one.astype(BF)
-    grad_one_full = whole(grad_one_low, plan.sibling(grad_one_low))
-    down_sum = (
-        lax.dot_general(act_own, grad_two_low, TN, preferred_element_type=F32)
-        + down_got.astype(F32)
-    ).astype(BF)
-    sum_w_down = scatter_sum(plan, blocks(down_sum), "xy", where)
-    up_sum = (
-        lax.dot_general(nl_own, grad_hidden_low, TN, preferred_element_type=F32)
-        + up_got.astype(F32)
-    ).astype(BF)
-    sum_w_up = scatter_sum(plan, blocks(up_sum), "yx", where)
-    out_sum = lax.dot_general(context, grad_one_full, TN, preferred_element_type=F32).astype(BF)
-    sum_w_out = scatter_sum(plan, blocks(out_sum), "xy", where)
+    qkv = ((jnp.dot(start_full, w_all, preferred_element_type=F32) + bias) * scale).astype(BF)
+    fwd = [attn_fwd(info, qkv, g.start, len(g)) for g in groups]
+    mine_of, away_of = [], []
+    for g in range(GROUPS):
+        split = fwd[g][0].reshape(2, rows, -1)
+        mine_of.append(pick(split, c, 0))
+        away_of.append(plan.sibling(pick(split, 1 - c, 0)))
+    vecs = jnp.stack(
+        [v.astype(F32) for v in (w_time, b_time, b_out, ln1_gain, ln1_bias, b_down, ln2_gain, ln2_bias)]
+    )
+    result, normed_low, act, two_low, hid, grad_one, one_low, small_sums, up_sums = middle(
+        core,
+        fraction[None],
+        own_inputs,
+        jnp.concatenate(mine_of, axis=1),
+        jnp.concatenate(away_of, axis=1),
+        own_cotangent,
+        vecs,
+        b_up.astype(F32)[None],
+        w_out.reshape(quads, 2, -1, model),
+        w_up,
+        w_down,
+    )
+    grad_one_full = whole(one_low, plan.sibling(one_low))
+    down_got = plan.sibling(weight_grad(away, act, two_low, quads=quads))
+    up_got = plan.sibling(weight_grad(away, normed_low, hid, quads=quads))
+    output = spread_rows(result)
     grad_context = lax.dot_general(
         grad_one_full, w_out_own, NT, preferred_element_type=F32
     ).astype(BF)
-    grads = attn_bwd(seg13, query_rows, qkv, context, context_rest, grad_context)
-    grad_qkv = jnp.concatenate(grads, axis=1)
-    both = grad_qkv.reshape(2, rows, 3 * half)
-    qkv_mine = pick(both, c, 0)
-    qkv_got = plan.sibling(pick(both, 1 - c, 0))
-    grad_start = (
-        grad_one
-        + lax.dot_general(qkv_mine, w_own, NT, preferred_element_type=F32)
-        + lax.dot_general(qkv_got, w_oth, NT, preferred_element_type=F32)
-    )
+    down_sum = weight_grad(core, act, two_low, down_got, quads=quads)
+    up_sum = weight_grad(core, normed_low, hid, up_got, quads=quads)
+    grad_context, down_sum, up_sum = lax.optimization_barrier((grad_context, down_sum, up_sum))
+    sum_w_down = scatter_sum(plan, blocks(down_sum), "xy", where)
+    sum_w_up = scatter_sum(plan, blocks(up_sum), "yx", where)
+    context = jnp.concatenate([f[0] for f in fwd], axis=1)
+    out_sum = weight_grad(0 * core, context, grad_one_full, quads=quads, pairs=1, cols=512)
+    sum_w_out = scatter_sum(plan, blocks(out_sum), "yx", where)
+    grad_start = grad_one
+    keeps, crosses, b_sums = [], [], []
+    for g in range(GROUPS):
+        heads = groups[g]
+        dq, dk, dv, b_sum = attn_bwd(
+            info, fwd[g][2], qkv, fwd[g][0], fwd[g][1], grad_context, heads.start, len(heads), 0
+        )
+        b_sums.append(b_sum)
+        grad_qkv = jnp.concatenate([dq, dk, dv], axis=1)
+        both_halves = grad_qkv.reshape(2, rows, -1)
+        got = plan.sibling(pick(both_halves, 1 - c, 0))
+        cols = grad_qkv.shape[1]
+        cross = plan.sibling(weight_grad(away, start_full, grad_qkv, quads=quads, cols=cols))
+        keep = weight_grad(core, start_full, grad_qkv, quads=quads, cols=cols)
+        keeps.append(scatter_sum(plan, blocks(keep), "xy", where))
+        crosses.append(scatter_sum(plan, blocks(cross), "yx", where))
+        grad_start = (
+            grad_start
+            + lax.dot_general(pick(both_halves, c, 0), w_cut[g], NT, preferred_element_type=F32)
+            + lax.dot_general(got, w_cut_oth[g], NT, preferred_element_type=F32)
+        )
+        if g + 1 < GROUPS:
+            grad_context, grad_qkv = lax.optimization_barrier((grad_context, grad_qkv))
     grad_inputs = spread_rows(grad_start.astype(BF))
-    sf_own, sf_oth = halves(start_full, 1)
-    qkv_away = lax.dot_general(sf_oth, grad_qkv, TN, preferred_element_type=F32).astype(BF)
-    qkv_keep = lax.dot_general(sf_own, grad_qkv, TN, preferred_element_type=F32).astype(BF)
-    qkv_cross = plan.sibling(qkv_away)
-    sum_own = scatter_sum(plan, blocks(qkv_keep), "xy", where)
-    sum_oth = scatter_sum(plan, blocks(qkv_cross), "yx", where)
-    quads = plan.ny * plan.nx
+    split3 = lambda parts: jnp.concatenate(
+        [p.reshape(p.shape[0], 3, quads // GROUPS, -1) for p in parts], axis=2
+    )
+    sum_own, sum_oth = split3(keeps), split3(crosses)
+    b_sum = jnp.concatenate(b_sums, axis=1)
+    grad_b_query, grad_b_value = b_sum[0], b_sum[1]
     pair = jnp.where(c == 0, jnp.stack([sum_own, sum_oth]), jnp.stack([sum_oth, sum_own]))
     sum_w_qkv = (
-        pair.reshape(2, -1, 3, quads, half // quads).transpose(1, 2, 3, 0, 4).reshape(-1, 3 * model)
-    )
-    grad_b_own = jnp.sum(grad_qkv.astype(F32), axis=0)
+        pair.transpose(1, 2, 3, 0, 4).reshape(-1, 3 * model)
+    )
     grad_b_time = jnp.sum(grad_start, axis=0)
     grad_w_time = fraction * grad_b_time
     zero = jnp.zeros((quads, 2, half // quads), F32)
@@ -725,18 +1008,18 @@
         return lax.dynamic_update_index_in_dim(zero, v.reshape(quads, half // quads), c, 1).reshape(-1)
 
     vectors = [
-        placed(grad_b_own[:half]),
-        placed(grad_b_own[2 * half :]),
-        grad_b_out,
-        grad_ln1_gain,
-        grad_ln1_bias,
-        grad_b_down,
-        grad_ln2_gain,
-        grad_ln2_bias,
+        placed(grad_b_query),
+        placed(grad_b_value),
+        small_sums[0],
+        small_sums[1],
+        small_sums[2],
+        small_sums[3],
+        small_sums[4],
+        small_sums[5],
         grad_w_time,
         grad_b_time,
     ]
-    small = jnp.concatenate([v[:, None] for v in vectors] + [grad_b_up.reshape(model, -1)], axis=1)
+    small = jnp.concatenate([v[:, None] for v in vectors] + [up_sums.reshape(model, -1)], axis=1)
     small_own, small_oth = halves(small, 0)
     small_own = small_own + plan.sibling(small_oth)
     small_sum = scatter_sum(plan, blocks(small_own), "xy", where)

time: 797 us -> 664 us (0.83)
  Pallas kernels: 107 us -> 256 us
  matrix products: 172 us -> 23.8 us
  local copies, waits for them, and re-layouts: 162 us -> 79 us
  starting transfers between devices: 121 us -> 82.4 us
  waiting for transfers between devices: 169 us -> 159 us
    pallas_call x2 -> x14, Pallas kernels: 107 us -> 256 us  [the longest x2 110 us: attn_bwd(): pl.pallas_call(functools.partial(bwd_kernel, bk), out_shape=(jax.ShapeDty...]
    dot_general x15 -> x5, matrix products: 165 us -> 20.4 us  [the longest x1 7.7 us: per_chip(): jnp.dot(start_full, w_all, preferred_element_type=F32) + bias]
    ppermute x47 -> x60, starting transfers between devices: 121 us -> 82.4 us  [send(): return lax.ppermute(value, AXES, self.perm(target))]
    unnamed x157 -> x124, local copies, waits for them, and re-layouts: 62.1 us -> 26.3 us
    reshape x3 -> x5, local copies, waits for them, and re-layouts: 23.1 us -> 1.27 us  [the longest x1 1.06 us: per_chip(): sum_w_qkv = pair.transpose(1, 2, 3, 0, 4).reshape(-1, 3 * model)]
    concatenate x12 -> x8, local copies, waits for them, and re-layouts: 17.6 us -> 0.86 us  [the longest x5 0.73 us: per_chip(): jnp.concatenate([v[:, None] for v in vectors] + [up_sums.reshape(model, -...]
    dynamic_slice x11 -> x9, local copies, waits for them, and re-layouts: 32.1 us -> 16 us  [pick(): return lax.dynamic_index_in_dim(array, index, axis, keepdims=False)]
    ppermute x47 -> x60, waiting for transfers between devices: 169 us -> 159 us  [send(): return lax.ppermute(value, AXES, self.perm(target))]
  transfers between devices with their start and end apart: 47 -> 60, of which waited for: 20 -> 23; matrix products, arithmetic and copies ran while one was open for 33% -> 17% of each run, Pallas kernels for 9% -> 11%
where the time goes in v2:
time: 664 us; the launch traced here: 652 us
  Pallas kernels  256 us (39%)
  waiting for transfers between devices  159 us (24%)
  starting transfers between devices  82.4 us (12%)
  local copies, waits for them, and re-layouts  79 us (12%)
  other arithmetic  46.7 us (7%)
  matrix products  23.8 us (4%)
    ppermute x60, waiting for transfers between devices, send(): return lax.ppermute(value, AXES, self.perm(target))  159 us
    pallas_call x2, Pallas kernels, attn_bwd(): pl.pallas_call(functools.partial(bwd_kernel, bk), out_shape=(jax.ShapeDty...  110 us
    ppermute x60, starting transfers between devices, send(): return lax.ppermute(value, AXES, self.perm(target))  82.4 us
    pallas_call x1, Pallas kernels, middle(): pl.pallas_call(functools.partial(middle_kernel, fc), out_shape=(out(model...  54.2 us
    pallas_call x9, Pallas kernels, weight_grad(): pl.pallas_call(functools.partial(grad_kernel, count, extra), out_shape=ja...  50 us
    pallas_call x2, Pallas kernels, attn_fwd(): pl.pallas_call(functools.partial(fwd_kernel, bq), out_shape=(jax.ShapeDty...  41.4 us
    unnamed x124, local copies, waits for them, and re-layouts  26.3 us
    dynamic_slice x9, local copies, waits for them, and re-layouts, pick(): return lax.dynamic_index_in_dim(array, index, axis, keepdims=False)  16 us
  transfers between devices with their start and end apart: 60, of which 23 were waited for; matrix products, arithmetic and copies ran while one was open for 17% of the time, Pallas kernels for 11%

profile of v2, /device:TPU:0, one launch (start us, length us, event | category | flops | bytes accessed | tf_op | source)
XLA Modules:
  0.0 651.9 jit_solution(11715292227922172522)
XLA Ops:
  3.3 2.8 dynamic-slice_bitcast_fusion.13
  6.1 8.2 %collective-permute-start.1 = (bf16[432,1024]{1,0:T(8,128)(2,1)}, bf16[432,1024]{1,0:T(8,128)(2,1)}, u32[]{:S(2)}, u32[]{:S(2)}) collective-permute-start(bf16[432,1024]{1,0:T(8,128)(2,1)} %get-tuple-element.111), channel_id=1, source_target_pairs={{0,0},{1,1},{2,4},{3,5},{4,2},{5,3},{6,6},{7,7},{8,8},{9,9},{10,12... | collective-permute-start | bytes 2654216 | tf_op jit(solution)/shard_map/ppermute | solution.py:764
  14.3 3.0 collective-permute-start.2
  18.5 8.7 %copy.130 = bf16[1024,3072]{0,1:T(8,128)(2,1)} copy(bf16[1024,3072]{1,0:T(8,128)(2,1)} %param.23) | data formatting | bytes 12582912 | tf_op args[4]
  27.2 6.6 %constant_dynamic-slice_fusion.9 = (bf16[1024,3,4,1,128]{0,4,3,2,1:T(8,128)(2,1)}, bf16[1024,3,4,1,128]{0,4,3,2,1:T(8,128)(2,1)}) fusion(bf16[1024,3,4,2,128]{0,4,3,2,1:T(8,128)(2,1)} %bitcast.324, s32[]{:T(128)S(6)} %select_n.411, s32[]{:T(128)S(6)} %select_n.410), kind=kLoop, calls=%fused_computation.167 | loop fusion | bytes 12582920 | tf_op jit(solution)/shard_map/jit(dynamic_index_in_dim)/dynamic_slice | solution.py:771
  33.8 3.5 copy.131
  37.3 1.8 fusion.44
  39.1 3.5 copy.134
  42.6 1.9 fusion.43
  44.5 2.7 copy.133
  47.2 2.7 copy.135
  53.1 2.3 constant_dynamic-slice_fusion.8
  73.3 3.1 maximum_select_fusion.refs_1_.refs_2_.refs_3_.refs_4_
  78.3 7.7 %multiply_convert_fusion.q_ref.k_ref.v_ref = bf16[1728,1536]{1,0:T(8,128)(2,1)} fusion(bf16[1728,1024]{1,0:T(8,128)(2,1)S(1)} %maximum_select_fusion.refs_1_.refs_2_.refs_3_.refs_4_, bf16[1024,1536]{0,1:T(8,128)(2,1)S(1)} %bitcast.327, f32[1536]{0:T(1024)S(1)} %fusion.39, f32[1536]{0:T(1024)S(1)} %pad_maximum_fusion.9), kind=kOutput, calls=%fused_computation | convolution fusion | flops 5443780608 | bytes 12005376 | tf_op jit(solution)/shard_map/dot_general | solution.py:931
  86.0 20.7 %attn_forward.2 = (bf16[1728,256]{1,0:T(8,128)(2,1)S(1)}, bf16[1728,256]{1,0:T(8,128)(2,1)S(1)}, bf16[4,1728,128]{2,1,0:T(8,128)(2,1)S(1)}) custom-call(s32[27]{0:T(128)S(1)} %pad_add_fusion.1.info, bf16[1728,1536]{1,0:T(8,128)(2,1)} %multiply_convert_fusion.q_ref.k_ref.v_ref, bf16[1728,1536]{1,0:T(8,128)(2,1)} %multiply_convert_fusion.q_ref.k_ref.v_ref, ...), custom_call_target="tpu_custom_call" | custom-call | flops 12230590464 | bytes 4423680 | tf_op jit(solution)/shard_map/attn_forward/pallas_call | solution.py:87
  108.8 3.4 collective-permute-start.4
  112.2 20.8 %attn_forward.3 = (bf16[1728,256]{1,0:T(8,128)(2,1)S(1)}, bf16[1728,256]{1,0:T(8,128)(2,1)S(1)}, bf16[4,1728,128]{2,1,0:T(8,128)(2,1)S(1)}) custom-call(s32[27]{0:T(128)S(1)} %pad_add_fusion.1.info, bf16[1728,1536]{1,0:T(8,128)(2,1)} %multiply_convert_fusion.q_ref.k_ref.v_ref, bf16[1728,1536]{1,0:T(8,128)(2,1)} %multiply_convert_fusion.q_ref.k_ref.v_ref, ...), custom_call_target="tpu_custom_call" | custom-call | flops 12230590464 | bytes 4423680 | tf_op jit(solution)/shard_map/attn_forward/pallas_call | solution.py:87
  137.8 54.2 %middle.1 = (bf16[864,1024]{1,0:T(8,128)(2,1)}, bf16[864,1024]{1,0:T(8,128)(2,1)}, bf16[864,4096]{1,0:T(8,128)(2,1)}, bf16[864,1024]{1,0:T(8,128)(2,1)}, bf16[86...) custom-call(s32[1]{0:T(128)} %bitcast.1.sel_ref.refs_0_, ...), custom_call_target="tpu_custom_call" | custom-call | flops 30802968576 | bytes 45088768 | tf_op jit(solution)/shard_map/middle/pallas_call | solution.py:631
  193.6 8.6 %weight_grad.11 = bf16[512,4096]{1,0:T(8,128)(2,1)} custom-call(s32[1]{0:T(128)S(6)} %sub.24.refs_0_, bf16[864,1024]{1,0:T(8,128)(2,1)S(1)} %copy-done, bf16[864,1024]{1,0:T(8,128)(2,1)S(1)} %copy-done, bf16[864,1024]{1,0:T(8,128)(2,1)S(1)} %copy-done, bf16[864,1024]{1,0:T(8,128)(2,1)S(1)} %copy-done, bf16[864,4096]{1,0:T(8,128)(2,1)} %get-tuple-element.66.refs_5_), custom_call_target="tpu_custom_call" | custom-call | flops 3623878656 | bytes 12156928 | tf_op jit(solution)/shard_map/weight_grad/pallas_call | solution.py:723
  202.7 7.7 %weight_grad.9 = bf16[2048,1024]{1,0:T(8,128)(2,1)} custom-call(s32[1]{0:T(128)S(6)} %sub.24.refs_0_, bf16[864,4096]{1,0:T(8,128)(2,1)} %get-tuple-element.63.refs_1_, bf16[864,1024]{1,0:T(8,128)(2,1)S(1)} %copy-done.10), custom_call_target="tpu_custom_call" | custom-call | flops 3623878656 | bytes 9502720 | tf_op jit(solution)/shard_map/weight_grad/pallas_call | solution.py:723
  211.8 4.2 maximum_select_fusion.1.refs_5_
  216.0 4.0 weight_grad.17
  220.9 1.9 collective-permute-start.45
  223.8 1.8 collective-permute-start.8
  227.6 7.6 %collective-permute-done.45 = bf16[2,4,32,1024]{3,2,1,0:T(8,128)(2,1)} collective-permute-done((bf16[2,4,32,1024]{3,2,1,0:T(8,128)(2,1)}, bf16[2,4,32,1024]{3,2,1,0:T(8,128)(2,1)}, u32[]{:S(2)}, u32[]{:S(2)}) %collective-permute-start.45) | collective-permute-done | bytes 524320 | tf_op jit(solution)/shard_map/ppermute | solution.py:764
  236.5 1.8 collective-permute-start.46
  238.3 19.5 %collective-permute-done.9 = bf16[432,1024]{1,0:T(8,128)(2,1)} collective-permute-done((bf16[432,1024]{1,0:T(8,128)(2,1)S(1)}, bf16[432,1024]{1,0:T(8,128)(2,1)}, u32[]{:S(2)}, u32[]{:S(2)}) %collective-permute-start.9) | collective-permute-done | bytes 884768 | tf_op jit(solution)/shard_map/ppermute | solution.py:764
  260.6 8.4 %collective-permute-start.48 = (bf16[32,1024]{1,0:T(8,128)(2,1)S(1)}, bf16[32,1024]{1,0:T(8,128)(2,1)S(1)}, u32[]{:S(2)}, u32[]{:S(2)}) collective-permute-start(bf16[32,1024]{1,0:T(8,128)(2,1)S(1)} %get-tuple-element.125), channel_id=1, source_target_pairs={{0,2},{1,3},{2,0},{3,1},{4,6},{5,7},{6,4},{7,5},{8,10},{9,11},{10,... | collective-permute-start | bytes 196616 | tf_op jit(solution)/shard_map/ppermute | solution.py:764
  269.0 2.8 collective-permute-start.49
  271.9 3.3 convolution_convert_fusion.g_ref
  275.9 7.9 %weight_grad.12 = bf16[512,4096]{1,0:T(8,128)(2,1)S(1)} custom-call(s32[1]{0:T(128)} %bitcast.1.sel_ref.refs_0_, bf16[864,1024]{1,0:T(8,128)(2,1)S(1)} %copy-done.1, bf16[864,1024]{1,0:T(8,128)(2,1)S(1)} %copy-done.1, bf16[864,1024]{1,0:T(8,128)(2,1)S(1)} %copy-done.1, bf16[864,1024]{1,0:T(8,128)(2,1)S(1)} %copy-done.1, ...), custom_call_target="tpu_custom_call" | custom-call | flops 3623878656 | bytes 16351232 | tf_op jit(solution)/shard_map/weight_grad/pallas_call | solution.py:723
  283.8 8.4 %weight_grad.10 = bf16[2048,1024]{1,0:T(8,128)(2,1)S(1)} custom-call(s32[1]{0:T(128)} %bitcast.1.sel_ref.refs_0_, bf16[864,4096]{1,0:T(8,128)(2,1)} %get-tuple-element.63.refs_1_, bf16[864,1024]{1,0:T(8,128)(2,1)S(1)} %copy-done.11, bf16[2048,1024]{1,0:T(8,128)(2,1)} %collective-permute-done.11.refs_3_), custom_call_target="tpu_custom_call" | custom-call | flops 3623878656 | bytes 13697024 | tf_op jit(solution)/shard_map/weight_grad/pallas_call | solution.py:723
  292.3 2.0 copy-done.4
  294.3 55.2 %attn_backward.2 = (bf16[1728,256]{1,0:T(8,128)(2,1)}, bf16[1728,256]{1,0:T(8,128)(2,1)}, bf16[1728,256]{1,0:T(8,128)(2,1)}, f32[2,256]{1,0:T(2,128)}) custom-call(s32[27]{0:T(128)} %copy-done.12, bf16[4,1728,128]{2,1,0:T(8,128)(2,1)} %copy-done.14, bf16[1728,1536]{1,0:T(8,128)(2,1)} %multiply_convert_fusion.q_ref.k_ref.v_ref, ...), custom_call_target="tpu_custom_call" | custom-call | flops 30576476160 | bytes 7077888 | tf_op jit(solution)/shard_map/attn_backward/pallas_call | solution.py:163
  352.1 3.1 weight_grad.13
  355.2 54.7 %attn_backward.3 = (bf16[1728,256]{1,0:T(8,128)(2,1)}, bf16[1728,256]{1,0:T(8,128)(2,1)}, bf16[1728,256]{1,0:T(8,128)(2,1)}, f32[2,256]{1,0:T(2,128)}) custom-call(s32[27]{0:T(128)} %copy-done.12, bf16[4,1728,128]{2,1,0:T(8,128)(2,1)} %copy-done.13, bf16[1728,1536]{1,0:T(8,128)(2,1)} %multiply_convert_fusion.q_ref.k_ref.v_ref, ...), custom_call_target="tpu_custom_call" | custom-call | flops 30576476160 | bytes 7077888 | tf_op jit(solution)/shard_map/attn_backward/pallas_call | solution.py:163
  412.6 3.1 weight_grad.14
  416.6 4.2 weight_grad.16
  425.1 3.3 fusion.6
  430.3 3.3 fusion.4
  435.9 3.1 weight_grad.15
  439.6 6.1 collective-permute-done.17
  446.4 6.2 collective-permute-done.22
  454.3 4.2 collective-permute-done.23
  471.4 9.2 %collective-permute-done.28 = bf16[2,4,32,768]{3,2,1,0:T(8,128)(2,1)} collective-permute-done((bf16[2,4,32,768]{3,2,1,0:T(8,128)(2,1)}, bf16[2,4,32,768]{3,2,1,0:T(8,128)(2,1)}, u32[]{:S(2)}, u32[]{:S(2)}) %collective-permute-start.28) | collective-permute-done | bytes 393248 | tf_op jit(solution)/shard_map/ppermute | solution.py:764
  482.7 6.2 collective-permute-done.34
  490.5 3.0 fusion.49
  494.4 3.2 fusion.42
  501.6 21.1 %collective-permute-done.40 = f32[2,4,32,14]{2,1,3,0:T(4,128)S(1)} collective-permute-done((f32[2,4,32,14]{2,1,3,0:T(4,128)S(1)}, f32[2,4,32,14]{2,1,3,0:T(4,128)S(1)}, u32[]{:S(2)}, u32[]{:S(2)}) %collective-permute-start.40) | collective-permute-done | bytes 14368 | tf_op jit(solution)/shard_map/ppermute | solution.py:764
  525.2 8.8 %collective-permute-done.41 = f32[4,32,14]{1,0,2:T(4,128)S(1)} collective-permute-done((f32[4,32,14]{1,0,2:T(4,128)S(1)}, f32[4,32,14]{1,0,2:T(4,128)S(1)}, u32[]{:S(2)}, u32[]{:S(2)}) %collective-permute-start.41) | collective-permute-done | bytes 7200 | tf_op jit(solution)/shard_map/ppermute | solution.py:764
  534.1 2.3 collective-permute-start.43
  541.0 2.5 collective-permute-start.32
  545.5 8.2 %collective-permute-start.15 = (bf16[432,1024]{1,0:T(8,128)(2,1)}, bf16[432,1024]{1,0:T(8,128)(2,1)}, u32[]{:S(2)}, u32[]{:S(2)}) collective-permute-start(bf16[432,1024]{1,0:T(8,128)(2,1)} %get-tuple-element.99), channel_id=1, source_target_pairs={{0,0},{1,1},{2,4},{3,5},{4,2},{5,3},{6,6},{7,7},{8,8},{9,9},{10,12... | collective-permute-start | bytes 2654216 | tf_op jit(solution)/shard_map/ppermute | solution.py:764
  553.7 2.0 collective-permute-start.36
  555.9 3.4 fusion
  559.3 2.5 collective-permute-start.38
  561.8 2.4 fusion.1
  565.3 14.2 %collective-permute-done.36 = bf16[32,768]{1,0:T(8,128)(2,1)S(1)} collective-permute-done((bf16[32,768]{1,0:T(8,128)(2,1)S(1)}, bf16[32,768]{1,0:T(8,128)(2,1)S(1)}, u32[]{:S(2)}, u32[]{:S(2)}) %collective-permute-start.36) | collective-permute-done | bytes 49184 | tf_op jit(solution)/shard_map/ppermute | solution.py:764
  580.3 10.2 %collective-permute-done.37 = bf16[32,768]{1,0:T(8,128)(2,1)S(1)} collective-permute-done((bf16[32,768]{1,0:T(8,128)(2,1)S(1)}, bf16[32,768]{1,0:T(8,128)(2,1)S(1)}, u32[]{:S(2)}, u32[]{:S(2)}) %collective-permute-start.37) | collective-permute-done | bytes 49184 | tf_op jit(solution)/shard_map/ppermute | solution.py:764
  597.3 8.0 %collective-permute-done.56 = bf16[4,128,1024]{2,1,0:T(8,128)(2,1)} collective-permute-done((bf16[4,128,1024]{2,1,0:T(8,128)(2,1)}, bf16[4,128,1024]{2,1,0:T(8,128)(2,1)}, u32[]{:S(2)}, u32[]{:S(2)}) %collective-permute-start.56) | collective-permute-done | bytes 1048608 | tf_op jit(solution)/shard_map/ppermute | solution.py:764
  607.6 3.4 collective-permute-start.59
  613.1 3.3 collective-permute-start.53
  620.7 17.7 %collective-permute-done.58 = bf16[128,1024]{1,0:T(8,128)(2,1)S(1)} collective-permute-done((bf16[128,1024]{1,0:T(8,128)(2,1)S(1)}, bf16[128,1024]{1,0:T(8,128)(2,1)S(1)}, u32[]{:S(2)}, u32[]{:S(2)}) %collective-permute-start.58) | collective-permute-done | bytes 262176 | tf_op jit(solution)/shard_map/ppermute | solution.py:764
  639.3 11.5 %collective-permute-done.53 = bf16[32,4096]{1,0:T(8,128)(2,1)S(1)} collective-permute-done((bf16[32,4096]{1,0:T(8,128)(2,1)S(1)}, bf16[32,4096]{1,0:T(8,128)(2,1)S(1)}, u32[]{:S(2)}, u32[]{:S(2)}) %collective-permute-start.53) | collective-permute-done | bytes 262176 | tf_op jit(solution)/shard_map/ppermute | solution.py:764
  (339 shorter events, 109.3 us)
Async XLA Ops:
  6.1 50.6 %collective-permute-start.1 = (bf16[432,1024]{1,0:T(8,128)(2,1)}, bf16[432,1024]{1,0:T(8,128)(2,1)}, u32[]{:S(2)}, u32[]{:S(2)}) collective-permute-start(bf16[432,1024]{1,0:T(8,128)(2,1)} %get-tuple-element.111), channel_id=1, source_target_pairs={{0,0},{1,1},{2,4},{3,5},{4,2},{5,3},{6,6},{7,7},{8,8},{9,9},{10,12... | collective-permute-start | bytes 2654216 | tf_op jit(solution)/shard_map/ppermute | solution.py:764
  14.3 42.4 %collective-permute-start.2 = (bf16[432,1024]{1,0:T(8,128)(2,1)}, bf16[432,1024]{1,0:T(8,128)(2,1)}, u32[]{:S(2)}, u32[]{:S(2)}) collective-permute-start(bf16[432,1024]{1,0:T(8,128)(2,1)} %get-tuple-element.112), channel_id=1, source_target_pairs={{0,1},{1,0},{2,5},{3,4},{4,3},{5,2},{6,7},{7,6},{8,9},{9,8},{10,13... | collective-permute-start | bytes 2654216 | tf_op jit(solution)/shard_map/ppermute | solution.py:764
  18.4 37.0 %collective-permute-start = (s32[2,16]{1,0:T(2,128)S(1)}, s32[2,16]{1,0:T(2,128)S(1)}, u32[]{:S(2)}, u32[]{:S(2)}) collective-permute-start(s32[2,16]{1,0:T(2,128)S(1)} %pad_add_fusion), channel_id=1, source_target_pairs={{0,4},{1,5},{2,6},{3,7},{4,0},{5,1},{6,2},{7,3},{8,12},{9,13},{10,... | collective-permute-start | bytes 392 | tf_op jit(solution)/shard_map/ppermute | solution.py:764
  59.0 14.4 %collective-permute-start.3 = (bf16[864,1024]{1,0:T(8,128)(2,1)S(1)}, bf16[864,1024]{1,0:T(8,128)(2,1)}, u32[]{:S(2)}, u32[]{:S(2)}) collective-permute-start(bf16[864,1024]{1,0:T(8,128)(2,1)S(1)} %add_convert_fusion), channel_id=1, source_target_pairs={{0,4},{1,5},{2,6},{3,7},{4,0},{5,1},{6,2},{7,3},{8,12},{9,13},{10,... | collective-permute-start | bytes 5308424 | tf_op jit(solution)/shard_map/ppermute | solution.py:764
  70.9 41.3 %copy-start.12 = (s32[27]{0:T(128)}, s32[27]{0:T(128)S(1)}, u32[]{:S(2)}) copy-start(s32[27]{0:T(128)S(1)} %pad_add_fusion.1.info) | copy-start | bytes 328
  72.5 60.7 %collective-permute-start.6 = (bf16[432,1024]{1,0:T(8,128)(2,1)S(1)}, bf16[432,1024]{1,0:T(8,128)(2,1)S(1)}, u32[]{:S(2)}, u32[]{:S(2)}) collective-permute-start(bf16[432,1024]{1,0:T(8,128)(2,1)S(1)} %get-tuple-element.107), channel_id=1, source_target_pairs={{0,0},{1,1},{2,4},{3,5},{4,2},{5,3},{6,6},{7,7},{8,8},{9,9},{10,12... | collective-permute-start | bytes 2654216 | tf_op jit(solution)/shard_map/ppermute | solution.py:764
  73.3 59.9 %collective-permute-start.7 = (bf16[432,1024]{1,0:T(8,128)(2,1)S(1)}, bf16[432,1024]{1,0:T(8,128)(2,1)S(1)}, u32[]{:S(2)}, u32[]{:S(2)}) collective-permute-start(bf16[432,1024]{1,0:T(8,128)(2,1)S(1)} %get-tuple-element.108), channel_id=1, source_target_pairs={{0,1},{1,0},{2,5},{3,4},{4,3},{5,2},{6,7},{7,6},{8,9},{9,8},{10,13... | collective-permute-start | bytes 2654216 | tf_op jit(solution)/shard_map/ppermute | solution.py:764
  107.9 102.5 %copy-start.7 = (bf16[1728,256]{1,0:T(8,128)(2,1)}, bf16[1728,256]{1,0:T(8,128)(2,1)S(1)}, u32[]{:S(2)}) copy-start(bf16[1728,256]{1,0:T(8,128)(2,1)S(1)} %get-tuple-element.54.o_ref) | copy-start | bytes 2654212
  108.8 28.1 %collective-permute-start.4 = (bf16[864,256]{1,0:T(8,128)(2,1)S(1)}, bf16[864,256]{1,0:T(8,128)(2,1)S(1)}, u32[]{:S(2)}, u32[]{:S(2)}) collective-permute-start(bf16[864,256]{1,0:T(8,128)(2,1)S(1)} %get-tuple-element.119), channel_id=1, source_target_pairs={{0,4},{1,5},{2,6},{3,7},{4,0},{5,1},{6,2},{7,3},{8,12},{9,13},{10,... | collective-permute-start | bytes 1327112 | tf_op jit(solution)/shard_map/ppermute | solution.py:764
  133.0 77.3 %copy-start.6 = (bf16[1728,256]{1,0:T(8,128)(2,1)}, bf16[1728,256]{1,0:T(8,128)(2,1)S(1)}, u32[]{:S(2)}) copy-start(bf16[1728,256]{1,0:T(8,128)(2,1)S(1)} %get-tuple-element.55.o_ref) | copy-start | bytes 2654212
  133.1 3.8 collective-permute-start.5
  192.1 18.4 %collective-permute-start.10 = (bf16[864,1024]{1,0:T(8,128)(2,1)}, bf16[864,1024]{1,0:T(8,128)(2,1)}, u32[]{:S(2)}, u32[]{:S(2)}) collective-permute-start(bf16[864,1024]{1,0:T(8,128)(2,1)} %get-tuple-element.61), channel_id=1, source_target_pairs={{0,4},{1,5},{2,6},{3,7},{4,0},{5,1},{6,2},{7,3},{8,12},{9,13},{10,... | collective-permute-start | bytes 5308424 | tf_op jit(solution)/shard_map/ppermute | solution.py:764
  202.2 73.7 %collective-permute-start.12 = (bf16[512,4096]{1,0:T(8,128)(2,1)}, bf16[512,4096]{1,0:T(8,128)(2,1)}, u32[]{:S(2)}, u32[]{:S(2)}) collective-permute-start(bf16[512,4096]{1,0:T(8,128)(2,1)} %weight_grad.11), channel_id=1, source_target_pairs={{0,4},{1,5},{2,6},{3,7},{4,0},{5,1},{6,2},{7,3},{8,12},{9,13},{10,... | collective-permute-start | bytes 12582920 | tf_op jit(solution)/shard_map/ppermute | solution.py:764
  210.3 73.5 %collective-permute-start.11 = (bf16[2048,1024]{1,0:T(8,128)(2,1)}, bf16[2048,1024]{1,0:T(8,128)(2,1)}, u32[]{:S(2)}, u32[]{:S(2)}) collective-permute-start(bf16[2048,1024]{1,0:T(8,128)(2,1)} %weight_grad.9), channel_id=1, source_target_pairs={{0,4},{1,5},{2,6},{3,7},{4,0},{5,1},{6,2},{7,3},{8,12},{9,13},{10,... | collective-permute-start | bytes 12582920 | tf_op jit(solution)/shard_map/ppermute | solution.py:764
  220.9 14.3 %collective-permute-start.45 = (bf16[2,4,32,1024]{3,2,1,0:T(8,128)(2,1)}, bf16[2,4,32,1024]{3,2,1,0:T(8,128)(2,1)}, u32[]{:S(2)}, u32[]{:S(2)}) collective-permute-start(bf16[2,4,32,1024]{3,2,1,0:T(8,128)(2,1)} %dynamic-slice_bitcast_fusion.14), channel_id=1, source_target_pairs={{0,16},{1,17},{2,18},{3,19},{4,20},{5,21},{6,22},{7,23},{8,24},{9,... | collective-permute-start | bytes 1572872 | tf_op jit(solution)/shard_map/ppermute | solution.py:764
  223.8 14.4 %collective-permute-start.8 = (bf16[432,1024]{1,0:T(8,128)(2,1)}, bf16[432,1024]{1,0:T(8,128)(2,1)S(1)}, u32[]{:S(2)}, u32[]{:S(2)}) collective-permute-start(bf16[432,1024]{1,0:T(8,128)(2,1)} %get-tuple-element.103), channel_id=1, source_target_pairs={{0,0},{1,1},{2,4},{3,5},{4,2},{5,3},{6,6},{7,7},{8,8},{9,9},{10,12... | collective-permute-start | bytes 2654216 | tf_op jit(solution)/shard_map/ppermute | solution.py:764
  225.6 32.1 %collective-permute-start.9 = (bf16[432,1024]{1,0:T(8,128)(2,1)S(1)}, bf16[432,1024]{1,0:T(8,128)(2,1)}, u32[]{:S(2)}, u32[]{:S(2)}) collective-permute-start(bf16[432,1024]{1,0:T(8,128)(2,1)S(1)} %get-tuple-element.104), channel_id=1, source_target_pairs={{0,1},{1,0},{2,5},{3,4},{4,3},{5,2},{6,7},{7,6},{8,9},{9,8},{10,13... | collective-permute-start | bytes 2654216 | tf_op jit(solution)/shard_map/ppermute | solution.py:764
  236.5 24.0 %collective-permute-start.46 = (bf16[4,32,1024]{2,1,0:T(8,128)(2,1)S(1)}, bf16[4,32,1024]{2,1,0:T(8,128)(2,1)S(1)}, u32[]{:S(2)}, u32[]{:S(2)}) collective-permute-start(bf16[4,32,1024]{2,1,0:T(8,128)(2,1)S(1)} %dynamic-slice_bitcast_fusion.29), channel_id=1, source_target_pairs={{0,8},{1,9},{2,10},{3,11},{4,12},{5,13},{6,14},{7,15},{8,0},{9,1},... | collective-permute-start | bytes 786440 | tf_op jit(solution)/shard_map/ppermute | solution.py:764
  260.5 14.7 %collective-permute-start.47 = (bf16[32,1024]{1,0:T(8,128)(2,1)S(1)}, bf16[32,1024]{1,0:T(8,128)(2,1)S(1)}, u32[]{:S(2)}, u32[]{:S(2)}) collective-permute-start(bf16[32,1024]{1,0:T(8,128)(2,1)S(1)} %get-tuple-element.123), channel_id=1, source_target_pairs={{0,1},{1,2},{2,3},{3,0},{4,5},{5,6},{6,7},{7,4},{8,9},{9,10},{10,1... | collective-permute-start | bytes 196616 | tf_op jit(solution)/shard_map/ppermute | solution.py:764
  260.6 14.6 %collective-permute-start.48 = (bf16[32,1024]{1,0:T(8,128)(2,1)S(1)}, bf16[32,1024]{1,0:T(8,128)(2,1)S(1)}, u32[]{:S(2)}, u32[]{:S(2)}) collective-permute-start(bf16[32,1024]{1,0:T(8,128)(2,1)S(1)} %get-tuple-element.125), channel_id=1, source_target_pairs={{0,2},{1,3},{2,0},{3,1},{4,6},{5,7},{6,4},{7,5},{8,10},{9,11},{10,... | collective-permute-start | bytes 196616 | tf_op jit(solution)/shard_map/ppermute | solution.py:764
  269.0 6.2 collective-permute-start.49
  283.8 138.5 %copy-start.2 = (bf16[512,4096]{1,0:T(8,128)(2,1)}, bf16[512,4096]{1,0:T(8,128)(2,1)S(1)}, u32[]{:S(2)}) copy-start(bf16[512,4096]{1,0:T(8,128)(2,1)S(1)} %weight_grad.12) | copy-start | bytes 12582916
  433.6 12.1 %collective-permute-start.17 = (bf16[2,4,32,768]{3,2,1,0:T(8,128)(2,1)S(1)}, bf16[2,4,32,768]{3,2,1,0:T(8,128)(2,1)S(1)}, u32[]{:S(2)}, u32[]{:S(2)}) collective-permute-start(bf16[2,4,32,768]{3,2,1,0:T(8,128)(2,1)S(1)} %dynamic-slice_bitcast_fusion.22), channel_id=1, source_target_pairs={{0,8},{1,9},{2,10},{3,11},{4,12},{5,13},{6,14},{7,15},{8,0},{9,1},... | collective-permute-start | bytes 1179656 | tf_op jit(solution)/shard_map/ppermute | solution.py:764
  435.2 17.5 %collective-permute-start.22 = (bf16[2,4,32,768]{3,2,1,0:T(8,128)(2,1)S(1)}, bf16[2,4,32,768]{3,2,1,0:T(8,128)(2,1)S(1)}, u32[]{:S(2)}, u32[]{:S(2)}) collective-permute-start(bf16[2,4,32,768]{3,2,1,0:T(8,128)(2,1)S(1)} %dynamic-slice_bitcast_fusion.21), channel_id=1, source_target_pairs={{0,8},{1,9},{2,10},{3,11},{4,12},{5,13},{6,14},{7,15},{8,0},{9,1},... | collective-permute-start | bytes 1179656 | tf_op jit(solution)/shard_map/ppermute | solution.py:764
  435.8 33.4 %collective-permute-start.33 = (bf16[512,768]{1,0:T(8,128)(2,1)}, bf16[512,768]{1,0:T(8,128)(2,1)S(1)}, u32[]{:S(2)}, u32[]{:S(2)}) collective-permute-start(bf16[512,768]{1,0:T(8,128)(2,1)} %weight_grad.16), channel_id=1, source_target_pairs={{0,4},{1,5},{2,6},{3,7},{4,0},{5,1},{6,2},{7,3},{8,12},{9,13},{10,... | collective-permute-start | bytes 2359304 | tf_op jit(solution)/shard_map/ppermute | solution.py:764
  439.0 24.5 %collective-permute-start.27 = (bf16[512,768]{1,0:T(8,128)(2,1)S(1)}, bf16[512,768]{1,0:T(8,128)(2,1)S(1)}, u32[]{:S(2)}, u32[]{:S(2)}) collective-permute-start(bf16[512,768]{1,0:T(8,128)(2,1)S(1)} %weight_grad.15), channel_id=1, source_target_pairs={{0,4},{1,5},{2,6},{3,7},{4,0},{5,1},{6,2},{7,3},{8,12},{9,13},{10,... | collective-permute-start | bytes 2359304 | tf_op jit(solution)/shard_map/ppermute | solution.py:764
  445.8 7.4 %collective-permute-start.18 = (bf16[4,32,768]{2,1,0:T(8,128)(2,1)S(1)}, bf16[4,32,768]{2,1,0:T(8,128)(2,1)S(1)}, u32[]{:S(2)}, u32[]{:S(2)}) collective-permute-start(bf16[4,32,768]{2,1,0:T(8,128)(2,1)S(1)} %dynamic-slice_bitcast_fusion.33), channel_id=1, source_target_pairs={{0,16},{1,17},{2,18},{3,19},{4,20},{5,21},{6,22},{7,23},{8,24},{9,... | collective-permute-start | bytes 589832 | tf_op jit(solution)/shard_map/ppermute | solution.py:764
  452.8 5.7 collective-permute-start.23
  453.3 6.3 collective-permute-start.19
  453.4 6.3 collective-permute-start.20
  458.5 4.1 collective-permute-start.21
  459.6 30.9 %collective-permute-start.13 = (bf16[864,768]{1,0:T(8,128)(2,1)}, bf16[864,768]{1,0:T(8,128)(2,1)}, u32[]{:S(2)}, u32[]{:S(2)}) collective-permute-start(bf16[864,768]{1,0:T(8,128)(2,1)} %dynamic-slice_bitcast_fusion.3), channel_id=1, source_target_pairs={{0,4},{1,5},{2,6},{3,7},{4,0},{5,1},{6,2},{7,3},{8,12},{9,13},{10,... | collective-permute-start | bytes 3981320 | tf_op jit(solution)/shard_map/ppermute | solution.py:764
  459.6 6.4 collective-permute-start.24
  462.6 5.6 collective-permute-start.25
  463.5 4.8 collective-permute-start.26
  466.1 89.7 %collective-permute-start.55 = (bf16[2,4,128,1024]{3,2,1,0:T(8,128)(2,1)}, bf16[2,4,128,1024]{3,2,1,0:T(8,128)(2,1)}, u32[]{:S(2)}, u32[]{:S(2)}) collective-permute-start(bf16[2,4,128,1024]{3,2,1,0:T(8,128)(2,1)} %dynamic-slice_bitcast_fusion), channel_id=1, source_target_pairs={{0,8},{1,9},{2,10},{3,11},{4,12},{5,13},{6,14},{7,15},{8,0},{9,1},... | collective-permute-start | bytes 6291464 | tf_op jit(solution)/shard_map/ppermute | solution.py:764
  468.2 25.3 %collective-permute-start.14 = (bf16[864,768]{1,0:T(8,128)(2,1)}, bf16[864,768]{1,0:T(8,128)(2,1)}, u32[]{:S(2)}, u32[]{:S(2)}) collective-permute-start(bf16[864,768]{1,0:T(8,128)(2,1)} %dynamic-slice_bitcast_fusion.2), channel_id=1, source_target_pairs={{0,4},{1,5},{2,6},{3,7},{4,0},{5,1},{6,2},{7,3},{8,12},{9,13},{10,... | collective-permute-start | bytes 3981320 | tf_op jit(solution)/shard_map/ppermute | solution.py:764
  468.3 12.2 %collective-permute-start.28 = (bf16[2,4,32,768]{3,2,1,0:T(8,128)(2,1)}, bf16[2,4,32,768]{3,2,1,0:T(8,128)(2,1)}, u32[]{:S(2)}, u32[]{:S(2)}) collective-permute-start(bf16[2,4,32,768]{3,2,1,0:T(8,128)(2,1)} %dynamic-slice_bitcast_fusion.20), channel_id=1, source_target_pairs={{0,16},{1,17},{2,18},{3,19},{4,20},{5,21},{6,22},{7,23},{8,24},{9,... | collective-permute-start | bytes 1179656 | tf_op jit(solution)/shard_map/ppermute | solution.py:764
  469.2 19.6 %collective-permute-start.34 = (bf16[2,4,32,768]{3,2,1,0:T(8,128)(2,1)S(1)}, bf16[2,4,32,768]{3,2,1,0:T(8,128)(2,1)S(1)}, u32[]{:S(2)}, u32[]{:S(2)}) collective-permute-start(bf16[2,4,32,768]{3,2,1,0:T(8,128)(2,1)S(1)} %dynamic-slice_bitcast_fusion.19), channel_id=1, source_target_pairs={{0,16},{1,17},{2,18},{3,19},{4,20},{5,21},{6,22},{7,23},{8,24},{9,... | collective-permute-start | bytes 1179656 | tf_op jit(solution)/shard_map/ppermute | solution.py:764
  480.6 78.8 %collective-permute-start.50 = (bf16[2,4,32,4096]{3,2,1,0:T(8,128)(2,1)}, bf16[2,4,32,4096]{3,2,1,0:T(8,128)(2,1)}, u32[]{:S(2)}, u32[]{:S(2)}) collective-permute-start(bf16[2,4,32,4096]{3,2,1,0:T(8,128)(2,1)} %dynamic-slice_bitcast_fusion.1), channel_id=1, source_target_pairs={{0,16},{1,17},{2,18},{3,19},{4,20},{5,21},{6,22},{7,23},{8,24},{9,... | collective-permute-start | bytes 6291464 | tf_op jit(solution)/shard_map/ppermute | solution.py:764
  488.9 35.2 %collective-permute-start.29 = (bf16[4,32,768]{2,1,0:T(8,128)(2,1)S(1)}, bf16[4,32,768]{2,1,0:T(8,128)(2,1)}, u32[]{:S(2)}, u32[]{:S(2)}) collective-permute-start(bf16[4,32,768]{2,1,0:T(8,128)(2,1)S(1)} %dynamic-slice_bitcast_fusion.31), channel_id=1, source_target_pairs={{0,8},{1,9},{2,10},{3,11},{4,12},{5,13},{6,14},{7,15},{8,0},{9,1},... | collective-permute-start | bytes 589832 | tf_op jit(solution)/shard_map/ppermute | solution.py:764
  497.8 1.3 collective-permute-start.39
  497.9 27.2 %collective-permute-start.35 = (bf16[4,32,768]{2,1,0:T(8,128)(2,1)S(1)}, bf16[4,32,768]{2,1,0:T(8,128)(2,1)S(1)}, u32[]{:S(2)}, u32[]{:S(2)}) collective-permute-start(bf16[4,32,768]{2,1,0:T(8,128)(2,1)S(1)} %dynamic-slice_bitcast_fusion.30), channel_id=1, source_target_pairs={{0,8},{1,9},{2,10},{3,11},{4,12},{5,13},{6,14},{7,15},{8,0},{9,1},... | collective-permute-start | bytes 589832 | tf_op jit(solution)/shard_map/ppermute | solution.py:764
  499.2 23.5 %collective-permute-start.40 = (f32[2,4,32,14]{2,1,3,0:T(4,128)S(1)}, f32[2,4,32,14]{2,1,3,0:T(4,128)S(1)}, u32[]{:S(2)}, u32[]{:S(2)}) collective-permute-start(f32[2,4,32,14]{2,1,3,0:T(4,128)S(1)} %bitcast.347), channel_id=1, source_target_pairs={{0,8},{1,9},{2,10},{3,11},{4,12},{5,13},{6,14},{7,15},{8,0},{9,1},... | collective-permute-start | bytes 43016 | tf_op jit(solution)/shard_map/ppermute | solution.py:764
  522.8 11.2 %collective-permute-start.41 = (f32[4,32,14]{1,0,2:T(4,128)S(1)}, f32[4,32,14]{1,0,2:T(4,128)S(1)}, u32[]{:S(2)}, u32[]{:S(2)}) collective-permute-start(f32[4,32,14]{1,0,2:T(4,128)S(1)} %dynamic-slice_bitcast_fusion.49), channel_id=1, source_target_pairs={{0,16},{1,17},{2,18},{3,19},{4,20},{5,21},{6,22},{7,23},{8,24},{9,... | collective-permute-start | bytes 21512 | tf_op jit(solution)/shard_map/ppermute | solution.py:764
  534.0 5.5 collective-permute-start.42
  534.1 5.4 collective-permute-start.43
  536.4 4.6 collective-permute-start.44
  539.5 6.0 collective-permute-start.30
  539.5 14.2 %collective-permute-start.31 = (bf16[32,768]{1,0:T(8,128)(2,1)S(1)}, bf16[32,768]{1,0:T(8,128)(2,1)S(1)}, u32[]{:S(2)}, u32[]{:S(2)}) collective-permute-start(bf16[32,768]{1,0:T(8,128)(2,1)S(1)} %get-tuple-element.134), channel_id=1, source_target_pairs={{0,2},{1,3},{2,0},{3,1},{4,6},{5,7},{6,4},{7,5},{8,10},{9,11},{10,... | collective-permute-start | bytes 147464 | tf_op jit(solution)/shard_map/ppermute | solution.py:764
  541.0 12.8 %collective-permute-start.32 = (bf16[32,768]{1,0:T(8,128)(2,1)S(1)}, bf16[32,768]{1,0:T(8,128)(2,1)S(1)}, u32[]{:S(2)}, u32[]{:S(2)}) collective-permute-start(bf16[32,768]{1,0:T(8,128)(2,1)S(1)} %get-tuple-element.133), channel_id=1, source_target_pairs={{0,3},{1,0},{2,1},{3,2},{4,7},{5,4},{6,5},{7,6},{8,11},{9,8},{10,9... | collective-permute-start | bytes 147464 | tf_op jit(solution)/shard_map/ppermute | solution.py:764
  545.5 50.1 %collective-permute-start.15 = (bf16[432,1024]{1,0:T(8,128)(2,1)}, bf16[432,1024]{1,0:T(8,128)(2,1)}, u32[]{:S(2)}, u32[]{:S(2)}) collective-permute-start(bf16[432,1024]{1,0:T(8,128)(2,1)} %get-tuple-element.99), channel_id=1, source_target_pairs={{0,0},{1,1},{2,4},{3,5},{4,2},{5,3},{6,6},{7,7},{8,8},{9,9},{10,12... | collective-permute-start | bytes 2654216 | tf_op jit(solution)/shard_map/ppermute | solution.py:764
  553.7 41.9 %collective-permute-start.16 = (bf16[432,1024]{1,0:T(8,128)(2,1)}, bf16[432,1024]{1,0:T(8,128)(2,1)}, u32[]{:S(2)}, u32[]{:S(2)}) collective-permute-start(bf16[432,1024]{1,0:T(8,128)(2,1)} %get-tuple-element.100), channel_id=1, source_target_pairs={{0,1},{1,0},{2,5},{3,4},{4,3},{5,2},{6,7},{7,6},{8,9},{9,8},{10,13... | collective-permute-start | bytes 2654216 | tf_op jit(solution)/shard_map/ppermute | solution.py:764
  553.7 25.8 %collective-permute-start.36 = (bf16[32,768]{1,0:T(8,128)(2,1)S(1)}, bf16[32,768]{1,0:T(8,128)(2,1)S(1)}, u32[]{:S(2)}, u32[]{:S(2)}) collective-permute-start(bf16[32,768]{1,0:T(8,128)(2,1)S(1)} %get-tuple-element.135), channel_id=1, source_target_pairs={{0,1},{1,2},{2,3},{3,0},{4,5},{5,6},{6,7},{7,4},{8,9},{9,10},{10,1... | collective-permute-start | bytes 147464 | tf_op jit(solution)/shard_map/ppermute | solution.py:764
  555.8 34.7 %collective-permute-start.37 = (bf16[32,768]{1,0:T(8,128)(2,1)S(1)}, bf16[32,768]{1,0:T(8,128)(2,1)S(1)}, u32[]{:S(2)}, u32[]{:S(2)}) collective-permute-start(bf16[32,768]{1,0:T(8,128)(2,1)S(1)} %get-tuple-element.137), channel_id=1, source_target_pairs={{0,2},{1,3},{2,0},{3,1},{4,6},{5,7},{6,4},{7,5},{8,10},{9,11},{10,... | collective-permute-start | bytes 147464 | tf_op jit(solution)/shard_map/ppermute | solution.py:764
  559.3 32.6 %collective-permute-start.38 = (bf16[32,768]{1,0:T(8,128)(2,1)S(1)}, bf16[32,768]{1,0:T(8,128)(2,1)S(1)}, u32[]{:S(2)}, u32[]{:S(2)}) collective-permute-start(bf16[32,768]{1,0:T(8,128)(2,1)S(1)} %get-tuple-element.136), channel_id=1, source_target_pairs={{0,3},{1,0},{2,1},{3,2},{4,7},{5,4},{6,5},{7,6},{8,11},{9,8},{10,9... | collective-permute-start | bytes 147464 | tf_op jit(solution)/shard_map/ppermute | solution.py:764
  579.5 25.9 %collective-permute-start.56 = (bf16[4,128,1024]{2,1,0:T(8,128)(2,1)}, bf16[4,128,1024]{2,1,0:T(8,128)(2,1)}, u32[]{:S(2)}, u32[]{:S(2)}) collective-permute-start(bf16[4,128,1024]{2,1,0:T(8,128)(2,1)} %dynamic-slice_bitcast_fusion.4), channel_id=1, source_target_pairs={{0,16},{1,17},{2,18},{3,19},{4,20},{5,21},{6,22},{7,23},{8,24},{9,... | collective-permute-start | bytes 3145736 | tf_op jit(solution)/shard_map/ppermute | solution.py:764
  590.5 20.4 %collective-permute-start.51 = (bf16[4,32,4096]{2,1,0:T(8,128)(2,1)S(1)}, bf16[4,32,4096]{2,1,0:T(8,128)(2,1)}, u32[]{:S(2)}, u32[]{:S(2)}) collective-permute-start(bf16[4,32,4096]{2,1,0:T(8,128)(2,1)S(1)} %dynamic-slice_bitcast_fusion.5), channel_id=1, source_target_pairs={{0,8},{1,9},{2,10},{3,11},{4,12},{5,13},{6,14},{7,15},{8,0},{9,1},... | collective-permute-start | bytes 3145736 | tf_op jit(solution)/shard_map/ppermute | solution.py:764
  607.1 11.2 %collective-permute-start.57 = (bf16[128,1024]{1,0:T(8,128)(2,1)S(1)}, bf16[128,1024]{1,0:T(8,128)(2,1)S(1)}, u32[]{:S(2)}, u32[]{:S(2)}) collective-permute-start(bf16[128,1024]{1,0:T(8,128)(2,1)S(1)} %get-tuple-element.113), channel_id=1, source_target_pairs={{0,1},{1,2},{2,3},{3,0},{4,5},{5,6},{6,7},{7,4},{8,9},{9,10},{10,1... | collective-permute-start | bytes 786440 | tf_op jit(solution)/shard_map/ppermute | solution.py:764
  607.1 31.2 %collective-permute-start.58 = (bf16[128,1024]{1,0:T(8,128)(2,1)S(1)}, bf16[128,1024]{1,0:T(8,128)(2,1)S(1)}, u32[]{:S(2)}, u32[]{:S(2)}) collective-permute-start(bf16[128,1024]{1,0:T(8,128)(2,1)S(1)} %get-tuple-element.115), channel_id=1, source_target_pairs={{0,2},{1,3},{2,0},{3,1},{4,6},{5,7},{6,4},{7,5},{8,10},{9,11},{10,... | collective-permute-start | bytes 786440 | tf_op jit(solution)/shard_map/ppermute | solution.py:764
  607.6 30.8 %collective-permute-start.59 = (bf16[128,1024]{1,0:T(8,128)(2,1)S(1)}, bf16[128,1024]{1,0:T(8,128)(2,1)S(1)}, u32[]{:S(2)}, u32[]{:S(2)}) collective-permute-start(bf16[128,1024]{1,0:T(8,128)(2,1)S(1)} %get-tuple-element.114), channel_id=1, source_target_pairs={{0,3},{1,0},{2,1},{3,2},{4,7},{5,4},{6,5},{7,6},{8,11},{9,8},{10,9... | collective-permute-start | bytes 786440 | tf_op jit(solution)/shard_map/ppermute | solution.py:764
  612.5 26.8 %collective-permute-start.52 = (bf16[32,4096]{1,0:T(8,128)(2,1)S(1)}, bf16[32,4096]{1,0:T(8,128)(2,1)S(1)}, u32[]{:S(2)}, u32[]{:S(2)}) collective-permute-start(bf16[32,4096]{1,0:T(8,128)(2,1)S(1)} %get-tuple-element.116), channel_id=1, source_target_pairs={{0,1},{1,2},{2,3},{3,0},{4,5},{5,6},{6,7},{7,4},{8,9},{9,10},{10,1... | collective-permute-start | bytes 786440 | tf_op jit(solution)/shard_map/ppermute | solution.py:764
  613.1 37.6 %collective-permute-start.53 = (bf16[32,4096]{1,0:T(8,128)(2,1)S(1)}, bf16[32,4096]{1,0:T(8,128)(2,1)S(1)}, u32[]{:S(2)}, u32[]{:S(2)}) collective-permute-start(bf16[32,4096]{1,0:T(8,128)(2,1)S(1)} %get-tuple-element.118), channel_id=1, source_target_pairs={{0,2},{1,3},{2,0},{3,1},{4,6},{5,7},{6,4},{7,5},{8,10},{9,11},{10,... | collective-permute-start | bytes 786440 | tf_op jit(solution)/shard_map/ppermute | solution.py:764
  618.2 32.5 %collective-permute-start.54 = (bf16[32,4096]{1,0:T(8,128)(2,1)S(1)}, bf16[32,4096]{1,0:T(8,128)(2,1)S(1)}, u32[]{:S(2)}, u32[]{:S(2)}) collective-permute-start(bf16[32,4096]{1,0:T(8,128)(2,1)S(1)} %get-tuple-element.117), channel_id=1, source_target_pairs={{0,3},{1,0},{2,1},{3,2},{4,7},{5,4},{6,5},{7,6},{8,11},{9,8},{10,9... | collective-permute-start | bytes 786440 | tf_op jit(solution)/shard_map/ppermute | solution.py:764
  (46 other events, 268.0 us)

commit v3 on v2

--- a/solution.py
+++ b/solution.py
@@ -16,6 +16,7 @@
 BF=jnp.bfloat16; F32=jnp.float32
 NT=(((1,),(1,)),((),())); NN=(((1,),(0,)),((),())); TN=(((0,),(0,)),((),()))
 def dot(a,b,d): return lax.dot_general(a,b,d,preferred_element_type=F32)
+PHASE=1
 FILLED=1664; PAD=64
 def lanes(rows):
     return lax.broadcasted_iota(jnp.int32,(rows,128),1)
@@ -33,54 +34,83 @@
     f=base.astype(F32)
     f=jnp.where((lane>=o)&(lane<o+64),jnp.where(lane<o+n,1.0,0.0),f)
     return f.astype(BF)
-def fwd_tile(q,k,vs,lane,keep):
-    outs=[];augs=[]
-    for h in (0,1):
-        qh=jnp.where((lane//64)==h,q.astype(F32),0.0).astype(BF)
-        s=dot(qh,k,NT)
-        if keep is not None: s=jnp.where(keep,s,-1e30)
-        m=jnp.max(s,axis=1,keepdims=True)
-        p=jnp.exp2(s-m).astype(BF)
-        o=dot(p,vs[h],NN)
-        l=o[:,(1-h)*64:(1-h)*64+1]
-        outs.append(o/l)
-        augs.append(augment(q,h,-(m+jnp.log2(l)),lane))
-    return jnp.where(lane<64,outs[0],outs[1]),augs
+def spread(base,h,x,lane):
+    a=x.astype(BF).astype(F32); r=x-a; b=r.astype(BF).astype(F32); c=r-b
+    o=(1-h)*64
+    f=jnp.where(lane==o,a,jnp.where(lane==o+1,b,jnp.where(lane==o+2,c,0.0)))
+    return jnp.where((lane//64)==h,base.astype(F32),f).astype(BF)
+def fwd_tiles(tasks,lane):
+    scores=[]
+    for q,k,vs,keep in tasks:
+        for h in (0,1):
+            qh=jnp.where((lane//64)==h,q.astype(F32),0.0).astype(BF)
+            s=dot(qh,k,NT)
+            scores.append(s if keep is None else jnp.where(keep,s,-1e30))
+    tops=[];outs=[]
+    depth=PHASE
+    n=len(scores)
+    def soft(i):
+        m=jnp.max(scores[i],axis=1,keepdims=True)
+        tops.append(m)
+        return jnp.exp2(scores[i]-m).astype(BF)
+    ps=[]
+    for i in range(n+depth):
+        if i<n: ps.append(soft(i))
+        if i>=depth: outs.append(dot(ps[i-depth],tasks[(i-depth)//2][2][(i-depth)%2],NN))
+    done=[]
+    for t,(q,_,_,_) in enumerate(tasks):
+        os=[];augs=[]
+        for h in (0,1):
+            o=outs[2*t+h]
+            os.append(o/pltpu.roll(o,64,1))
+            augs.append(spread(q,h,-(tops[2*t+h]+jnp.log2(o)),lane))
+        done.append((jnp.where(lane<64,os[0],os[1]),augs))
+    return done
 def fwd_store(refs,rows,o,augs):
     o_ref,ol_ref,qa_ref=refs
     o_ref[rows,:]=o.astype(BF)
     ol_ref[rows,:]=(o-o.astype(BF).astype(F32)).astype(BF)
     for h in (0,1): qa_ref[h,rows,:]=augs[h]
 def fwd_kernel(bq,info,q_ref,k_ref,v_ref,*refs):
+    *refs,vs_ref=refs
     single=info[0]==1
     @pl.when(single)
     def _():
-        k=k_ref[0:FILLED,:]; v=v_ref[0:FILLED,:]
-        vs=[ones3(v,h,lanes(FILLED),1) for h in (0,1)]
-        for r in range(0,FILLED,bq):
-            n=min(bq,FILLED-r)
-            o,augs=fwd_tile(q_ref[r:r+n,:],k,vs,lanes(n),None)
-            fwd_store(refs,slice(r,r+n),o,augs)
-    @pl.when(jnp.logical_not(single))
+        v=v_ref[0:FILLED,:]
+        for h in (0,1): vs_ref[h,...]=ones3(v,h,lanes(FILLED),64)
+        lq=lanes(bq)
+        @pl.loop(0,FILLED//bq)
+        def _(r):
+            rows=pl.ds(pl.multiple_of(r*bq,bq),bq)
+            (o,augs),=fwd_tiles([(q_ref[rows,:],k_ref[0:FILLED,:],(vs_ref[0],vs_ref[1]),None)],lq)
+            fwd_store(refs,rows,o,augs)
+    @pl.when(info[0]==2)
+    def _():
+        lq=lanes(128)
+        each=[slice(i*128,i*128+128) for i in range(13)]
+        tasks=[(q_ref[r,:],k_ref[r,:],[ones3(v_ref[r,:],h,lq,64) for h in (0,1)],None) for r in each]
+        for r,(o,augs) in zip(each,fwd_tiles(tasks,lq)): fwd_store(refs,r,o,augs)
+    @pl.when(info[0]==0)
     def _():
         col=lax.broadcasted_iota(jnp.int32,(128,512),1)
         lw=lanes(512); lq=lanes(128)
-        for i in range(13):
+        @pl.loop(0,13)
+        def _(i):
             lo=info[1+i]; hi=info[14+i]
             at=jnp.minimum(lo,9)
             window=pl.ds(pl.multiple_of(at*128,128),512)
             k=k_ref[window,:]; v=v_ref[window,:]
-            vs=[ones3(v,h,lw,1) for h in (0,1)]
+            vs=[ones3(v,h,lw,64) for h in (0,1)]
             keep=(col>=(lo-at)*128)&(col<(hi-at)*128)
-            rows=slice(i*128,i*128+128)
-            o,augs=fwd_tile(q_ref[rows,:],k,vs,lq,keep)
+            rows=pl.ds(pl.multiple_of(i*128,128),128)
+            (o,augs),=fwd_tiles([(q_ref[rows,:],k,vs,keep)],lq)
             fwd_store(refs,rows,o,augs)
     rows=slice(FILLED,FILLED+PAD)
     lp=lanes(PAD)
     v=v_ref[rows,:]
-    o,augs=fwd_tile(q_ref[rows,:],k_ref[rows,:],[ones3(v,h,lp,1) for h in (0,1)],lp,None)
+    (o,augs),=fwd_tiles([(q_ref[rows,:],k_ref[rows,:],[ones3(v,h,lp,64) for h in (0,1)],None)],lp)
     fwd_store(refs,rows,o,augs)
-def attn_fwd(info,qkv,first,count,bq=832):
+def attn_fwd(info,qkv,first,count,bq=416):
     L,W3=qkv.shape; n=W3//384
     spec=lambda j: pl.BlockSpec((L,128),lambda p,s,j=j:(0,p+first+j*n))
     one=pl.BlockSpec((L,128),lambda p,s:(0,p))
@@ -88,56 +118,84 @@
         out_shape=(jax.ShapeDtypeStruct((L,count*128),BF),)*2+(jax.ShapeDtypeStruct((2*count,L,128),BF),),
         grid_spec=pltpu.PrefetchScalarGridSpec(num_scalar_prefetch=1,grid=(count,),
             in_specs=[spec(0),spec(1),spec(2)],
-            out_specs=(one,one,pl.BlockSpec((2,L,128),lambda p,s:(p,0,0)))),
+            out_specs=(one,one,pl.BlockSpec((2,L,128),lambda p,s:(p,0,0))),
+            scratch_shapes=[pltpu.VMEM((2,FILLED,128),BF)]),
         compiler_params=pltpu.CompilerParams(vmem_limit_bytes=50<<20),name="attn_forward",
         cost_estimate=pl.CostEstimate(flops=8*count*L*L*256,bytes_accessed=10*L*count*128,transcendentals=2*count*L*L))(info,qkv,qkv,qkv)
 def deltas(g,o,ol,lane):
     prod=g.astype(F32)*(o.astype(F32)+ol.astype(F32))
     return [augment(g,h,-jnp.sum(jnp.where((lane//64)==h,prod,0.0),axis=1,keepdims=True),lane) for h in (0,1)]
-def bwd_tile(qa,k,v,ga,h,lane,keep):
-    kh=ones3(k,h,lane); vh=ones3(v,h,lane)
-    p=jnp.exp2(dot(kh,qa,NT))
-    d=dot(vh,ga,NT)
-    if keep is not None: p=jnp.where(keep,p,0.0)
-    ds=(p*d).astype(BF)
-    return dot(ds,kh,TN),dot(ds,qa,NN),dot(p.astype(BF),ga,NN)
+def bwd_tiles(tasks,lane):
+    khs=[ones3(t[1],t[4],lane) for t in tasks]
+    ps=[dot(kh,t[0],NT) for kh,t in zip(khs,tasks)]
+    ds=[dot(ones3(t[2],t[4],lane),t[3],NT) for t in tasks]
+    done=[]
+    for kh,p,d,(qa,_,_,ga,h,keep) in zip(khs,ps,ds,tasks):
+        p=jnp.exp2(p)
+        if keep is not None: p=jnp.where(keep,p,0.0)
+        d=(p*d).astype(BF)
+        done.append((kh,p.astype(BF),d,qa,ga))
+    return [(dot(d,kh,TN),dot(d,qa,NN),dot(p,ga,NN)) for kh,p,d,qa,ga in done]
 LN2=0.6931471805599453
 def both(a,lane): return jnp.where(lane<64,a[0],a[1])
-def bwd_kernel(bk,info,qa_ref,k_ref,v_ref,o_ref,ol_ref,g_ref,dq_ref,dk_ref,dv_ref,sum_ref,acc,acc_k,acc_v):
+def bwd_alone(each,lane,qa_ref,k_ref,v_ref,o_ref,ol_ref,g_ref,dq_ref,dk_ref,dv_ref):
+    tasks=[]
+    for r in each:
+        gas=deltas(g_ref[r,:],o_ref[r,:],ol_ref[r,:],lane)
+        tasks+=[(qa_ref[h,r,:],k_ref[r,:],v_ref[r,:],gas[h],h,None) for h in (0,1)]
+    got=bwd_tiles(tasks,lane)
+    for i,r in enumerate(each):
+        x,y=got[2*i],got[2*i+1]
+        dq_ref[r,:]=(both((x[0],y[0]),lane)*0.125).astype(BF)
+        dk_ref[r,:]=(both((x[1],y[1]),lane)*LN2).astype(BF)
+        dv_ref[r,:]=both((x[2],y[2]),lane).astype(BF)
+def bwd_kernel(bk,joined,info,qa_ref,k_ref,v_ref,o_ref,ol_ref,g_ref,*rest):
+    d_ref,sum_ref,acc,acc_k,acc_v,ga_ref=rest[1:] if joined else rest
+    dq_ref,dk_ref,dv_ref=d_ref.at[0],d_ref.at[1],d_ref.at[2]
+    tile_refs=(qa_ref,k_ref,v_ref,o_ref,ol_ref,g_ref,dq_ref,dk_ref,dv_ref)
     single=info[0]==1
     @pl.when(single)
     def _():
         lf=lanes(FILLED)
         gas=deltas(g_ref[0:FILLED,:],o_ref[0:FILLED,:],ol_ref[0:FILLED,:],lf)
-        for r in range(0,FILLED,bk):
-            n=min(bk,FILLED-r)
-            rows=slice(r,r+n); lb=lanes(n)
+        acc[...]=jnp.zeros_like(acc)
+        lb=lanes(bk)
+        ga_ref[0,...]=gas[0]; ga_ref[1,...]=gas[1]
+        @pl.loop(0,FILLED//bk)
+        def _(r):
+            rows=pl.ds(pl.multiple_of(r*bk,bk),bk)
             k=k_ref[rows,:]; v=v_ref[rows,:]
             dks=[];dvs=[]
+            got=bwd_tiles([(qa_ref[h,0:FILLED,:],k,v,ga_ref[h],h,None) for h in (0,1)],lb)
             for h in (0,1):
-                dq,dk,dv=bwd_tile(qa_ref[h,0:FILLED,:],k,v,gas[h],h,lb,None)
-                if r==0: acc[h,0:FILLED,:]=dq
-                else: acc[h,0:FILLED,:]+=dq
+                dq,dk,dv=got[h]
+                acc[h,0:FILLED,:]+=dq
                 dks.append(dk); dvs.append(dv)
             dk_ref[rows,:]=(both(dks,lb)*LN2).astype(BF)
             dv_ref[rows,:]=both(dvs,lb).astype(BF)
         dq_ref[0:FILLED,:]=(jnp.where(lf<64,acc[0,0:FILLED,:],acc[1,0:FILLED,:])*0.125).astype(BF)
-    @pl.when(jnp.logical_not(single))
+    @pl.when(info[0]==2)
+    def _():
+        lq=lanes(128)
+        bwd_alone([slice(i*128,i*128+128) for i in range(13)],lq,*tile_refs)
+    @pl.when(info[0]==0)
     def _():
         row=lax.broadcasted_iota(jnp.int32,(512,128),0)
         lw=lanes(512); lq=lanes(128)
         acc_k[...]=jnp.zeros_like(acc_k); acc_v[...]=jnp.zeros_like(acc_v)
-        for i in range(13):
+        @pl.loop(0,13)
+        def _(i):
             lo=info[1+i]; hi=info[14+i]
             at=jnp.minimum(lo,9)
             window=pl.ds(pl.multiple_of(at*128,128),512)
             k=k_ref[window,:]; v=v_ref[window,:]
             keep=(row>=(lo-at)*128)&(row<(hi-at)*128)
-            rows=slice(i*128,i*128+128)
+            rows=pl.ds(pl.multiple_of(i*128,128),128)
             gas=deltas(g_ref[rows,:],o_ref[rows,:],ol_ref[rows,:],lq)
             dqs=[]
+            got=bwd_tiles([(qa_ref[h,rows,:],k,v,gas[h],h,keep) for h in (0,1)],lw)
             for h in (0,1):
-                dq,dk,dv=bwd_tile(qa_ref[h,rows,:],k,v,gas[h],h,lw,keep)
+                dq,dk,dv=got[h]
                 dqs.append(dq)
                 acc_k[h,window,:]+=dk
                 acc_v[h,window,:]+=dv
@@ -145,29 +203,24 @@
         lf=lanes(FILLED)
         dk_ref[0:FILLED,:]=(jnp.where(lf<64,acc_k[0],acc_k[1])*LN2).astype(BF)
         dv_ref[0:FILLED,:]=jnp.where(lf<64,acc_v[0],acc_v[1]).astype(BF)
-    rows=slice(FILLED,FILLED+PAD)
-    lp=lanes(PAD)
-    gas=deltas(g_ref[rows,:],o_ref[rows,:],ol_ref[rows,:],lp)
-    t=[bwd_tile(qa_ref[h,rows,:],k_ref[rows,:],v_ref[rows,:],gas[h],h,lp,None) for h in (0,1)]
-    dq_ref[rows,:]=(both([a[0] for a in t],lp)*0.125).astype(BF)
-    dk_ref[rows,:]=(both([a[1] for a in t],lp)*LN2).astype(BF)
-    dv_ref[rows,:]=both([a[2] for a in t],lp).astype(BF)
+    bwd_alone([slice(FILLED,FILLED+PAD)],lanes(PAD),*tile_refs)
     sum_ref[0:1,:]=jnp.sum(dq_ref[...].astype(F32),axis=0,keepdims=True)
     sum_ref[1:2,:]=jnp.sum(dv_ref[...].astype(F32),axis=0,keepdims=True)
-def attn_bwd(info,qa,qkv,o,ol,g,first,count,inner,bk=832):
+def attn_bwd(info,qa,qkv,o,ol,g,first,count,inner,wide,at,into=None,bk=416):
     L,W3=qkv.shape; n=W3//384
     spec=lambda j: pl.BlockSpec((L,128),lambda p,s,j=j:(0,p+first+j*n))
     one=pl.BlockSpec((L,128),lambda p,s:(0,p))
     part=pl.BlockSpec((L,128),lambda p,s:(0,p+inner))
     every=pl.BlockSpec((L,128),lambda p,s:(0,p+first))
-    return pl.pallas_call(functools.partial(bwd_kernel,bk),
-        out_shape=(jax.ShapeDtypeStruct((L,count*128),BF),)*3+(jax.ShapeDtypeStruct((2,count*128),F32),),
+    return pl.pallas_call(functools.partial(bwd_kernel,bk,into is not None),
+        input_output_aliases={} if into is None else {7:0},
+        out_shape=(jax.ShapeDtypeStruct((3,L,wide*128),BF),jax.ShapeDtypeStruct((2,count*128),F32)),
         grid_spec=pltpu.PrefetchScalarGridSpec(num_scalar_prefetch=1,grid=(count,),
-            in_specs=[pl.BlockSpec((2,L,128),lambda p,s:(p+inner,0,0)),spec(1),spec(2),part,part,every],
-            out_specs=(one,one,one,pl.BlockSpec((2,128),lambda p,s:(0,p))),
-            scratch_shapes=[pltpu.VMEM((2,FILLED,128),F32)]*3),
+            in_specs=[pl.BlockSpec((2,L,128),lambda p,s:(p+inner,0,0)),spec(1),spec(2),part,part,every]+([] if into is None else [pl.BlockSpec(memory_space=pl.ANY)]),
+            out_specs=(pl.BlockSpec((3,L,128),lambda p,s:(0,0,p+at)),pl.BlockSpec((2,128),lambda p,s:(0,p))),
+            scratch_shapes=[pltpu.VMEM((2,FILLED,128),F32)]*3+[pltpu.VMEM((2,FILLED,128),BF)]),
         compiler_params=pltpu.CompilerParams(vmem_limit_bytes=56<<20),name="attn_backward",
-        cost_estimate=pl.CostEstimate(flops=20*count*L*L*256,bytes_accessed=16*L*count*128,transcendentals=2*count*L*L))(info,qa,qkv,qkv,o,ol,g)
+        cost_estimate=pl.CostEstimate(flops=20*count*L*L*256,bytes_accessed=16*L*count*128,transcendentals=2*count*L*L))(*((info,qa,qkv,qkv,o,ol,g) if into is None else (info,qa,qkv,qkv,o,ol,g,into)))
 
 
 def gelu_exact(values):
@@ -490,7 +543,6 @@
     )
 
 
-GROUPS = 2
 SLOPE = F32
 LOG2E = 1.4426950408889634
 
@@ -690,7 +742,8 @@
     rhs_ref = refs[1 + count]
     out_ref = refs[-1]
     left = lhs[0] if count == 1 else jnp.concatenate(lhs, axis=1)
-    total = dot(left, rhs_ref[...], TN)
+    right = rhs_ref[0] if len(rhs_ref.shape) == 3 else rhs_ref[...]
+    total = dot(left, right, TN)
     if extra:
         total = total + refs[2 + count][...].astype(F32)
     out_ref[...] = total.astype(BF)
@@ -698,7 +751,9 @@
 
 def weight_grad(sel, lhs, rhs, add=None, cols=1024, quads=4, pairs=2):
     depth, width = lhs.shape
-    n = rhs.shape[1]
+    three = rhs.ndim == 3
+    n = rhs.shape[0] * rhs.shape[2] if three else rhs.shape[1]
+    cols = rhs.shape[2] if three else cols
     w = width // (quads * pairs)
     extra = add is not None
     if w >= 512:
@@ -713,7 +768,11 @@
         grid, count = (n // cols,), quads
         ins = [
             pl.BlockSpec((depth, w), lambda i, s, q=q: (0, pairs * q + s[0])) for q in range(quads)
-        ] + [pl.BlockSpec((depth, cols), lambda i, s: (0, i))]
+        ] + [
+            pl.BlockSpec((1, depth, cols), lambda i, s: (i, 0, 0))
+            if three
+            else pl.BlockSpec((depth, cols), lambda i, s: (0, i))
+        ]
         out = pl.BlockSpec((quads * w, cols), lambda i, s: (0, i))
         args = [lhs] * quads + [rhs]
     if extra:
@@ -736,6 +795,59 @@
     )(sel, *args)
 
 
+def finish_kernel(sel_ref, base_ref, mine_ref, got_ref, w_mine_ref, w_got_ref, out_ref, *rest):
+    n = mine_ref.shape[2]
+    total = base_ref[...]
+    for t in range(3):
+        total = total + dot(mine_ref[t], w_mine_ref[:, t * n : (t + 1) * n], NT)
+        total = total + dot(got_ref[t], w_got_ref[:, t * n : (t + 1) * n], NT)
+    out_ref[...] = total.astype(out_ref.dtype)
+    if rest:
+        step = pl.program_id(0)
+
+        @pl.when(step == 0)
+        def _():
+            rest[0][...] = jnp.zeros_like(rest[0])
+
+        rest[0][...] += jnp.sum(total, axis=0, keepdims=True)
+
+
+def add_start(core, base, grads, got, w_mine, w_got, last, br=288):
+    rows, model = base.shape
+    n = got.shape[2]
+    steps = rows // br
+    fixed = lambda w: pl.BlockSpec(w.shape, lambda i, s: (0, 0))
+    row = pl.BlockSpec((br, model), lambda i, s: (i, 0))
+    outs = [jax.ShapeDtypeStruct((rows, model), BF if last else F32)]
+    specs = [row]
+    if last:
+        outs.append(jax.ShapeDtypeStruct((1, model), F32))
+        specs.append(pl.BlockSpec((1, model), lambda i, s: (0, 0)))
+    return pl.pallas_call(
+        finish_kernel,
+        out_shape=tuple(outs),
+        grid_spec=pltpu.PrefetchScalarGridSpec(
+            num_scalar_prefetch=1,
+            grid=(steps,),
+            in_specs=[
+                row,
+                pl.BlockSpec((3, br, n), lambda i, s: (0, s[0] * steps + i, 0)),
+                pl.BlockSpec((3, br, n), lambda i, s: (0, i, 0)),
+                fixed(w_mine),
+                fixed(w_got),
+            ],
+            out_specs=tuple(specs),
+        ),
+        compiler_params=pltpu.CompilerParams(vmem_limit_bytes=40 << 20),
+        cost_estimate=pl.CostEstimate(
+            flops=12 * rows * n * model,
+            bytes_accessed=8 * rows * model + 12 * n * (rows + model),
+            transcendentals=0,
+        ),
+        name="add_start",
+    )(core, base, grads, got, w_mine, w_got)
+
+
 class Plan:
     def __init__(self, mesh):
         sizes = dict(mesh.shape)
@@ -753,7 +865,7 @@
                 for c in range(2):
                     for z in range(self.depth):
                         to = target(y, x, c, z)
-                        if to is not None:
+                        if to != (y, x, c, z):
                             pairs.append((self.index(y, x, c, z), self.index(*to)))
         return pairs
 
@@ -771,38 +883,48 @@
     return lax.dynamic_index_in_dim(array, index, axis, keepdims=False)
 
 
-def scatter_sum(plan, terms, order, where):
-    y, x, z = where
-    for axis in order:
-        if axis == "x":
-            if plan.nx == 1:
-                terms = terms[:, 0]
-                continue
-            at = terms.ndim - 4
-            total = pick(terms, x, at).astype(F32)
-            for r in range(1, plan.nx):
-                got = plan.send(
-                    pick(terms, (x + r) % plan.nx, at),
-                    lambda y, x, c, z, r=r: (y, (x + r) % plan.nx, c, z),
-                )
-                total = total + got.astype(F32)
-        else:
-            total = pick(terms, y, 0).astype(F32)
-            for r in range(1, plan.ny):
-                got = plan.send(
-                    pick(terms, (y + r) % plan.ny, 0),
-                    lambda y, x, c, z, r=r: ((y + r) % plan.ny, x, c, z),
-                )
-                total = total + got.astype(F32)
-        terms = total.astype(terms.dtype)
-    total = pick(terms, z, 0).astype(F32)
-    for r in range(1, plan.depth):
-        got = plan.send(
-            pick(terms, (z + r) % plan.depth, 0),
-            lambda y, x, c, z, r=r: (y, x, c, (z + r) % plan.depth),
-        )
-        total = total + got.astype(F32)
-    return total
+def tie(*values):
+    return lax.optimization_barrier(values)
+
+
+class Sum:
+    def __init__(self, plan, terms, where):
+        self.plan, self.terms = plan, terms
+        self.where = dict(zip("yxz", where))
+
+    def send(self, axis):
+        plan, terms = self.plan, self.terms
+        self.axis = axis
+        self.at = terms.ndim - 4 if axis == "x" else 0
+        if axis == "z":
+            self.got = [lax.all_to_all(terms, "seq", 0, 0, tiled=True)]
+            return self
+        size = {"x": plan.nx, "y": plan.ny}[axis]
+        here = self.where[axis]
+        self.got = []
+        for r in range(1, size):
+
+            def target(y, x, c, z, r=r):
+                at = {"y": y, "x": x}
+                at[axis] = (at[axis] + r) % size
+                return at["y"], at["x"], c, z
+
+            self.got.append(plan.send(pick(terms, (here + r) % size, self.at), target))
+        return self
+
+    def add(self):
+        if self.axis == "z":
+            self.terms = jnp.sum(self.got[0].astype(F32), axis=0)
+            return self.terms
+        total = pick(self.terms, self.where[self.axis], self.at).astype(F32)
+        for got in self.got:
+            total = total + got.astype(F32)
+        self.terms = total.astype(self.terms.dtype)
+        return self.terms
+
+    def hold(self, *others):
+        self.terms, *rest = tie(self.terms, *others)
+        return rest
 
 
 def per_chip(
@@ -847,34 +969,40 @@
     marks = mine[:13]
     info = jnp.concatenate(
         [
-            (marks[:1] == marks[12:]).astype(jnp.int32),
+            jnp.where(marks[:1] == marks[12:], 1, jnp.where(marks[12:] == marks[:1] + 12, 2, 0)),
             jnp.sum((marks[None, :] < marks[:, None]).astype(jnp.int32), axis=1),
             jnp.sum((marks[None, :] <= marks[:, None]).astype(jnp.int32), axis=1),
         ]
     )
     fraction = mine[13].astype(F32) / TSTEPS
 
-    def gather_rows(array):
+    stays = z // 2 == c
+
+    def exchange(parts):
         got = [
-            plan.send(
-                pick(array, which((part + j) % 2), 0),
-                lambda y, x, c, z, j=j: (y, x, z // 2, 2 * c + (z + j) % 2),
-            )
-            for j in (0, 1)
+            plan.send(v, lambda y, x, c, z, j=j: (y, x, z // 2, 2 * c + (z + j) % 2))
+            for j, v in enumerate(parts)
         ]
+        return [(got[0], parts[0]), (got[1], None)]
+
+    def arrived(got):
+        return [jnp.where(stays, got[0][1], got[0][0]), got[1][0]]
+
+    def gather_parts(array):
+        return [pick(array, which((part + j) % 2), 0) for j in (0, 1)]
+
+    def gather_end(got):
+        got = arrived(got)
         return jnp.concatenate(
             [jnp.where(part == 0, got[0], got[1]), jnp.where(part == 0, got[1], got[0])], axis=0
         )
 
-    def spread_rows(array):
+    def spread_parts(array):
         array = array.reshape(2, local_len, array.shape[-1])
-        got = [
-            plan.send(
-                pick(array, (part + j) % 2, 0),
-                lambda y, x, c, z, j=j: (y, x, z // 2, 2 * c + (z + j) % 2),
-            )
-            for j in (0, 1)
-        ]
+        return [pick(array, (part + j) % 2, 0) for j in (0, 1)]
+
+    def spread_end(got):
+        got = arrived(got)
         swap = (part + first) % 2
         return jnp.stack(
             [jnp.where(swap == 0, got[0], got[1]), jnp.where(swap == 0, got[1], got[0])], axis=0
@@ -912,32 +1040,33 @@
     )
     w_out_own = halves(w_out, 0)[0]
     w_all = w_own.reshape(model, 3 * half)
-    groups = [range(g * (quads // GROUPS), (g + 1) * (quads // GROUPS)) for g in range(GROUPS)]
+    ahead = [range(0, quads // 2), range(quads // 2, quads)]
+    groups = ahead
     cut = lambda w: [w[:, :, g.start : g.stop].reshape(model, -1) for g in groups]
     w_cut, w_cut_oth = cut(w_own), cut(w_oth)
-    own_inputs = gather_rows(inputs)
-    own_inputs, w_all, w_cut, w_cut_oth, w_out_own = lax.optimization_barrier(
-        (own_inputs, w_all, w_cut, w_cut_oth, w_out_own)
+    own_inputs = gather_end(exchange(gather_parts(inputs)))
+    vecs = jnp.stack(
+        [v.astype(F32) for v in (w_time, b_time, b_out, ln1_gain, ln1_bias, b_down, ln2_gain, ln2_bias)]
+    )
+    cot_parts = gather_parts(cotangent)
+    own_inputs, w_all, w_cut, w_cut_oth, w_out_own, vecs, info, bias, cot_parts = tie(
+        own_inputs, w_all, w_cut, w_cut_oth, w_out_own, vecs, info, bias, cot_parts
     )
     start = (
         own_inputs.astype(F32) + fraction * w_time.astype(F32)[None] + b_time.astype(F32)[None]
     )
     start_low = start.astype(BF)
-    start_sib = plan.sibling(start_low)
-    cotangent, _ = lax.optimization_barrier((cotangent, start_low))
-    own_cotangent = gather_rows(cotangent)
-    start_full = whole(start_low, start_sib)
+    cot_parts, start_low = tie(cot_parts, start_low)
+    own_cotangent = gather_end(exchange(cot_parts))
+    start_full = whole(start_low, plan.sibling(start_low))
     scale = jnp.where(jnp.arange(3 * half) < half, 0.125 * LOG2E, 1.0)
     qkv = ((jnp.dot(start_full, w_all, preferred_element_type=F32) + bias) * scale).astype(BF)
-    fwd = [attn_fwd(info, qkv, g.start, len(g)) for g in groups]
+    fwd = [attn_fwd(info, qkv, g.start, len(g)) for g in ahead]
     mine_of, away_of = [], []
-    for g in range(GROUPS):
+    for g in range(2):
         split = fwd[g][0].reshape(2, rows, -1)
         mine_of.append(pick(split, c, 0))
         away_of.append(plan.sibling(pick(split, 1 - c, 0)))
-    vecs = jnp.stack(
-        [v.astype(F32) for v in (w_time, b_time, b_out, ln1_gain, ln1_bias, b_down, ln2_gain, ln2_bias)]
-    )
     result, normed_low, act, two_low, hid, grad_one, one_low, small_sums, up_sums = middle(
         core,
         fraction[None],
@@ -951,79 +1080,139 @@
         w_up,
         w_down,
     )
-    grad_one_full = whole(one_low, plan.sibling(one_low))
-    down_got = plan.sibling(weight_grad(away, act, two_low, quads=quads))
-    up_got = plan.sibling(weight_grad(away, normed_low, hid, quads=quads))
-    output = spread_rows(result)
+    one_sib = plan.sibling(one_low)
+    output_got = exchange(spread_parts(result))
+    down_part = weight_grad(away, act, two_low, quads=quads)
+    normed_low, down_part = tie(normed_low, down_part)
+    down_got = plan.sibling(down_part)
+    up_part = weight_grad(away, normed_low, hid, quads=quads)
+    act, up_part = tie(act, up_part)
+    up_got = plan.sibling(up_part)
+    down_sum = weight_grad(core, act, two_low, down_got, quads=quads)
+    normed_low, down_sum = tie(normed_low, down_sum)
+    down = Sum(plan, blocks(down_sum), where).send("x")
+    up_sum = weight_grad(core, normed_low, hid, up_got, quads=quads)
+    one_low, one_sib, up_sum = tie(one_low, one_sib, up_sum)
+    up = Sum(plan, blocks(up_sum), where).send("y")
+    grad_one_full = whole(one_low, one_sib)
+    context = jnp.concatenate([f[0] for f in fwd], axis=1)
+    out_sum = weight_grad(0 * core, context, grad_one_full, quads=quads, pairs=1, cols=512)
+    grad_one_full, out_sum = tie(grad_one_full, out_sum)
+    out = Sum(plan, blocks(out_sum), where).send("x")
     grad_context = lax.dot_general(
         grad_one_full, w_out_own, NT, preferred_element_type=F32
     ).astype(BF)
-    down_sum = weight_grad(core, act, two_low, down_got, quads=quads)
-    up_sum = weight_grad(core, normed_low, hid, up_got, quads=quads)
-    grad_context, down_sum, up_sum = lax.optimization_barrier((grad_context, down_sum, up_sum))
-    sum_w_down = scatter_sum(plan, blocks(down_sum), "xy", where)
-    sum_w_up = scatter_sum(plan, blocks(up_sum), "yx", where)
-    context = jnp.concatenate([f[0] for f in fwd], axis=1)
-    out_sum = weight_grad(0 * core, context, grad_one_full, quads=quads, pairs=1, cols=512)
-    sum_w_out = scatter_sum(plan, blocks(out_sum), "yx", where)
-    grad_start = grad_one
-    keeps, crosses, b_sums = [], [], []
-    for g in range(GROUPS):
-        heads = groups[g]
-        dq, dk, dv, b_sum = attn_bwd(
-            info, fwd[g][2], qkv, fwd[g][0], fwd[g][1], grad_context, heads.start, len(heads), 0
+
+    def back(first, count, into=None):
+        f = first // (quads // 2)
+        start = ahead[f].start
+        return attn_bwd(
+            info,
+            fwd[f][2],
+            qkv,
+            fwd[f][0],
+            fwd[f][1],
+            grad_context,
+            first,
+            count,
+            first - start,
+            quads // 2,
+            first - start,
+            into,
         )
-        b_sums.append(b_sum)
-        grad_qkv = jnp.concatenate([dq, dk, dv], axis=1)
-        both_halves = grad_qkv.reshape(2, rows, -1)
-        got = plan.sibling(pick(both_halves, 1 - c, 0))
-        cols = grad_qkv.shape[1]
-        cross = plan.sibling(weight_grad(away, start_full, grad_qkv, quads=quads, cols=cols))
-        keep = weight_grad(core, start_full, grad_qkv, quads=quads, cols=cols)
-        keeps.append(scatter_sum(plan, blocks(keep), "xy", where))
-        crosses.append(scatter_sum(plan, blocks(cross), "yx", where))
-        grad_start = (
-            grad_start
-            + lax.dot_general(pick(both_halves, c, 0), w_cut[g], NT, preferred_element_type=F32)
-            + lax.dot_general(got, w_cut_oth[g], NT, preferred_element_type=F32)
-        )
-        if g + 1 < GROUPS:
-            grad_context, grad_qkv = lax.optimization_barrier((grad_context, grad_qkv))
-    grad_inputs = spread_rows(grad_start.astype(BF))
+
+    def away_rows(grads):
+        return plan.sibling(pick(grads.reshape(3, 2, rows, -1), 1 - c, 1))
+
+    def products(grads):
+        cross_part = weight_grad(away, start_full, grads, quads=quads)
+        grads, cross_part = tie(grads, cross_part)
+        cross = plan.sibling(cross_part)
+        keep = weight_grad(core, start_full, grads, quads=quads)
+        return Sum(plan, blocks(cross), where), Sum(plan, blocks(keep), where)
+
+    def settle(items, other):
+        for item in items:
+            item.got, other = tie(item.got, other)
+            item.add()
+            item.terms, other = tie(item.terms, other)
+        return other
+
+    grads, b_sum0 = back(0, quads // 2)
+    got = away_rows(grads)
+    output_got, grads = tie(output_got, grads)
+    grads = settle([down, up, out], grads)
+    down.send("y")
+    up.send("x")
+    out.send("y")
+    cross0, keep0 = products(grads)
+    got, cross0.terms, keep0.terms = tie(got, cross0.terms, keep0.terms)
+    (grad_start,) = add_start(core, grad_one, grads, got, w_cut[0], w_cut_oth[0], False)
+    keep0.send("x")
+    cross0.send("y")
+    grad_context, grad_start = tie(grad_context, grad_start)
+    grads, b_sum1 = back(quads // 2, quads // 4)
+    grads = settle([down, up], grads)
+    down.send("z")
+    up.send("z")
+    grads, b_sum2 = back(quads // 2 + quads // 4, quads // 4, grads)
+    got = away_rows(grads)
+    cross1, keep1 = products(grads)
+    got, keep1.terms = tie(got, keep1.terms)
+    grad_low, b_time_sum = add_start(core, grad_start, grads, got, w_cut[1], w_cut_oth[1], True)
+    in_parts, b_time_sum = tie(spread_parts(grad_low), b_time_sum)
+    grad_inputs_got = exchange(in_parts)
+    keep1.send("x")
+    cross1.send("y")
+    for item in (out, keep0, cross0, keep1, cross1, down, up):
+        item.got, b_time_sum = tie(item.got, b_time_sum)
+    out.add()
+    keep0.add()
+    cross0.add()
+    keep0.send("y")
+    cross0.send("x")
+    keep1.add()
+    cross1.add()
+    keep1.send("y")
+    cross1.send("x")
+    for item in (keep0, cross0, keep1, cross1):
+        item.add()
+    late = Sum(
+        plan,
+        jnp.concatenate([i.terms for i in (keep0, cross0, keep1, cross1, out)], axis=2),
+        where,
+    ).send("z")
+    small_sums, up_sums, b_time_sum = tie(small_sums, up_sums, b_time_sum)
+    b_sum = jnp.concatenate([b_sum0, b_sum1, b_sum2], axis=1)
+    zero = jnp.zeros((quads, 2, half // quads), F32)
+
+    def placed(v):
+        return lax.dynamic_update_index_in_dim(zero, v.reshape(quads, half // quads), c, 1).reshape(-1)
+
+    vectors = [small_sums[i] for i in range(6)]
+    vectors += [placed(b_sum[0]), placed(b_sum[1]), fraction * b_time_sum[0], b_time_sum[0]]
+    small = jnp.concatenate([v[:, None] for v in vectors] + [up_sums.reshape(model, -1)], axis=1)
+    small_own, small_oth = halves(small, 0)
+    small = Sum(plan, blocks(small_own + plan.sibling(small_oth)), where)
+    for axis in "xyz":
+        small.send(axis).add()
+    small = small.terms
+    late = late.add()
+    wide = 3 * half // 2
+    keeps = [late[:, :wide], late[:, 2 * wide : 3 * wide]]
+    crosses = [late[:, wide : 2 * wide], late[:, 3 * wide : 4 * wide]]
+    sum_w_down, sum_w_up, sum_w_out = down.add(), up.add(), late[:, 4 * wide :]
+    output = spread_end(output_got)
+    grad_inputs = spread_end(grad_inputs_got)
     split3 = lambda parts: jnp.concatenate(
-        [p.reshape(p.shape[0], 3, quads // GROUPS, -1) for p in parts], axis=2
+        [p.reshape(p.shape[0], 3, len(g), -1) for p, g in zip(parts, groups)], axis=2
     )
     sum_own, sum_oth = split3(keeps), split3(crosses)
-    b_sum = jnp.concatenate(b_sums, axis=1)
-    grad_b_query, grad_b_value = b_sum[0], b_sum[1]
     pair = jnp.where(c == 0, jnp.stack([sum_own, sum_oth]), jnp.stack([sum_oth, sum_own]))
     sum_w_qkv = (
         pair.transpose(1, 2, 3, 0, 4).reshape(-1, 3 * model)
     )
-    grad_b_time = jnp.sum(grad_start, axis=0)
-    grad_w_time = fraction * grad_b_time
-    zero = jnp.zeros((quads, 2, half // quads), F32)
-
-    def placed(v):
-        return lax.dynamic_update_index_in_dim(zero, v.reshape(quads, half // quads), c, 1).reshape(-1)
-
-    vectors = [
-        placed(grad_b_query),
-        placed(grad_b_value),
-        small_sums[0],
-        small_sums[1],
-        small_sums[2],
-        small_sums[3],
-        small_sums[4],
-        small_sums[5],
-        grad_w_time,
-        grad_b_time,
-    ]
-    small = jnp.concatenate([v[:, None] for v in vectors] + [up_sums.reshape(model, -1)], axis=1)
-    small_own, small_oth = halves(small, 0)
-    small_own = small_own + plan.sibling(small_oth)
-    small_sum = scatter_sum(plan, blocks(small_own), "xy", where)
-    v = [small_sum[:, i] for i in range(10)]
+    v = [small[:, i] for i in (6, 7, 0, 1, 2, 3, 4, 5, 8, 9)]
     return (
         output,
         grad_inputs,
@@ -1035,7 +1224,7 @@
         v[3],
         v[4],
         sum_w_up,
-        small_sum[:, 10:].reshape(-1),
+        small[:, 10:].reshape(-1),
         sum_w_down,
         v[5],
         v[6],

time: 664 us -> 519 us (0.78)
  waiting for transfers between devices: 159 us -> 44.9 us
  starting transfers between devices: 82.4 us -> 55.8 us
  local copies, waits for them, and re-layouts: 79 us -> 96.1 us
  Pallas kernels: 256 us -> 242 us
  matrix products: 23.8 us -> 11 us
    ppermute x60 -> x36, waiting for transfers between devices: 159 us -> 12.5 us  [send(): return lax.ppermute(value, AXES, self.perm(target))]
    ppermute x60 -> x36, starting transfers between devices: 82.4 us -> 36.7 us  [send(): return lax.ppermute(value, AXES, self.perm(target))]
    all_to_all x0 -> x4, waiting for transfers between devices: none -> 32.3 us  [send(): self.got = [lax.all_to_all(terms, 'seq', 0, 0, tiled=True)]]
    pallas_call x2 -> x5, Pallas kernels: 110 us -> 90.6 us  [the longest x3 82.3 us: attn_bwd(): pl.pallas_call(functools.partial(bwd_kernel, bk, into is not None), input...]
    all_to_all x0 -> x4, starting transfers between devices: none -> 19.2 us  [send(): self.got = [lax.all_to_all(terms, 'seq', 0, 0, tiled=True)]]
    dot_general x4 -> x0, matrix products: 12.8 us -> none  [the longest x2 6.55 us: per_chip(): lax.dot_general(pick(both_halves, c, 0), w_cut[g], NT, preferred_element_...]
    pallas_call x1, Pallas kernels: 54.2 us -> 64 us  [middle(): pl.pallas_call(functools.partial(middle_kernel, fc), out_shape=(out(model...]
    squeeze x30 -> x23, local copies, waits for them, and re-layouts: 15.5 us -> 20.7 us  [pick(): return lax.dynamic_index_in_dim(array, index, axis, keepdims=False)]
  transfers between devices with their start and end apart: 60 -> 40, of which waited for: 23 -> 9; matrix products, arithmetic and copies ran while one was open for 17% -> 25% of each run, Pallas kernels for 11% -> 29%
where the time goes in v3:
time: 519 us; the launch traced here: 508 us
  Pallas kernels  242 us (47%)
  local copies, waits for them, and re-layouts  96.1 us (19%)
  starting transfers between devices  55.8 us (11%)
  other arithmetic  51.3 us (10%)
  waiting for transfers between devices  44.9 us (9%)
  matrix products  11 us (2%)
  between operations  7.03 us (1%)
    pallas_call x3, Pallas kernels, attn_bwd(): pl.pallas_call(functools.partial(bwd_kernel, bk, into is not None), input...  82.3 us
    pallas_call x1, Pallas kernels, middle(): pl.pallas_call(functools.partial(middle_kernel, fc), out_shape=(out(model...  64 us
    pallas_call x9, Pallas kernels, weight_grad(): pl.pallas_call(functools.partial(grad_kernel, count, extra), out_shape=ja...  49.9 us
    pallas_call x2, Pallas kernels, attn_fwd(): pl.pallas_call(functools.partial(fwd_kernel, bq), out_shape=(jax.ShapeDty...  37.8 us
    ppermute x36, starting transfers between devices, send(): return lax.ppermute(value, AXES, self.perm(target))  36.7 us
    all_to_all x4, waiting for transfers between devices, send(): self.got = [lax.all_to_all(terms, 'seq', 0, 0, tiled=True)]  32.3 us
    unnamed x138, local copies, waits for them, and re-layouts  29.6 us
    squeeze x23, local copies, waits for them, and re-layouts, pick(): return lax.dynamic_index_in_dim(array, index, axis, keepdims=False)  20.7 us
  transfers between devices with their start and end apart: 40, of which 9 were waited for; matrix products, arithmetic and copies ran while one was open for 25% of the time, Pallas kernels for 29%

profile of v3, /device:TPU:0, one launch (start us, length us, event | category | flops | bytes accessed | tf_op | source)
XLA Modules:
  0.0 508.3 jit_solution(15805456171500889343)
XLA Ops:
  3.3 2.8 dynamic-slice_bitcast_fusion.13
  7.7 3.0 collective-permute-start.2
  11.8 2.6 collective-permute-start
  14.4 8.6 %copy.140 = bf16[1024,3072]{0,1:T(8,128)(2,1)} copy(bf16[1024,3072]{1,0:T(8,128)(2,1)} %param.23) | data formatting | bytes 12582912 | tf_op args[4]
  23.0 6.6 %constant_dynamic-slice_fusion.5 = (bf16[1024,3,4,1,128]{0,4,3,2,1:T(8,128)(2,1)}, bf16[1024,3,4,1,128]{0,4,3,2,1:T(8,128)(2,1)}) fusion(bf16[1024,3,4,2,128]{0,4,3,2,1:T(8,128)(2,1)} %bitcast.240, s32[]{:T(128)S(6)} %select_n.339, s32[]{:T(128)S(6)} %select_n.338), kind=kLoop, calls=%fused_computation.119 | loop fusion | bytes 12582920 | tf_op jit(solution)/shard_map/jit(dynamic_index_in_dim)/dynamic_slice | solution.py:883
  29.6 3.5 copy.141
  36.9 3.0 copy.143
  39.9 1.7 reshape.246.w_mine_ref
  41.6 4.7 copy.144
  46.2 3.2 fusion.23
  52.7 3.0 copy.146
  55.8 1.9 reshape.248.w_got_ref
  57.8 2.9 dynamic-slice_bitcast_fusion.10
  60.7 2.3 constant_dynamic-slice_fusion.4
  75.4 3.0 maximum_select_fusion.refs_1_.refs_2_.refs_3_.refs_4_
  78.5 1.7 copy-done.24
  80.2 7.7 %multiply_convert_fusion.q_ref.k_ref.v_ref = bf16[1728,1536]{1,0:T(8,128)(2,1)} fusion(bf16[1728,1024]{1,0:T(8,128)(2,1)S(1)} %maximum_select_fusion.refs_1_.refs_2_.refs_3_.refs_4_, bf16[1024,1536]{0,1:T(8,128)(2,1)S(1)} %bitcast.243, f32[1536]{0:T(1024)S(1)} %fusion.20, f32[1536]{0:T(1024)S(1)} %pad_maximum_fusion.7), kind=kOutput, calls=%fused_computation | convolution fusion | flops 5443780608 | bytes 12005376 | tf_op jit(solution)/shard_map/dot_general | solution.py:1063
  87.9 18.9 %attn_forward.2 = (bf16[1728,256]{1,0:T(8,128)(2,1)S(1)}, bf16[1728,256]{1,0:T(8,128)(2,1)S(1)}, bf16[4,1728,128]{2,1,0:T(8,128)(2,1)S(1)}) custom-call(s32[27]{0:T(128)S(1)} %pad_add_fusion.1.info, bf16[1728,1536]{1,0:T(8,128)(2,1)} %multiply_convert_fusion.q_ref.k_ref.v_ref, bf16[1728,1536]{1,0:T(8,128)(2,1)} %multiply_convert_fusion.q_ref.k_ref.v_ref, ...), custom_call_target="tpu_custom_call" | custom-call | flops 12230590464 | bytes 4423680 | tf_op jit(solution)/shard_map/attn_forward/pallas_call | solution.py:117
  109.2 2.2 collective-permute-start.4
  111.5 18.9 %attn_forward.3 = (bf16[1728,256]{1,0:T(8,128)(2,1)S(1)}, bf16[1728,256]{1,0:T(8,128)(2,1)S(1)}, bf16[4,1728,128]{2,1,0:T(8,128)(2,1)S(1)}) custom-call(s32[27]{0:T(128)S(1)} %pad_add_fusion.1.info, bf16[1728,1536]{1,0:T(8,128)(2,1)} %multiply_convert_fusion.q_ref.k_ref.v_ref, bf16[1728,1536]{1,0:T(8,128)(2,1)} %multiply_convert_fusion.q_ref.k_ref.v_ref, ...), custom_call_target="tpu_custom_call" | custom-call | flops 12230590464 | bytes 4423680 | tf_op jit(solution)/shard_map/attn_forward/pallas_call | solution.py:117
  130.6 1.7 copy-done.32
  135.8 64.0 %middle.1 = (bf16[864,1024]{1,0:T(8,128)(2,1)}, bf16[864,1024]{1,0:T(8,128)(2,1)}, bf16[864,4096]{1,0:T(8,128)(2,1)}, bf16[864,1024]{1,0:T(8,128)(2,1)}, bf16[86...) custom-call(s32[1]{0:T(128)} %bitcast.1.sel_ref.refs_0_, ...), custom_call_target="tpu_custom_call" | custom-call | flops 30802968576 | bytes 45088768 | tf_op jit(solution)/shard_map/middle/pallas_call | solution.py:683
  201.2 7.8 %weight_grad.9 = bf16[2048,1024]{1,0:T(8,128)(2,1)} custom-call(s32[1]{0:T(128)S(6)} %sub.25.refs_0_, bf16[864,4096]{1,0:T(8,128)(2,1)} %get-tuple-element.142.refs_1_, bf16[864,1024]{1,0:T(8,128)(2,1)S(1)} %copy-done.15), custom_call_target="tpu_custom_call" | custom-call | flops 3623878656 | bytes 9502720 | tf_op jit(solution)/shard_map/weight_grad/pallas_call | solution.py:782
  209.0 8.4 %weight_grad.10 = bf16[512,4096]{1,0:T(8,128)(2,1)} custom-call(s32[1]{0:T(128)S(6)} %sub.25.refs_0_, bf16[864,1024]{1,0:T(8,128)(2,1)S(1)} %copy-done, bf16[864,1024]{1,0:T(8,128)(2,1)S(1)} %copy-done, bf16[864,1024]{1,0:T(8,128)(2,1)S(1)} %copy-done, bf16[864,1024]{1,0:T(8,128)(2,1)S(1)} %copy-done, bf16[864,4096]{1,0:T(8,128)(2,1)} %get-tuple-element.141.refs_5_), custom_call_target="tpu_custom_call" | custom-call | flops 3623878656 | bytes 12156928 | tf_op jit(solution)/shard_map/weight_grad/pallas_call | solution.py:782
  217.9 1.7 pad_maximum_fusion.2.refs_1_.refs_2_.refs_3_.refs_4_
  222.8 7.0 %weight_grad.11 = bf16[2048,1024]{1,0:T(8,128)(2,1)S(1)} custom-call(s32[1]{0:T(128)} %bitcast.1.sel_ref.refs_0_, bf16[864,4096]{1,0:T(8,128)(2,1)} %get-tuple-element.142.refs_1_, bf16[864,1024]{1,0:T(8,128)(2,1)S(1)} %copy-done.16, bf16[2048,1024]{1,0:T(8,128)(2,1)} %collective-permute-done.11.refs_3_), custom_call_target="tpu_custom_call" | custom-call | flops 3623878656 | bytes 13697024 | tf_op jit(solution)/shard_map/weight_grad/pallas_call | solution.py:782
  232.9 7.7 %weight_grad.12 = bf16[512,4096]{1,0:T(8,128)(2,1)S(1)} custom-call(s32[1]{0:T(128)} %bitcast.1.sel_ref.refs_0_, bf16[864,1024]{1,0:T(8,128)(2,1)S(1)} %copy-done, bf16[864,1024]{1,0:T(8,128)(2,1)S(1)} %copy-done, bf16[864,1024]{1,0:T(8,128)(2,1)S(1)} %copy-done, bf16[864,1024]{1,0:T(8,128)(2,1)S(1)} %copy-done, ...), custom_call_target="tpu_custom_call" | custom-call | flops 3623878656 | bytes 16351232 | tf_op jit(solution)/shard_map/weight_grad/pallas_call | solution.py:782
  240.7 6.3 %maximum_select_fusion.1.refs_5_ = bf16[1728,1024]{1,0:T(8,128)(2,1)} fusion(bf16[864,1024]{1,0:T(8,128)(2,1)} %collective-permute-done.10, bf16[864,1024]{1,0:T(8,128)(2,1)} %get-tuple-element.146, pred[]{:T(512)S(6)} %eq.74), kind=kLoop, calls=%fused_computation.6 | loop fusion | flops 15925248 | bytes 7077889 | tf_op jit(solution)/shard_map/jit(_where)/select_n | solution.py:1012
  247.0 4.0 weight_grad.13
  254.1 3.3 convolution_convert_fusion.g_ref
  257.4 39.5 %attn_backward.3 = (bf16[3,1728,256]{2,1,0:T(8,128)(2,1)}, f32[2,256]{1,0:T(2,128)}) custom-call(s32[27]{0:T(128)} %copy-done.19, bf16[4,1728,128]{2,1,0:T(8,128)(2,1)} %copy-done.21, bf16[1728,1536]{1,0:T(8,128)(2,1)} %multiply_convert_fusion.q_ref.k_ref.v_ref, bf16[1728,1536]{1,0:T(8,128)(2,1)} %multiply_convert_fusion.q_ref.k_ref.v_ref, ...), custom_call_target="tpu_custom_call" | custom-call | flops 30576476160 | bytes 7077888 | tf_op jit(solution)/shard_map/attn_backward/pallas_call | solution.py:215
  297.6 2.5 dynamic-slice_bitcast_fusion.3
  300.1 1.7 collective-permute-start.16
  301.8 4.1 fusion
  305.9 2.5 fusion.1
  308.4 2.4 collective-permute-done.13
  311.8 3.8 weight_grad.14
  319.5 4.0 weight_grad.15
  324.4 4.5 add_start.2.base_ref
  328.9 1.8 copy-done.5
  330.7 21.4 %attn_backward.4 = (bf16[3,1728,256]{2,1,0:T(8,128)(2,1)}, f32[2,128]{1,0:T(2,128)}) custom-call(s32[27]{0:T(128)} %copy-done.19, bf16[4,1728,128]{2,1,0:T(8,128)(2,1)} %copy-done.20, bf16[1728,1536]{1,0:T(8,128)(2,1)} %multiply_convert_fusion.q_ref.k_ref.v_ref, bf16[1728,1536]{1,0:T(8,128)(2,1)} %multiply_convert_fusion.q_ref.k_ref.v_ref, ...), custom_call_target="tpu_custom_call" | custom-call | flops 15288238080 | bytes 3538944 | tf_op jit(solution)/shard_map/attn_backward/pallas_call | solution.py:215
  352.1 2.8 fusion.2
  354.9 2.4 fusion.3
  357.3 21.5 %attn_backward.5 = (bf16[3,1728,256]{2,1,0:T(8,128)(2,1)}, f32[2,128]{1,0:T(2,128)}) custom-call(s32[27]{0:T(128)} %copy-done.19, bf16[4,1728,128]{2,1,0:T(8,128)(2,1)} %copy-done.20, bf16[1728,1536]{1,0:T(8,128)(2,1)} %multiply_convert_fusion.q_ref.k_ref.v_ref, ...), custom_call_target="tpu_custom_call", output_to_operand_aliasing={{0}: (7, {})} | custom-call | flops 15288238080 | bytes 3538944 | tf_op jit(solution)/shard_map/attn_backward/pallas_call | solution.py:215
  378.8 4.2 all-to-all-start.2
  390.5 3.6 weight_grad.16
  394.3 3.7 weight_grad.17
  402.1 6.7 %all-to-all-done.2 = bf16[4,128,1024]{2,1,0:T(8,128)(2,1)} async-done(((bf16[4,128,1024]{2,1,0:T(8,128)(2,1)}), bf16[4,128,1024]{2,1,0:T(8,128)(2,1)}, u32[]{:S(2)}, u32[]{:S(2)}) %all-to-all-start.2) | async-done | bytes 1048608 | tf_op jit(solution)/shard_map/all_to_all | solution.py:900
  408.8 4.3 all-to-all-start.1
  413.1 2.0 copy-done.6
  419.2 3.8 add_start.3
  431.3 1.8 collective-permute-start.22
  434.2 6.2 %all-to-all-done.1 = bf16[4,32,4096]{2,1,0:T(8,128)(2,1)} async-done(((bf16[4,32,4096]{2,1,0:T(8,128)(2,1)}), bf16[4,32,4096]{2,1,0:T(8,128)(2,1)}, u32[]{:S(2)}, u32[]{:S(2)}) %all-to-all-start.1) | async-done | bytes 1048608 | tf_op jit(solution)/shard_map/all_to_all | solution.py:900
  443.9 2.3 collective-permute-start.32
  447.5 5.4 %collective-permute-done.34 = f32[2,4,32,14]{2,1,0,3:T(4,128)S(1)} collective-permute-done((f32[2,4,32,14]{2,1,0,3:T(4,128)S(1)}, f32[2,4,32,14]{2,1,0,3:T(4,128)S(1)}, u32[]{:S(2)}, u32[]{:S(2)}) %collective-permute-start.34) | collective-permute-done | bytes 14368 | tf_op jit(solution)/shard_map/ppermute | solution.py:876
  455.2 2.1 collective-permute-done.35
  458.0 6.9 %all-to-all-start.3 = ((f32[4,1,448]{2,1,0:T(1,128)}), f32[4,1,448]{2,1,0:T(1,128)S(1)}, u32[]{:S(2)}, u32[]{:S(2)}) async-start(f32[4,1,448]{2,1,0:T(1,128)} %reshape.334), calls=%async_computation.3 | async-start | bytes 16384 | tf_op jit(solution)/shard_map/all_to_all | solution.py:900
  465.6 1.7 fusion.19
  467.3 1.8 fusion.15
  469.1 7.3 %all-to-all-done.3 = f32[4,1,448]{2,1,0:T(1,128)S(1)} async-done(((f32[4,1,448]{2,1,0:T(1,128)}), f32[4,1,448]{2,1,0:T(1,128)S(1)}, u32[]{:S(2)}, u32[]{:S(2)}) %all-to-all-start.3) | async-done | bytes 7200 | tf_op jit(solution)/shard_map/all_to_all | solution.py:900
  476.3 3.8 all-to-all-start
  483.1 2.2 convert_reduce_fusion.1
  485.3 2.3 convert_reduce_fusion
  492.8 12.3 %all-to-all-done = bf16[4,32,4096]{2,1,0:T(8,128)(2,1)S(1)} async-done(((bf16[4,32,4096]{2,1,0:T(8,128)(2,1)}), bf16[4,32,4096]{2,1,0:T(8,128)(2,1)S(1)}, u32[]{:S(2)}, u32[]{:S(2)}) %all-to-all-start) | async-done | bytes 1048608 | tf_op jit(solution)/shard_map/all_to_all | solution.py:900
  (306 shorter events, 88.3 us)
Async XLA Ops:
  0.7 10.8 %copy-start.58 = (s32[2]{0:T(128)S(1)}, s32[2]{0:T(128)}, u32[]{:S(2)}) copy-start(s32[2]{0:T(128)} %param.20) | copy-start | bytes 28
  6.1 62.0 %collective-permute-start.1 = (bf16[432,1024]{1,0:T(8,128)(2,1)}, bf16[432,1024]{1,0:T(8,128)(2,1)}, u32[]{:S(2)}, u32[]{:S(2)}) collective-permute-start(bf16[432,1024]{1,0:T(8,128)(2,1)} %get-tuple-element.247), channel_id=1, source_target_pairs={{2,4},{3,5},{4,2},{5,3},{10,12},{11,13},{12,10},{13,11},{18,20},{1... | collective-permute-start | bytes 2654216 | tf_op jit(solution)/shard_map/ppermute | solution.py:876
  7.7 60.4 %collective-permute-start.2 = (bf16[432,1024]{1,0:T(8,128)(2,1)}, bf16[432,1024]{1,0:T(8,128)(2,1)}, u32[]{:S(2)}, u32[]{:S(2)}) collective-permute-start(bf16[432,1024]{1,0:T(8,128)(2,1)} %get-tuple-element.248), channel_id=1, source_target_pairs={{0,1},{1,0},{2,5},{3,4},{4,3},{5,2},{6,7},{7,6},{8,9},{9,8},{10,13... | collective-permute-start | bytes 2654216 | tf_op jit(solution)/shard_map/ppermute | solution.py:876
  11.8 52.1 %collective-permute-start = (s32[2,16]{1,0:T(2,128)S(1)}, s32[2,16]{1,0:T(2,128)S(1)}, u32[]{:S(2)}, u32[]{:S(2)}) collective-permute-start(s32[2,16]{1,0:T(2,128)S(1)} %pad_add_fusion), channel_id=1, source_target_pairs={{0,4},{1,5},{2,6},{3,7},{4,0},{5,1},{6,2},{7,3},{8,12},{9,13},{10,... | collective-permute-start | bytes 392 | tf_op jit(solution)/shard_map/ppermute | solution.py:876
  57.7 5.3 %copy-start.46 = (bf16[1024]{0:T(1024)(128)(2,1)S(1)}, bf16[1024]{0:T(1024)(128)(2,1)}, u32[]{:S(2)}) copy-start(bf16[1024]{0:T(1024)(128)(2,1)} %param.37) | copy-start | bytes 6148
  57.8 5.3 %copy-start.48 = (bf16[1024]{0:T(1024)(128)(2,1)S(1)}, bf16[1024]{0:T(1024)(128)(2,1)}, u32[]{:S(2)}) copy-start(bf16[1024]{0:T(1024)(128)(2,1)} %param.28) | copy-start | bytes 6148
  57.8 5.3 %copy-start.49 = (bf16[1024]{0:T(1024)(128)(2,1)S(1)}, bf16[1024]{0:T(1024)(128)(2,1)}, u32[]{:S(2)}) copy-start(bf16[1024]{0:T(1024)(128)(2,1)} %param.29) | copy-start | bytes 6148
  57.8 5.3 %copy-start.50 = (bf16[1024]{0:T(1024)(128)(2,1)S(1)}, bf16[1024]{0:T(1024)(128)(2,1)}, u32[]{:S(2)}) copy-start(bf16[1024]{0:T(1024)(128)(2,1)} %param.33) | copy-start | bytes 6148
  57.8 5.3 %copy-start.51 = (bf16[1024]{0:T(1024)(128)(2,1)S(1)}, bf16[1024]{0:T(1024)(128)(2,1)}, u32[]{:S(2)}) copy-start(bf16[1024]{0:T(1024)(128)(2,1)} %param.34) | copy-start | bytes 6148
  57.8 5.3 %copy-start.52 = (bf16[1024]{0:T(1024)(128)(2,1)S(1)}, bf16[1024]{0:T(1024)(128)(2,1)}, u32[]{:S(2)}) copy-start(bf16[1024]{0:T(1024)(128)(2,1)} %param.35) | copy-start | bytes 6148
  57.8 5.4 %copy-start.53 = (bf16[1024]{0:T(1024)(128)(2,1)S(1)}, bf16[1024]{0:T(1024)(128)(2,1)}, u32[]{:S(2)}) copy-start(bf16[1024]{0:T(1024)(128)(2,1)} %param.24) | copy-start | bytes 6148
  57.8 5.4 %copy-start.54 = (bf16[1024]{0:T(1024)(128)(2,1)S(1)}, bf16[1024]{0:T(1024)(128)(2,1)}, u32[]{:S(2)}) copy-start(bf16[1024]{0:T(1024)(128)(2,1)} %param.25) | copy-start | bytes 6148
  68.0 43.4 %copy-start.19 = (s32[27]{0:T(128)}, s32[27]{0:T(128)S(1)}, u32[]{:S(2)}) copy-start(s32[27]{0:T(128)S(1)} %pad_add_fusion.1.info) | copy-start | bytes 328
  71.5 3.9 collective-permute-start.3
  72.3 8.0 %copy-start.26 = (bf16[1024,3,4,1,128]{0,4,3,2,1:T(8,128)(2,1)S(1)}, bf16[1024,3,4,1,128]{0,4,3,2,1:T(8,128)(2,1)}, u32[]{:S(2)}) copy-start(bf16[1024,3,4,1,128]{0,4,3,2,1:T(8,128)(2,1)} %get-tuple-element.228) | copy-start | bytes 9437188
  72.3 58.3 %collective-permute-start.6 = (bf16[432,1024]{1,0:T(8,128)(2,1)}, bf16[432,1024]{1,0:T(8,128)(2,1)S(1)}, u32[]{:S(2)}, u32[]{:S(2)}) collective-permute-start(bf16[432,1024]{1,0:T(8,128)(2,1)} %get-tuple-element.130), channel_id=1, source_target_pairs={{2,4},{3,5},{4,2},{5,3},{10,12},{11,13},{12,10},{13,11},{18,20},{1... | collective-permute-start | bytes 2654216 | tf_op jit(solution)/shard_map/ppermute | solution.py:876
  73.1 57.5 %collective-permute-start.7 = (bf16[432,1024]{1,0:T(8,128)(2,1)}, bf16[432,1024]{1,0:T(8,128)(2,1)S(1)}, u32[]{:S(2)}, u32[]{:S(2)}) collective-permute-start(bf16[432,1024]{1,0:T(8,128)(2,1)} %get-tuple-element.131), channel_id=1, source_target_pairs={{0,1},{1,0},{2,5},{3,4},{4,3},{5,2},{6,7},{7,6},{8,9},{9,8},{10,13... | collective-permute-start | bytes 2654216 | tf_op jit(solution)/shard_map/ppermute | solution.py:876
  109.2 25.5 %collective-permute-start.4 = (bf16[864,256]{1,0:T(8,128)(2,1)S(1)}, bf16[864,256]{1,0:T(8,128)(2,1)S(1)}, u32[]{:S(2)}, u32[]{:S(2)}) collective-permute-start(bf16[864,256]{1,0:T(8,128)(2,1)S(1)} %get-tuple-element.249), channel_id=1, source_target_pairs={{0,4},{1,5},{2,6},{3,7},{4,0},{5,1},{6,2},{7,3},{8,12},{9,13},{10,... | collective-permute-start | bytes 1327112 | tf_op jit(solution)/shard_map/ppermute | solution.py:876
  130.5 4.3 collective-permute-start.5
  201.2 7.8 %copy-start = (bf16[864,1024]{1,0:T(8,128)(2,1)S(1)}, bf16[864,1024]{1,0:T(8,128)(2,1)}, u32[]{:S(2)}) copy-start(bf16[864,1024]{1,0:T(8,128)(2,1)} %get-tuple-element.144.refs_1_.refs_2_.refs_3_.refs_4_) | copy-start | bytes 5308420
  209.0 13.8 %collective-permute-start.11 = (bf16[2048,1024]{1,0:T(8,128)(2,1)}, bf16[2048,1024]{1,0:T(8,128)(2,1)}, u32[]{:S(2)}, u32[]{:S(2)}) collective-permute-start(bf16[2048,1024]{1,0:T(8,128)(2,1)} %weight_grad.9), channel_id=1, source_target_pairs={{0,4},{1,5},{2,6},{3,7},{4,0},{5,1},{6,2},{7,3},{8,12},{9,13},{10,... | collective-permute-start | bytes 12582920 | tf_op jit(solution)/shard_map/ppermute | solution.py:876
  217.4 15.5 %collective-permute-start.12 = (bf16[512,4096]{1,0:T(8,128)(2,1)}, bf16[512,4096]{1,0:T(8,128)(2,1)}, u32[]{:S(2)}, u32[]{:S(2)}) collective-permute-start(bf16[512,4096]{1,0:T(8,128)(2,1)} %weight_grad.10), channel_id=1, source_target_pairs={{0,4},{1,5},{2,6},{3,7},{4,0},{5,1},{6,2},{7,3},{8,12},{9,13},{10,... | collective-permute-start | bytes 12582920 | tf_op jit(solution)/shard_map/ppermute | solution.py:876
  217.9 22.8 %collective-permute-start.10 = (bf16[864,1024]{1,0:T(8,128)(2,1)}, bf16[864,1024]{1,0:T(8,128)(2,1)}, u32[]{:S(2)}, u32[]{:S(2)}) collective-permute-start(bf16[864,1024]{1,0:T(8,128)(2,1)} %get-tuple-element.146), channel_id=1, source_target_pairs={{0,4},{1,5},{2,6},{3,7},{4,0},{5,1},{6,2},{7,3},{8,12},{9,13},{10,... | collective-permute-start | bytes 5308424 | tf_op jit(solution)/shard_map/ppermute | solution.py:876
  221.3 75.6 %collective-permute-start.8 = (bf16[432,1024]{1,0:T(8,128)(2,1)}, bf16[432,1024]{1,0:T(8,128)(2,1)}, u32[]{:S(2)}, u32[]{:S(2)}) collective-permute-start(bf16[432,1024]{1,0:T(8,128)(2,1)} %get-tuple-element.151), channel_id=1, source_target_pairs={{2,4},{3,5},{4,2},{5,3},{10,12},{11,13},{12,10},{13,11},{18,20},{1... | collective-permute-start | bytes 2654216 | tf_op jit(solution)/shard_map/ppermute | solution.py:876
  222.8 74.1 %collective-permute-start.9 = (bf16[432,1024]{1,0:T(8,128)(2,1)}, bf16[432,1024]{1,0:T(8,128)(2,1)}, u32[]{:S(2)}, u32[]{:S(2)}) collective-permute-start(bf16[432,1024]{1,0:T(8,128)(2,1)} %get-tuple-element.243), channel_id=1, source_target_pairs={{0,1},{1,0},{2,5},{3,4},{4,3},{5,2},{6,7},{7,6},{8,9},{9,8},{10,13... | collective-permute-start | bytes 2654216 | tf_op jit(solution)/shard_map/ppermute | solution.py:876
  231.4 70.4 %collective-permute-start.15 = (bf16[2,4,128,1024]{3,2,1,0:T(8,128)(2,1)}, bf16[2,4,128,1024]{3,2,1,0:T(8,128)(2,1)}, u32[]{:S(2)}, u32[]{:S(2)}) collective-permute-start(bf16[2,4,128,1024]{3,2,1,0:T(8,128)(2,1)} %dynamic-slice_bitcast_fusion), channel_id=1, source_target_pairs={{0,8},{1,9},{2,10},{3,11},{4,12},{5,13},{6,14},{7,15},{8,0},{9,1},... | collective-permute-start | bytes 6291464 | tf_op jit(solution)/shard_map/ppermute | solution.py:876
  240.6 10.3 %copy-start.3 = (bf16[512,4096]{1,0:T(8,128)(2,1)}, bf16[512,4096]{1,0:T(8,128)(2,1)S(1)}, u32[]{:S(2)}) copy-start(bf16[512,4096]{1,0:T(8,128)(2,1)S(1)} %weight_grad.12) | copy-start | bytes 12582916
  247.0 7.1 %copy-start.37 = (bf16[4,1,128,1024]{3,2,1,0:T(8,128)(2,1)S(1)}, bf16[4,1,128,1024]{3,2,1,0:T(8,128)(2,1)}, u32[]{:S(2)}) copy-start(bf16[4,1,128,1024]{3,2,1,0:T(8,128)(2,1)} %constant_dynamic-slice_fusion.4) | copy-start | bytes 3145732
  252.6 53.3 %collective-permute-start.14 = (bf16[2,4,32,4096]{3,2,1,0:T(8,128)(2,1)}, bf16[2,4,32,4096]{3,2,1,0:T(8,128)(2,1)}, u32[]{:S(2)}, u32[]{:S(2)}) collective-permute-start(bf16[2,4,32,4096]{3,2,1,0:T(8,128)(2,1)} %dynamic-slice_bitcast_fusion.1), channel_id=1, source_target_pairs={{0,16},{1,17},{2,18},{3,19},{4,20},{5,21},{6,22},{7,23},{8,24},{9,... | collective-permute-start | bytes 6291464 | tf_op jit(solution)/shard_map/ppermute | solution.py:876
  297.0 13.8 %collective-permute-start.13 = (bf16[2,4,32,1024]{3,2,1,0:T(8,128)(2,1)S(1)}, bf16[2,4,32,1024]{3,2,1,0:T(8,128)(2,1)S(1)}, u32[]{:S(2)}, u32[]{:S(2)}) collective-permute-start(bf16[2,4,32,1024]{3,2,1,0:T(8,128)(2,1)S(1)} %dynamic-slice_bitcast_fusion.14), channel_id=1, source_target_pairs={{0,8},{1,9},{2,10},{3,11},{4,12},{5,13},{6,14},{7,15},{8,0},{9,1},... | collective-permute-start | bytes 1572872 | tf_op jit(solution)/shard_map/ppermute | solution.py:876
  300.1 5.8 %copy-start.4 = (bf16[512,4096]{1,0:T(8,128)(2,1)S(1)}, bf16[512,4096]{1,0:T(8,128)(2,1)}, u32[]{:S(2)}) copy-start(bf16[512,4096]{1,0:T(8,128)(2,1)} %copy-done.3) | copy-start | bytes 12582916
  300.1 23.4 %collective-permute-start.16 = (bf16[3,864,256]{2,1,0:T(8,128)(2,1)}, bf16[3,864,256]{2,1,0:T(8,128)(2,1)}, u32[]{:S(2)}, u32[]{:S(2)}) collective-permute-start(bf16[3,864,256]{2,1,0:T(8,128)(2,1)} %dynamic-slice_bitcast_fusion.3), channel_id=1, source_target_pairs={{0,4},{1,5},{2,6},{3,7},{4,0},{5,1},{6,2},{7,3},{8,12},{9,13},{10,... | collective-permute-start | bytes 3981320 | tf_op jit(solution)/shard_map/ppermute | solution.py:876
  305.9 6.0 %copy-start.1 = (bf16[3,1728,256]{2,1,0:T(8,128)(2,1)S(1)}, bf16[3,1728,256]{2,1,0:T(8,128)(2,1)}, u32[]{:S(2)}) copy-start(bf16[3,1728,256]{2,1,0:T(8,128)(2,1)} %get-tuple-element.169.refs_5_.mine_ref) | copy-start | bytes 7962628
  308.4 10.4 %copy-start.29 = (bf16[2,4,32,4096]{3,2,1,0:T(8,128)(2,1)}, bf16[2,4,32,4096]{3,2,1,0:T(8,128)(2,1)S(1)}, u32[]{:S(2)}) copy-start(bf16[2,4,32,4096]{3,2,1,0:T(8,128)(2,1)S(1)} %fusion.1) | copy-start | bytes 6291460
  315.6 7.8 %collective-permute-start.17 = (bf16[512,768]{1,0:T(8,128)(2,1)S(1)}, bf16[512,768]{1,0:T(8,128)(2,1)S(1)}, u32[]{:S(2)}, u32[]{:S(2)}) collective-permute-start(bf16[512,768]{1,0:T(8,128)(2,1)S(1)} %weight_grad.14), channel_id=1, source_target_pairs={{0,4},{1,5},{2,6},{3,7},{4,0},{5,1},{6,2},{7,3},{8,12},{9,13},{10,... | collective-permute-start | bytes 2359304 | tf_op jit(solution)/shard_map/ppermute | solution.py:876
  317.6 34.5 %collective-permute-start.19 = (bf16[4,128,1024]{2,1,0:T(8,128)(2,1)}, bf16[4,128,1024]{2,1,0:T(8,128)(2,1)}, u32[]{:S(2)}, u32[]{:S(2)}) collective-permute-start(bf16[4,128,1024]{2,1,0:T(8,128)(2,1)} %dynamic-slice_bitcast_fusion.4), channel_id=1, source_target_pairs={{0,16},{1,17},{2,18},{3,19},{4,20},{5,21},{6,22},{7,23},{8,24},{9,... | collective-permute-start | bytes 3145736 | tf_op jit(solution)/shard_map/ppermute | solution.py:876
  318.8 5.6 %copy-start.7 = (bf16[1024,768]{1,0:T(8,128)(2,1)S(1)}, bf16[1024,768]{1,0:T(8,128)(2,1)}, u32[]{:S(2)}) copy-start(bf16[1024,768]{1,0:T(8,128)(2,1)} %reshape.247.w_got_ref) | copy-start | bytes 4718596
  318.9 36.0 %collective-permute-start.18 = (bf16[4,32,4096]{2,1,0:T(8,128)(2,1)S(1)}, bf16[4,32,4096]{2,1,0:T(8,128)(2,1)}, u32[]{:S(2)}, u32[]{:S(2)}) collective-permute-start(bf16[4,32,4096]{2,1,0:T(8,128)(2,1)S(1)} %dynamic-slice_bitcast_fusion.5), channel_id=1, source_target_pairs={{0,8},{1,9},{2,10},{3,11},{4,12},{5,13},{6,14},{7,15},{8,0},{9,1},... | collective-permute-start | bytes 3145736 | tf_op jit(solution)/shard_map/ppermute | solution.py:876
  323.4 64.8 %copy-start.13 = (bf16[512,768]{1,0:T(8,128)(2,1)}, bf16[512,768]{1,0:T(8,128)(2,1)S(1)}, u32[]{:S(2)}) copy-start(bf16[512,768]{1,0:T(8,128)(2,1)S(1)} %weight_grad.15) | copy-start | bytes 2359300
  330.7 21.4 %copy-start.28 = (bf16[2,4,128,1024]{3,2,1,0:T(8,128)(2,1)S(1)}, bf16[2,4,128,1024]{3,2,1,0:T(8,128)(2,1)}, u32[]{:S(2)}) copy-start(bf16[2,4,128,1024]{3,2,1,0:T(8,128)(2,1)} %fusion) | copy-start | bytes 6291460
  378.8 30.0 %all-to-all-start.2 = ((bf16[4,128,1024]{2,1,0:T(8,128)(2,1)}), bf16[4,128,1024]{2,1,0:T(8,128)(2,1)}, u32[]{:S(2)}, u32[]{:S(2)}) async-start(bf16[4,128,1024]{2,1,0:T(8,128)(2,1)} %fusion.2), calls=%async_computation.2 | async-start | bytes 2097152 | tf_op jit(solution)/shard_map/all_to_all | solution.py:900
  383.1 7.4 %copy-start.2 = (bf16[3,1728,256]{2,1,0:T(8,128)(2,1)S(1)}, bf16[3,1728,256]{2,1,0:T(8,128)(2,1)}, u32[]{:S(2)}) copy-start(bf16[3,1728,256]{2,1,0:T(8,128)(2,1)} %get-tuple-element.187.refs_5_.mine_ref) | copy-start | bytes 7962628
  384.6 15.1 %collective-permute-start.20 = (bf16[3,864,256]{2,1,0:T(8,128)(2,1)S(1)}, bf16[3,864,256]{2,1,0:T(8,128)(2,1)S(1)}, u32[]{:S(2)}, u32[]{:S(2)}) collective-permute-start(bf16[3,864,256]{2,1,0:T(8,128)(2,1)S(1)} %dynamic-slice_bitcast_fusion.2), channel_id=1, source_target_pairs={{0,4},{1,5},{2,6},{3,7},{4,0},{5,1},{6,2},{7,3},{8,12},{9,13},{10,... | collective-permute-start | bytes 3981320 | tf_op jit(solution)/shard_map/ppermute | solution.py:876
  385.5 38.6 %collective-permute-start.24 = (bf16[4,32,1024]{2,1,0:T(8,128)(2,1)}, bf16[4,32,1024]{2,1,0:T(8,128)(2,1)}, u32[]{:S(2)}, u32[]{:S(2)}) collective-permute-start(bf16[4,32,1024]{2,1,0:T(8,128)(2,1)} %dynamic-slice_bitcast_fusion.23), channel_id=1, source_target_pairs={{0,16},{1,17},{2,18},{3,19},{4,20},{5,21},{6,22},{7,23},{8,24},{9,... | collective-permute-start | bytes 786440 | tf_op jit(solution)/shard_map/ppermute | solution.py:876
  387.1 37.0 %collective-permute-start.26 = (bf16[2,4,32,768]{3,2,1,0:T(8,128)(2,1)}, bf16[2,4,32,768]{3,2,1,0:T(8,128)(2,1)}, u32[]{:S(2)}, u32[]{:S(2)}) collective-permute-start(bf16[2,4,32,768]{3,2,1,0:T(8,128)(2,1)} %dynamic-slice_bitcast_fusion.21), channel_id=1, source_target_pairs={{0,16},{1,17},{2,18},{3,19},{4,20},{5,21},{6,22},{7,23},{8,24},{9,... | collective-permute-start | bytes 1179656 | tf_op jit(solution)/shard_map/ppermute | solution.py:876
  389.0 35.0 %collective-permute-start.23 = (bf16[2,4,32,768]{3,2,1,0:T(8,128)(2,1)}, bf16[2,4,32,768]{3,2,1,0:T(8,128)(2,1)}, u32[]{:S(2)}, u32[]{:S(2)}) collective-permute-start(bf16[2,4,32,768]{3,2,1,0:T(8,128)(2,1)} %dynamic-slice_bitcast_fusion.22), channel_id=1, source_target_pairs={{0,8},{1,9},{2,10},{3,11},{4,12},{5,13},{6,14},{7,15},{8,0},{9,1},... | collective-permute-start | bytes 1179656 | tf_op jit(solution)/shard_map/ppermute | solution.py:876
  394.1 3.9 collective-permute-start.30
  398.9 35.4 %collective-permute-start.31 = (bf16[2,4,32,768]{3,2,1,0:T(8,128)(2,1)}, bf16[2,4,32,768]{3,2,1,0:T(8,128)(2,1)}, u32[]{:S(2)}, u32[]{:S(2)}) collective-permute-start(bf16[2,4,32,768]{3,2,1,0:T(8,128)(2,1)} %dynamic-slice_bitcast_fusion.19), channel_id=1, source_target_pairs={{0,16},{1,17},{2,18},{3,19},{4,20},{5,21},{6,22},{7,23},{8,24},{9,... | collective-permute-start | bytes 1179656 | tf_op jit(solution)/shard_map/ppermute | solution.py:876
  401.6 32.6 %collective-permute-start.28 = (bf16[2,4,32,768]{3,2,1,0:T(8,128)(2,1)}, bf16[2,4,32,768]{3,2,1,0:T(8,128)(2,1)}, u32[]{:S(2)}, u32[]{:S(2)}) collective-permute-start(bf16[2,4,32,768]{3,2,1,0:T(8,128)(2,1)} %dynamic-slice_bitcast_fusion.20), channel_id=1, source_target_pairs={{0,8},{1,9},{2,10},{3,11},{4,12},{5,13},{6,14},{7,15},{8,0},{9,1},... | collective-permute-start | bytes 1179656 | tf_op jit(solution)/shard_map/ppermute | solution.py:876
  408.8 31.6 %all-to-all-start.1 = ((bf16[4,32,4096]{2,1,0:T(8,128)(2,1)}), bf16[4,32,4096]{2,1,0:T(8,128)(2,1)}, u32[]{:S(2)}, u32[]{:S(2)}) async-start(bf16[4,32,4096]{2,1,0:T(8,128)(2,1)} %fusion.3), calls=%async_computation.1 | async-start | bytes 2097152 | tf_op jit(solution)/shard_map/all_to_all | solution.py:900
  424.0 16.3 %copy-start.42 = (f32[8,1024]{1,0:T(8,128)S(1)}, f32[8,1024]{1,0:T(8,128)}, u32[]{:S(2)}) copy-start(f32[8,1024]{1,0:T(8,128)} %get-tuple-element.217) | copy-start | bytes 98308
  424.0 17.0 %copy-start.43 = (f32[1,4096]{1,0:T(1,128)S(1)}, f32[1,4096]{1,0:T(1,128)}, u32[]{:S(2)}) copy-start(f32[1,4096]{1,0:T(1,128)} %get-tuple-element.222) | copy-start | bytes 49156
  425.4 5.9 %collective-permute-start.25 = (bf16[4,32,768]{2,1,0:T(8,128)(2,1)S(1)}, bf16[4,32,768]{2,1,0:T(8,128)(2,1)S(1)}, u32[]{:S(2)}, u32[]{:S(2)}) collective-permute-start(bf16[4,32,768]{2,1,0:T(8,128)(2,1)S(1)} %dynamic-slice_bitcast_fusion.27), channel_id=1, source_target_pairs={{0,16},{1,17},{2,18},{3,19},{4,20},{5,21},{6,22},{7,23},{8,24},{9,... | collective-permute-start | bytes 589832 | tf_op jit(solution)/shard_map/ppermute | solution.py:876
  427.4 5.7 %collective-permute-start.27 = (bf16[4,32,768]{2,1,0:T(8,128)(2,1)S(1)}, bf16[4,32,768]{2,1,0:T(8,128)(2,1)S(1)}, u32[]{:S(2)}, u32[]{:S(2)}) collective-permute-start(bf16[4,32,768]{2,1,0:T(8,128)(2,1)S(1)} %dynamic-slice_bitcast_fusion.26), channel_id=1, source_target_pairs={{0,8},{1,9},{2,10},{3,11},{4,12},{5,13},{6,14},{7,15},{8,0},{9,1},... | collective-permute-start | bytes 589832 | tf_op jit(solution)/shard_map/ppermute | solution.py:876
  428.9 61.2 %collective-permute-start.21 = (bf16[432,1024]{1,0:T(8,128)(2,1)S(1)}, bf16[432,1024]{1,0:T(8,128)(2,1)}, u32[]{:S(2)}, u32[]{:S(2)}) collective-permute-start(bf16[432,1024]{1,0:T(8,128)(2,1)S(1)} %get-tuple-element.193), channel_id=1, source_target_pairs={{2,4},{3,5},{4,2},{5,3},{10,12},{11,13},{12,10},{13,11},{18,20},{1... | collective-permute-start | bytes 2654216 | tf_op jit(solution)/shard_map/ppermute | solution.py:876
  431.3 58.8 %collective-permute-start.22 = (bf16[432,1024]{1,0:T(8,128)(2,1)}, bf16[432,1024]{1,0:T(8,128)(2,1)}, u32[]{:S(2)}, u32[]{:S(2)}) collective-permute-start(bf16[432,1024]{1,0:T(8,128)(2,1)} %get-tuple-element.194), channel_id=1, source_target_pairs={{0,1},{1,0},{2,5},{3,4},{4,3},{5,2},{6,7},{7,6},{8,9},{9,8},{10,13... | collective-permute-start | bytes 2654216 | tf_op jit(solution)/shard_map/ppermute | solution.py:876
  442.5 3.7 collective-permute-start.33
  443.8 23.5 %copy-start.34 = (bf16[2,4,32,1024]{3,2,1,0:T(8,128)(2,1)S(1)}, bf16[2,4,32,1024]{3,2,1,0:T(8,128)(2,1)}, u32[]{:S(2)}) copy-start(bf16[2,4,32,1024]{3,2,1,0:T(8,128)(2,1)} %fusion.4) | copy-start | bytes 1572868
  443.9 21.7 %collective-permute-start.32 = (bf16[4,32,768]{2,1,0:T(8,128)(2,1)S(1)}, bf16[4,32,768]{2,1,0:T(8,128)(2,1)}, u32[]{:S(2)}, u32[]{:S(2)}) collective-permute-start(bf16[4,32,768]{2,1,0:T(8,128)(2,1)S(1)} %dynamic-slice_bitcast_fusion.24), channel_id=1, source_target_pairs={{0,8},{1,9},{2,10},{3,11},{4,12},{5,13},{6,14},{7,15},{8,0},{9,1},... | collective-permute-start | bytes 589832 | tf_op jit(solution)/shard_map/ppermute | solution.py:876
  446.3 6.6 %collective-permute-start.34 = (f32[2,4,32,14]{2,1,0,3:T(4,128)S(1)}, f32[2,4,32,14]{2,1,0,3:T(4,128)S(1)}, u32[]{:S(2)}, u32[]{:S(2)}) collective-permute-start(f32[2,4,32,14]{2,1,0,3:T(4,128)S(1)} %dynamic-slice_bitcast_fusion.28), channel_id=1, source_target_pairs={{0,8},{1,9},{2,10},{3,11},{4,12},{5,13},{6,14},{7,15},{8,0},{9,1},... | collective-permute-start | bytes 43016 | tf_op jit(solution)/shard_map/ppermute | solution.py:876
  453.0 4.3 collective-permute-start.35
  453.7 11.2 %collective-permute-start.29 = (bf16[4,32,768]{2,1,0:T(8,128)(2,1)S(1)}, bf16[4,32,768]{2,1,0:T(8,128)(2,1)S(1)}, u32[]{:S(2)}, u32[]{:S(2)}) collective-permute-start(bf16[4,32,768]{2,1,0:T(8,128)(2,1)S(1)} %dynamic-slice_bitcast_fusion.25), channel_id=1, source_target_pairs={{0,16},{1,17},{2,18},{3,19},{4,20},{5,21},{6,22},{7,23},{8,24},{9,... | collective-permute-start | bytes 589832 | tf_op jit(solution)/shard_map/ppermute | solution.py:876
  458.0 18.3 %all-to-all-start.3 = ((f32[4,1,448]{2,1,0:T(1,128)}), f32[4,1,448]{2,1,0:T(1,128)S(1)}, u32[]{:S(2)}, u32[]{:S(2)}) async-start(f32[4,1,448]{2,1,0:T(1,128)} %reshape.334), calls=%async_computation.3 | async-start | bytes 16384 | tf_op jit(solution)/shard_map/all_to_all | solution.py:900
  476.3 28.7 %all-to-all-start = ((bf16[4,32,4096]{2,1,0:T(8,128)(2,1)}), bf16[4,32,4096]{2,1,0:T(8,128)(2,1)S(1)}, u32[]{:S(2)}, u32[]{:S(2)}) async-start(bf16[4,32,4096]{2,1,0:T(8,128)(2,1)} %fusion.15), calls=%async_computation | async-start | bytes 2097152 | tf_op jit(solution)/shard_map/all_to_all | solution.py:900
  (35 other events, 86.3 us)
